TPU v7x, 32 devices: a whole 2x2x4 slice. The times are simulated.
32 devices in a mesh: fsdp: 16 (over z, y, x), rep: 2 (over core).
Axes of the slice: x: 2, y: 2, z: 4, core: 2. Of those that a mesh axis runs over, the one named last changes fastest.
Arguments:
- tokens: bfloat16 [16, 256, 2048], P('fsdp', 'rep'), may hold values from -6 to 6
- segments: int32 [16, 256], P('fsdp'), may hold values from 0 to 1, never falling along the last dimension, each value on 1 to 192 neighbouring positions
- cotangent: bfloat16 [16, 256, 2048], P('fsdp', 'rep'), may hold values from -6 to 6
- w_query: bfloat16 [1, 2048, 2048], P(None, 'fsdp'), may hold values from -0.125 to 0.125
- w_key: bfloat16 [1, 2048, 1024], P(None, 'fsdp'), may hold values from -0.125 to 0.125
- w_value: bfloat16 [1, 2048, 1024], P(None, 'fsdp'), may hold values from -0.125 to 0.125
- w_output: bfloat16 [1, 2048, 2048], P(None, 'fsdp'), may hold values from -0.375 to 0.375
- w_gate: bfloat16 [1, 2048, 6144], P(None, 'fsdp'), may hold values from -0.125 to 0.125
- w_up: bfloat16 [1, 2048, 6144], P(None, 'fsdp'), may hold values from -0.125 to 0.125
- w_down: bfloat16 [1, 6144, 2048], P(None, 'fsdp'), may hold values from -0.078125 to 0.078125
- gain_in: float32 [1, 2048], replicated, may hold values from 0.25 to 1.75
- gain_query: float32 [1, 128], replicated, may hold values from 0.25 to 1.75
- gain_key: float32 [1, 128], replicated, may hold values from 0.25 to 1.75
- gain_post: float32 [1, 2048], replicated, may hold values from 0.25 to 1.75
Outputs:
- activations: bfloat16 [16, 256, 2048], P('fsdp', 'rep')
- d_tokens: bfloat16 [16, 256, 2048], P('fsdp', 'rep')
- grad_query: float32 [1, 2048, 2048], P(None, 'fsdp')
- grad_key: float32 [1, 2048, 1024], P(None, 'fsdp')
- grad_value: float32 [1, 2048, 1024], P(None, 'fsdp')
- grad_output: float32 [1, 2048, 2048], P(None, 'fsdp')
- grad_gate: float32 [1, 2048, 6144], P(None, 'fsdp')
- grad_up: float32 [1, 2048, 6144], P(None, 'fsdp')
- grad_down: float32 [1, 6144, 2048], P(None, 'fsdp')
- grad_gain_in: float32 [1, 2048], replicated
- grad_gain_query: float32 [1, 128], replicated
- grad_gain_key: float32 [1, 128], replicated
- grad_gain_post: float32 [1, 2048], replicated
Inputs may be any that keep to these rules, and one draw needn't show every extreme that they name: `segments`: segment numbers never fall along a sequence; each sequence holds 2 documents of 1 to 192 tokens.
All inputs are finite; a program needn't handle non-finite values.
Results may differ from a plain program's by a relative error of at most 0.015.
Values may be sent and summed in bfloat16 or wider, within the bound.
No kernel may reach another device: no remote copies, remote signals or barrier semaphores. Data moves between devices by JAX's collectives and lax.ppermute only.
A program may use at most 512 MiB of HBM per device.

v0:
```python
import functools
import math

import jax
import jax.numpy as jnp
from jax import lax
from jax.sharding import PartitionSpec as P

HD = 128
LAYERS = 1


NORM_EPS = 1e-06
NEG_FILL = -1e30
ROPE_BASE = 1000000.0


def contract(form, left_arr, right_arr):
    return jnp.einsum(form, left_arr, right_arr, preferred_element_type=jnp.float32)


def rms_scale(in_value, gain_vec):
    return (
        in_value
        * lax.rsqrt(jnp.mean(in_value * in_value, axis=-1, keepdims=True) + NORM_EPS)
        * gain_vec
    )


def head_prep(raw_heads, gain_vec, cosines, sines):
    normed = rms_scale(raw_heads, gain_vec)
    half_width = normed.shape[-1] // 2
    turned = jnp.concatenate([-normed[..., half_width:], normed[..., :half_width]], axis=-1)
    return normed * cosines + turned * sines


def layout(segments, span_len):
    seq_count, seq_len = segments.shape
    offset = lax.axis_index("rep") * span_len
    position_index = lax.broadcasted_iota(jnp.int32, (seq_count, seq_len), 1)
    prev_segment = jnp.concatenate([segments[:, :1] - 1, segments[:, :-1]], axis=1)
    doc_start = lax.cummax(jnp.where(segments != prev_segment, position_index, 0), axis=1)
    position = position_index - doc_start
    local_pos = lax.dynamic_slice_in_dim(position, offset, span_len, 1).astype(jnp.float32)
    local_seg = lax.dynamic_slice_in_dim(segments, offset, span_len, 1)
    query_index = offset + lax.broadcasted_iota(jnp.int32, (seq_count, span_len), 1)
    inv_freq = jnp.exp(jnp.arange(HD // 2, dtype=jnp.float32) * (-2.0 * math.log(ROPE_BASE) / HD))
    rotation = local_pos[:, :, None] * inv_freq
    rotation = jnp.concatenate([rotation, rotation], axis=-1)[:, :, None, :]
    causal = position_index[:, None, :] <= query_index[:, :, None]
    doc_match = local_seg[:, :, None] == segments[:, None, :]
    same_doc = (causal & doc_match)[:, None, None, :, :]
    return (same_doc, jnp.cos(rotation), jnp.sin(rotation))


def attention_scores(queries, key_heads, same_doc):
    seq_count, span_len, head_count, head_width = queries.shape
    kv_groups = key_heads.shape[2]
    grouped = queries.reshape(seq_count, span_len, kv_groups, head_count // kv_groups, head_width)
    raw_scores = contract("sqgrd,skgd->sgrqk", grouped, key_heads) * (1.0 / math.sqrt(head_width))
    return jnp.where(same_doc, raw_scores, NEG_FILL)


def layer_forward(resid_in, attn_w, mlp_w, gain_set, same_doc, cosines, sines):
    w_q, w_k, w_v, w_o = attn_w
    w_g, w_u, w_d = mlp_w
    g_in, g_q, g_k, g_post = gain_set
    seq_count, span_len, model_width = resid_in.shape
    row_count = seq_count * span_len
    head_count = w_q.shape[1] // HD
    kv_heads = w_k.shape[1] // HD
    normed = rms_scale(resid_in, g_in).astype(jnp.bfloat16).reshape(row_count, model_width)
    q_raw = jnp.dot(normed, w_q, preferred_element_type=jnp.float32).reshape(
        seq_count, span_len, head_count, HD
    )
    k_raw = jnp.dot(normed, w_k, preferred_element_type=jnp.float32).reshape(
        seq_count, span_len, kv_heads, HD
    )
    value_local = (
        jnp.dot(normed, w_v, preferred_element_type=jnp.float32)
        .astype(jnp.bfloat16)
        .reshape(seq_count, span_len, kv_heads, HD)
    )
    queries = head_prep(q_raw, g_q, cosines, sines).astype(jnp.bfloat16)
    key_local = head_prep(k_raw, g_k, cosines, sines).astype(jnp.bfloat16)
    key_heads, values = (
        lax.all_gather(key_local, "rep", axis=1, tiled=True),
        lax.all_gather(value_local, "rep", axis=1, tiled=True),
    )
    scores = attention_scores(queries, key_heads, same_doc)
    row_top = jnp.max(scores, axis=-1, keepdims=True)
    expo_terms = jnp.exp(scores - row_top)
    row_total = jnp.sum(expo_terms, axis=-1, keepdims=True)
    log_total = row_top + jnp.log(row_total)
    prob_rows = (expo_terms / row_total).astype(jnp.bfloat16)
    mixed_heads = (
        contract("sgrqk,skgd->sqgrd", prob_rows, values)
        .astype(jnp.bfloat16)
        .reshape(row_count, head_count * HD)
    )
    middle = resid_in + jnp.dot(mixed_heads, w_o, preferred_element_type=jnp.float32).reshape(
        seq_count, span_len, model_width
    )
    normed_two = rms_scale(middle, g_post).astype(jnp.bfloat16).reshape(row_count, model_width)
    gate_proj = jnp.dot(normed_two, w_g, preferred_element_type=jnp.float32)
    up_proj = jnp.dot(normed_two, w_u, preferred_element_type=jnp.float32)
    hidden = (jax.nn.silu(gate_proj) * up_proj).astype(jnp.bfloat16)
    layer_out = middle + jnp.dot(hidden, w_d, preferred_element_type=jnp.float32).reshape(
        seq_count, span_len, model_width
    )
    saved_state = (
        resid_in,
        normed,
        q_raw,
        k_raw,
        queries,
        key_heads,
        values,
        log_total,
        mixed_heads,
        middle,
        normed_two,
        gate_proj,
        up_proj,
        hidden,
    )
    return (layer_out, saved_state)


def layer_backward(d_out, saved_state, attn_w, mlp_w, gain_set, same_doc, cosines, sines):
    w_q, w_k, w_v, w_o = attn_w
    w_g, w_u, w_d = mlp_w
    g_in, g_q, g_k, g_post = gain_set
    (
        resid_in,
        normed,
        q_raw,
        k_raw,
        queries,
        key_heads,
        values,
        log_total,
        mixed_heads,
        middle,
        normed_two,
        gate_proj,
        up_proj,
        hidden,
    ) = saved_state
    seq_count, span_len, model_width = resid_in.shape
    row_count = seq_count * span_len
    head_count = w_q.shape[1] // HD
    kv_heads = w_k.shape[1] // HD
    d_rows = d_out.astype(jnp.bfloat16).reshape(row_count, model_width)
    grad_down = jnp.dot(hidden.T, d_rows, preferred_element_type=jnp.float32)
    d_hidden = jnp.dot(d_rows, w_d.T, preferred_element_type=jnp.float32)
    gate_sigmoid = jax.nn.sigmoid(gate_proj)
    d_upper = (d_hidden * gate_proj * gate_sigmoid).astype(jnp.bfloat16)
    d_gate = (d_hidden * up_proj * gate_sigmoid * (1.0 + gate_proj * (1.0 - gate_sigmoid))).astype(
        jnp.bfloat16
    )
    grad_gate = jnp.dot(normed_two.T, d_gate, preferred_element_type=jnp.float32)
    grad_up = jnp.dot(normed_two.T, d_upper, preferred_element_type=jnp.float32)
    d_normed_two = jnp.dot(d_gate, w_g.T, preferred_element_type=jnp.float32) + jnp.dot(
        d_upper, w_u.T, preferred_element_type=jnp.float32
    )
    _, post_back = jax.vjp(rms_scale, middle, g_post)
    d_post, grad_post = post_back(d_normed_two.reshape(seq_count, span_len, model_width))
    d_middle = d_out + d_post
    d_mid_rows = d_middle.astype(jnp.bfloat16).reshape(row_count, model_width)
    grad_out = jnp.dot(mixed_heads.T, d_mid_rows, preferred_element_type=jnp.float32)
    d_mixed = jnp.dot(d_mid_rows, w_o.T, preferred_element_type=jnp.float32).astype(jnp.bfloat16)
    d_mixed = d_mixed.reshape(seq_count, span_len, kv_heads, head_count // kv_heads, HD)
    probs_full = jnp.exp(attention_scores(queries, key_heads, same_doc) - log_total)
    prob_rows = probs_full.astype(jnp.bfloat16)
    d_values_all = contract("sgrqk,sqgrd->skgd", prob_rows, d_mixed)
    d_probs = contract("sqgrd,skgd->sgrqk", d_mixed, values)
    d_scores = (
        probs_full
        * (d_probs - jnp.sum(probs_full * d_probs, axis=-1, keepdims=True))
        * (1.0 / math.sqrt(HD))
    ).astype(jnp.bfloat16)
    d_queries = contract("sgrqk,skgd->sqgrd", d_scores, key_heads).reshape(
        seq_count, span_len, head_count, HD
    )
    grouped = queries.reshape(seq_count, span_len, kv_heads, head_count // kv_heads, HD)
    d_keys_all = contract("sgrqk,sqgrd->skgd", d_scores, grouped)
    d_keys, d_values = (
        lax.psum_scatter(d_keys_all, "rep", scatter_dimension=1, tiled=True),
        lax.psum_scatter(d_values_all, "rep", scatter_dimension=1, tiled=True),
    )
    _, q_back = jax.vjp(functools.partial(head_prep, cosines=cosines, sines=sines), q_raw, g_q)
    d_q_raw, grad_qgain = q_back(d_queries)
    _, k_back = jax.vjp(functools.partial(head_prep, cosines=cosines, sines=sines), k_raw, g_k)
    d_k_raw, grad_kgain = k_back(d_keys)
    d_query_rows = d_q_raw.astype(jnp.bfloat16).reshape(row_count, head_count * HD)
    d_key_rows = d_k_raw.astype(jnp.bfloat16).reshape(row_count, kv_heads * HD)
    d_value_rows = d_values.astype(jnp.bfloat16).reshape(row_count, kv_heads * HD)
    grad_query = jnp.dot(normed.T, d_query_rows, preferred_element_type=jnp.float32)
    grad_key = jnp.dot(normed.T, d_key_rows, preferred_element_type=jnp.float32)
    grad_value = jnp.dot(normed.T, d_value_rows, preferred_element_type=jnp.float32)
    d_normed = (
        jnp.dot(d_query_rows, w_q.T, preferred_element_type=jnp.float32)
        + jnp.dot(d_key_rows, w_k.T, preferred_element_type=jnp.float32)
        + jnp.dot(d_value_rows, w_v.T, preferred_element_type=jnp.float32)
    )
    _, in_back = jax.vjp(rms_scale, resid_in, g_in)
    d_resid, grad_in = in_back(d_normed.reshape(seq_count, span_len, model_width))
    return (
        d_middle + d_resid,
        (grad_query, grad_key, grad_value, grad_out),
        (grad_gate, grad_up, grad_down),
        (grad_in, grad_qgain, grad_kgain, grad_post),
    )


def fetch_forward(layer_idx, w_query, w_key, w_value, w_output, w_gate, w_up, w_down):
    whole = (
        lax.all_gather(w_query[layer_idx], "fsdp", axis=0, tiled=True),
        lax.all_gather(w_key[layer_idx], "fsdp", axis=0, tiled=True),
        lax.all_gather(w_value[layer_idx], "fsdp", axis=0, tiled=True),
        lax.all_gather(w_output[layer_idx], "fsdp", axis=0, tiled=True),
        lax.all_gather(w_gate[layer_idx], "fsdp", axis=0, tiled=True),
        lax.all_gather(w_up[layer_idx], "fsdp", axis=0, tiled=True),
        lax.all_gather(w_down[layer_idx], "fsdp", axis=0, tiled=True),
    )
    return ((whole[0], whole[1], whole[2], whole[3]), (whole[4], whole[5], whole[6]))


def per_device(
    tokens,
    segments,
    cotangent,
    w_query,
    w_key,
    w_value,
    w_output,
    w_gate,
    w_up,
    w_down,
    gain_in,
    gain_query,
    gain_key,
    gain_post,
):
    seq_count, span_len, model_width = tokens.shape
    same_doc, cosines, sines = layout(segments, span_len)
    resid = tokens.astype(jnp.float32)
    weight_set = (w_query, w_key, w_value, w_output, w_gate, w_up, w_down)
    layer_idx = 0
    attn_w, mlp_w = fetch_forward(layer_idx, *weight_set)
    gain_set = (
        gain_in[layer_idx],
        gain_query[layer_idx],
        gain_key[layer_idx],
        gain_post[layer_idx],
    )
    resid, saved_state = layer_forward(resid, attn_w, mlp_w, gain_set, same_doc, cosines, sines)
    saved_list = [saved_state]
    held_weights = [(attn_w, mlp_w)]
    d_resid = cotangent.astype(jnp.float32)
    shard_grads = [None] * LAYERS
    gain_terms = [None] * LAYERS
    for layer_idx in reversed(range(LAYERS)):
        attn_w, mlp_w = held_weights[layer_idx]
        gain_set = (
            gain_in[layer_idx],
            gain_query[layer_idx],
            gain_key[layer_idx],
            gain_post[layer_idx],
        )
        d_resid, attn_terms, mlp_terms, gain_grads = layer_backward(
            d_resid, saved_list[layer_idx], attn_w, mlp_w, gain_set, same_doc, cosines, sines
        )
        layer_shards = (
            lax.psum_scatter(attn_terms[0], "fsdp", scatter_dimension=0, tiled=True),
            lax.psum_scatter(attn_terms[1], "fsdp", scatter_dimension=0, tiled=True),
            lax.psum_scatter(attn_terms[2], "fsdp", scatter_dimension=0, tiled=True),
            lax.psum_scatter(attn_terms[3], "fsdp", scatter_dimension=0, tiled=True),
            lax.psum_scatter(mlp_terms[0], "fsdp", scatter_dimension=0, tiled=True),
            lax.psum_scatter(mlp_terms[1], "fsdp", scatter_dimension=0, tiled=True),
            lax.psum_scatter(mlp_terms[2], "fsdp", scatter_dimension=0, tiled=True),
        )
        layer_shards = lax.psum(
            (
                layer_shards[0],
                layer_shards[1],
                layer_shards[2],
                layer_shards[3],
                layer_shards[4],
                layer_shards[5],
                layer_shards[6],
            ),
            "rep",
        )
        shard_grads[layer_idx] = layer_shards
        gain_terms[layer_idx] = gain_grads
    stacked = [jnp.stack([shard_grads[0][entry]]) for entry in range(7)]
    gain_stacked = [jnp.stack([gain_terms[0][entry]]) for entry in range(4)]
    gain_sums = lax.psum(
        (gain_stacked[0], gain_stacked[1], gain_stacked[2], gain_stacked[3]), ("fsdp", "rep")
    )
    activations = resid.astype(jnp.bfloat16)
    d_tokens = d_resid.astype(jnp.bfloat16)
    return (
        activations,
        d_tokens,
        stacked[0],
        stacked[1],
        stacked[2],
        stacked[3],
        stacked[4],
        stacked[5],
        stacked[6],
        gain_sums[0],
        gain_sums[1],
        gain_sums[2],
        gain_sums[3],
    )


def solution(mesh):
    placed = (
        P("fsdp", "rep", None),
        P("fsdp", None),
        P("fsdp", "rep", None),
        P(None, "fsdp", None),
        P(None, "fsdp", None),
        P(None, "fsdp", None),
        P(None, "fsdp", None),
        P(None, "fsdp", None),
        P(None, "fsdp", None),
        P(None, "fsdp", None),
        P(),
        P(),
        P(),
        P(),
    )
    return jax.shard_map(
        per_device,
        mesh=mesh,
        in_specs=placed,
        out_specs=(
            P("fsdp", "rep", None),
            P("fsdp", "rep", None),
            P(None, "fsdp", None),
            P(None, "fsdp", None),
            P(None, "fsdp", None),
            P(None, "fsdp", None),
            P(None, "fsdp", None),
            P(None, "fsdp", None),
            P(None, "fsdp", None),
            P(),
            P(),
            P(),
            P(),
        ),
        check_vma=False,
    )
```

profile of v0, /device:TPU:0, one launch (start us, length us, event | category | flops | bytes accessed | tf_op | source)
XLA Modules:
  0.0 4568.0 jit_solution(6318604272821058868)
XLA Ops:
  15.5 74.1 %all-gather.15.cloned.1.call-done = bf16[1,2048,1024]{2,1,0:T(8,128)(2,1)} async-done(((bf16[1,128,1024]{2,1,0:T(8,128)(2,1)}), bf16[1,2048,1024]{2,1,0:T(8,128)(2,1)}) %all-gather.15.cloned.1.call-update) | async-done | bytes 4194320 | tf_op jit(solution)/shard_map/all_gather | solution.py:221
  89.6 3.0 fusion.66
  92.8 74.3 %all-gather.17.cloned.1.call-done = bf16[1,2048,1024]{2,1,0:T(8,128)(2,1)} async-done(((bf16[1,128,1024]{2,1,0:T(8,128)(2,1)}), bf16[1,2048,1024]{2,1,0:T(8,128)(2,1)}) %all-gather.17.cloned.1.call-update) | async-done | bytes 4194320 | tf_op jit(solution)/shard_map/all_gather | solution.py:220
  167.1 2.9 fusion.63
  170.4 2.3 all_gather.28
  173.6 2.3 all_gather.30
  175.9 105.5 %all-gather.19.cloned.1.call-done = bf16[1,2048,2048]{2,1,0:T(8,128)(2,1)} async-done(((bf16[1,128,2048]{2,1,0:T(8,128)(2,1)}), bf16[1,2048,2048]{2,1,0:T(8,128)(2,1)}) %all-gather.19.cloned.1.call-update) | async-done | bytes 8388624 | tf_op jit(solution)/shard_map/all_gather | solution.py:219
  281.3 6.9 fusion.18
  292.8 102.3 %all-gather.21.cloned.1.call-done = bf16[1,2048,2048]{2,1,0:T(8,128)(2,1)} async-done(((bf16[1,128,2048]{2,1,0:T(8,128)(2,1)}), bf16[1,2048,2048]{2,1,0:T(8,128)(2,1)}) %all-gather.21.cloned.1.call-update) | async-done | bytes 8388624 | tf_op jit(solution)/shard_map/all_gather | solution.py:222
  395.0 4.9 multiply_reduce_fusion.2
  401.9 265.2 %all-gather.27.cloned.1.call-done = bf16[1,6144,2048]{2,1,0:T(8,128)(2,1)} async-done(((bf16[1,384,2048]{2,1,0:T(8,128)(2,1)}), bf16[1,6144,2048]{2,1,0:T(8,128)(2,1)}) %all-gather.27.cloned.1.call-update) | async-done | bytes 25165840 | tf_op jit(solution)/shard_map/all_gather | solution.py:225
  667.1 14.5 fusion
  681.6 257.6 %all-gather.25.cloned.1.call-done = bf16[1,2048,6144]{2,1,0:T(8,128)(2,1)} async-done(((bf16[1,128,6144]{2,1,0:T(8,128)(2,1)}), bf16[1,2048,6144]{2,1,0:T(8,128)(2,1)}) %all-gather.25.cloned.1.call-update) | async-done | bytes 25165840 | tf_op jit(solution)/shard_map/all_gather | solution.py:224
  939.2 13.4 fusion.6
  952.6 258.8 %all-gather.23.cloned.1.call-done = bf16[1,2048,6144]{2,1,0:T(8,128)(2,1)} async-done(((bf16[1,128,6144]{2,1,0:T(8,128)(2,1)}), bf16[1,2048,6144]{2,1,0:T(8,128)(2,1)}) %all-gather.23.cloned.1.call-update) | async-done | bytes 25165840 | tf_op jit(solution)/shard_map/all_gather | solution.py:223
  1211.4 14.9 multiply_convert_fusion.1
  1226.3 14.3 fusion.4
  1240.6 15.8 fusion.82
  1256.4 2.0 fusion.71
  1259.4 7.1 fusion.49
  1266.5 2.0 copy.162
  1268.5 2.5 convolution_bitcast_fusion
  1271.1 1.8 fusion.55
  1276.0 1.9 reduce-scatter.12.cloned.1.call-done
  1279.7 4.6 fusion.119
  1284.4 6.1 reduce-scatter.10.cloned.1.call-done
  1293.4 4.7 fusion.121
  1299.5 8.1 fusion.99
  1311.4 8.2 fusion.123
  1320.6 21.1 fusion.102
  1342.7 21.0 fusion.132
  1363.8 21.1 fusion.133
  1385.3 86.5 %reduce-scatter.18.cloned.1.call-done = f32[128,1024]{1,0:T(8,128)} async-done(((f32[2048,1024]{1,0:T(8,128)}), f32[128,1024]{1,0:T(8,128)}) %reduce-scatter.18.cloned.1.call-update) | async-done | bytes 524304 | tf_op jit(solution)/shard_map/reduce_scatter | solution.py:278
  1471.7 182.6 %reduce-scatter.16.cloned.1.call-done = f32[128,1024]{1,0:T(8,128)} async-done(((f32[2048,1024]{1,0:T(8,128)}), f32[128,1024]{1,0:T(8,128)}) %reduce-scatter.16.cloned.1.call-update) | async-done | bytes 524304 | tf_op jit(solution)/shard_map/reduce_scatter | solution.py:277
  1654.3 351.0 %reduce-scatter.20.cloned.1.call-done = f32[128,2048]{1,0:T(8,128)} async-done(((f32[2048,2048]{1,0:T(8,128)}), f32[128,2048]{1,0:T(8,128)}) %reduce-scatter.20.cloned.1.call-update) | async-done | bytes 1048592 | tf_op jit(solution)/shard_map/reduce_scatter | solution.py:279
  2005.3 354.3 %reduce-scatter.14.cloned.1.call-done = f32[128,2048]{1,0:T(8,128)} async-done(((f32[2048,2048]{1,0:T(8,128)}), f32[128,2048]{1,0:T(8,128)}) %reduce-scatter.14.cloned.1.call-update) | async-done | bytes 1048592 | tf_op jit(solution)/shard_map/reduce_scatter | solution.py:276
  2359.6 711.3 %reduce-scatter.26.cloned.1.call-done = f32[384,2048]{1,0:T(8,128)} async-done(((f32[6144,2048]{1,0:T(8,128)}), f32[384,2048]{1,0:T(8,128)}) %reduce-scatter.26.cloned.1.call-update) | async-done | bytes 3145744 | tf_op jit(solution)/shard_map/reduce_scatter | solution.py:282
  3070.9 705.7 %reduce-scatter.22.cloned.1.call-done = f32[128,6144]{1,0:T(8,128)} async-done(((f32[2048,6144]{1,0:T(8,128)}), f32[128,6144]{1,0:T(8,128)}) %reduce-scatter.22.cloned.1.call-update) | async-done | bytes 3145744 | tf_op jit(solution)/shard_map/reduce_scatter | solution.py:280
  3776.6 704.5 %reduce-scatter.24.cloned.1.call-done = f32[128,6144]{1,0:T(8,128)} async-done(((f32[2048,6144]{1,0:T(8,128)}), f32[128,6144]{1,0:T(8,128)}) %reduce-scatter.24.cloned.1.call-update) | async-done | bytes 3145744 | tf_op jit(solution)/shard_map/reduce_scatter | solution.py:281
  4481.1 6.4 fusion.16
  4487.6 16.0 fusion.52
  4506.1 1.8 fusion.70
  4507.9 38.4 all-reduce.4
  4547.4 2.4 copy.177
  4549.8 1.9 copy.178
  4553.5 1.7 copy.181
  4556.5 1.7 copy.182
  4559.5 1.7 copy.183
  (197 shorter events, 39.4 us)
Async XLA Ops:
  7.2 4.8 copy-start.44
  7.2 82.4 %all-gather.15.cloned.1.call-start = ((), (), s32[]{:S(2)}) async-start(), calls=%async_computation.18 | async-start | bytes 4456448 | tf_op jit(solution)/shard_map/all_gather | solution.py:221
  7.9 159.2 %all-gather.17.cloned.1.call-start = ((), (), s32[]{:S(2)}) async-start(), calls=%async_computation.19 | async-start | bytes 4456448 | tf_op jit(solution)/shard_map/all_gather | solution.py:220
  8.7 5.9 copy-start
  8.7 272.7 %all-gather.19.cloned.1.call-start = ((), (), s32[]{:S(2)}) async-start(), calls=%async_computation.20 | async-start | bytes 8912896 | tf_op jit(solution)/shard_map/all_gather | solution.py:219
  9.4 80.2 %copy-start.25 = (f32[1,2048]{1,0:T(1,128)S(1)}, f32[1,2048]{1,0:T(1,128)}, u32[]{:S(2)}) copy-start(f32[1,2048]{1,0:T(1,128)} %param.24) | copy-start | bytes 24580
  9.4 385.6 %all-gather.21.cloned.1.call-start = ((), (), s32[]{:S(2)}) async-start(), calls=%async_computation.21 | async-start | bytes 8912896 | tf_op jit(solution)/shard_map/all_gather | solution.py:222
  10.0 657.1 %all-gather.27.cloned.1.call-start = ((), (), s32[]{:S(2)}) async-start(), calls=%async_computation.24 | async-start | bytes 26738688 | tf_op jit(solution)/shard_map/all_gather | solution.py:225
  10.6 928.6 %all-gather.25.cloned.1.call-start = ((), (), s32[]{:S(2)}) async-start(), calls=%async_computation.23 | async-start | bytes 26738688 | tf_op jit(solution)/shard_map/all_gather | solution.py:224
  11.2 1200.2 %all-gather.23.cloned.1.call-start = ((), (), s32[]{:S(2)}) async-start(), calls=%async_computation.22 | async-start | bytes 26738688 | tf_op jit(solution)/shard_map/all_gather | solution.py:223
  11.9 1266.0 %reduce-scatter.12.cloned.1.call-start = ((), (), s32[]{:S(2)}) async-start(), calls=%async_computation.10 | async-start | bytes 1572864 | tf_op jit(solution)/shard_map/reduce_scatter | solution.py:190
  14.4 158.8 %copy-start.27 = (f32[128,128]{1,0:T(8,128)}, f32[128,128]{1,0:T(8,128)S(1)}, u32[]{:S(2)}) copy-start(f32[128,128]{1,0:T(8,128)S(1)} %copy.127) | copy-start | bytes 196612
  14.5 158.7 %copy-start.29 = (f32[128,128]{1,0:T(8,128)}, f32[128,128]{1,0:T(8,128)S(1)}, u32[]{:S(2)}) copy-start(f32[128,128]{1,0:T(8,128)S(1)} %copy.128) | copy-start | bytes 196612
  14.8 155.3 %copy-start.50 = (f32[128]{0:T(128)}, f32[128]{0:T(128)S(1)}, u32[]{:S(2)}) copy-start(f32[128]{0:T(128)S(1)} %fusion.77) | copy-start | bytes 1540
  14.8 266.6 %copy-start.38 = (f32[128]{0:T(128)}, f32[128]{0:T(128)S(1)}, u32[]{:S(2)}) copy-start(f32[128]{0:T(128)S(1)} %fusion.117) | copy-start | bytes 1540
  92.7 80.0 %copy-start.45 = (f32[1,128]{1,0:T(1,128)S(1)}, f32[1,128]{1,0:T(1,128)}, u32[]{:S(2)}) copy-start(f32[1,128]{1,0:T(1,128)} %param.26) | copy-start | bytes 1540
  170.4 5.4 copy-start.41
  172.8 115.4 %copy-start.33 = (f32[128,8]{0,1:T(8,128)}, f32[128,8]{0,1:T(8,128)S(1)}, u32[]{:S(2)}) copy-start(f32[128,8]{0,1:T(8,128)S(1)} %fusion.113) | copy-start | bytes 12292
  175.9 113.2 %copy-start.47 = (f32[1,128]{1,0:T(1,128)S(1)}, f32[1,128]{1,0:T(1,128)}, u32[]{:S(2)}) copy-start(f32[1,128]{1,0:T(1,128)} %param.25) | copy-start | bytes 1540
  395.0 5.9 copy-start.35
  1271.1 19.5 reduce-scatter.10.cloned.1.call-start
  1274.5 5.2 copy-start.39
  1275.9 195.8 %reduce-scatter.18.cloned.1.call-start = ((), (), s32[]{:S(2)}) async-start(), calls=%async_computation.13 | async-start | bytes 8912896 | tf_op jit(solution)/shard_map/reduce_scatter | solution.py:278
  1284.3 6.3 copy-start.30
  1284.3 7.6 copy-start.28
  1284.4 7.6 copy-start.34
  1284.4 7.6 copy-start.46
  1284.4 8.5 copy-start.42
  1284.4 369.9 %reduce-scatter.16.cloned.1.call-start = ((), (), s32[]{:S(2)}) async-start(), calls=%async_computation.12 | async-start | bytes 8912896 | tf_op jit(solution)/shard_map/reduce_scatter | solution.py:277
  1298.1 707.2 %reduce-scatter.20.cloned.1.call-start = ((), (), s32[]{:S(2)}) async-start(), calls=%async_computation.14 | async-start | bytes 17825792 | tf_op jit(solution)/shard_map/reduce_scatter | solution.py:279
  1307.6 2.8 copy-start.2
  1307.6 1052.1 %reduce-scatter.14.cloned.1.call-start = ((), (), s32[]{:S(2)}) async-start(), calls=%async_computation.11 | async-start | bytes 17825792 | tf_op jit(solution)/shard_map/reduce_scatter | solution.py:276
  1308.6 1.8 copy-start.48
  1319.6 1751.3 %reduce-scatter.26.cloned.1.call-start = ((), (), s32[]{:S(2)}) async-start(), calls=%async_computation.17 | async-start | bytes 53477376 | tf_op jit(solution)/shard_map/reduce_scatter | solution.py:282
  1341.7 2434.9 %reduce-scatter.22.cloned.1.call-start = ((), (), s32[]{:S(2)}) async-start(), calls=%async_computation.15 | async-start | bytes 53477376 | tf_op jit(solution)/shard_map/reduce_scatter | solution.py:280
  1363.8 3117.3 %reduce-scatter.24.cloned.1.call-start = ((), (), s32[]{:S(2)}) async-start(), calls=%async_computation.16 | async-start | bytes 53477376 | tf_op jit(solution)/shard_map/reduce_scatter | solution.py:281
  1385.0 3162.4 %all-reduce.8.cloned.1.call-start = ((), (), s32[]{:S(2)}) async-start(), calls=%async_computation.25 | async-start | bytes 25165824 | tf_op jit(solution)/shard_map/psum | solution.py:284
  4481.1 6.5 copy-start.4
  4481.1 6.5 copy-start.10
  4487.6 16.0 copy-start.8
  4503.6 2.4 copy-start.5
  4503.6 2.4 copy-start.22
  4506.1 40.2 copy-start.51
  4547.4 4.3 copy-start.31
  4547.4 5.1 copy-start.26
  4547.4 6.1 copy-start.20
  4553.5 3.0 copy-start.19
  4556.5 3.0 copy-start.18
  (21 other events, 24.0 us)
Sparse Core Ops, SparseCore 0:
  10.8 78.7 all-gather.14
  92.4 74.6 all-gather.16
  169.9 111.4 all-gather.18
  284.0 111.0 all-gather.20
  397.6 269.4 all-gather.26
  669.7 269.4 all-gather.24
  941.9 269.4 all-gather.22
  1271.2 6.7 reduce-scatter.11
  1280.8 9.6 reduce-scatter.9
  1292.7 178.9 reduce-scatter.17
  1474.0 180.2 reduce-scatter.15
  1656.5 348.7 reduce-scatter.19
  2007.6 351.9 reduce-scatter.13
  2365.5 705.3 reduce-scatter.25
  3077.7 698.7 reduce-scatter.21
  3782.4 698.5 reduce-scatter.23
  4484.6 49.7 all-reduce.7
where the time goes:
time: 4580 us; the launch traced here: 4570 us
  waiting for transfers between devices  4250 us (93%)
  matrix products  221 us (5%)
    reduce_scatter x1, waiting for transfers between devices, per_device(): lax.psum_scatter(mlp_terms[2], 'fsdp', scatter_dimension=0, tiled=True)  711 us
    reduce_scatter x1, waiting for transfers between devices, per_device(): lax.psum_scatter(mlp_terms[0], 'fsdp', scatter_dimension=0, tiled=True)  706 us
    reduce_scatter x1, waiting for transfers between devices, per_device(): lax.psum_scatter(mlp_terms[1], 'fsdp', scatter_dimension=0, tiled=True)  704 us
    reduce_scatter x1, waiting for transfers between devices, per_device(): lax.psum_scatter(attn_terms[0], 'fsdp', scatter_dimension=0, tiled=True)  354 us
    reduce_scatter x1, waiting for transfers between devices, per_device(): lax.psum_scatter(attn_terms[3], 'fsdp', scatter_dimension=0, tiled=True)  351 us
    all_gather x1, waiting for transfers between devices, fetch_forward(): lax.all_gather(w_down[layer_idx], 'fsdp', axis=0, tiled=True)  265 us
    all_gather x1, waiting for transfers between devices, fetch_forward(): lax.all_gather(w_gate[layer_idx], 'fsdp', axis=0, tiled=True)  259 us
    all_gather x1, waiting for transfers between devices, fetch_forward(): lax.all_gather(w_up[layer_idx], 'fsdp', axis=0, tiled=True)  258 us
  transfers between devices with their start and end apart: 17, of which 16 were waited for; matrix products, arithmetic and copies ran while one was open for 4% of the time, Pallas kernels for 0%

commit v1 on v0

v1 whole, which is shorter than its diff:
```python
import functools
import math

import jax
import jax.numpy as jnp
from jax import lax
from jax.sharding import PartitionSpec as P

HD = 128
NORM_EPS = 1e-06
NEG_FILL = -1e30
ROPE_BASE = 1000000.0
BF16 = jnp.bfloat16
F32 = jnp.float32


def dot(x, y):
    return jnp.dot(x, y, preferred_element_type=F32)


def dot_tn(x, y):
    return lax.dot_general(x, y, (((0,), (0,)), ((), ())), preferred_element_type=F32)


def dot_nt(x, y):
    return lax.dot_general(x, y, (((1,), (1,)), ((), ())), preferred_element_type=F32)


def contract(form, x, y):
    return jnp.einsum(form, x, y, preferred_element_type=F32)


def rms_scale(v, gain):
    return v * lax.rsqrt(jnp.mean(v * v, axis=-1, keepdims=True) + NORM_EPS) * gain


def head_prep(raw, gain, cosines, sines):
    normed = rms_scale(raw, gain)
    half = normed.shape[-1] // 2
    turned = jnp.concatenate([-normed[..., half:], normed[..., :half]], axis=-1)
    return normed * cosines + turned * sines


class Grid:
    def __init__(self, mesh):
        n = mesh.shape["fsdp"]
        assert mesh.shape["rep"] == 2 and n % 16 == 0 and n & (n - 1) == 0
        self.n = n
        self.F = n // 4
        self.B = 2 ** (int(math.log2(self.F)) // 2)
        self.A = self.F // self.B
        self.Q = self.F // 4
        self.tmask, self.umask = 2 * self.B, 1

    def place(self):
        i = lax.axis_index("fsdp")
        self.u = i % 2
        self.b = (i // 2) % self.B
        self.t = (i // (2 * self.B)) % 2
        self.a = i // (4 * self.B)
        self.c = lax.axis_index("rep")

    def px(self, x, mask):
        return lax.ppermute(x, "fsdp", [(i, i ^ mask) for i in range(self.n)])

    def pc(self, x):
        return lax.ppermute(x, "rep", [(0, 1), (1, 0)])

    def pa(self, x, delta):
        return self.px(x, 4 * self.B * delta)

    def pb(self, x, delta):
        return self.px(x, 2 * delta)

    def pt(self, x, dt, du):
        return self.px(x, dt * self.tmask + du * self.umask)

    def kv_head(self, t, u, c, rows):
        first = (u * 2 + c) * self.Q
        block = ((first // self.B * 2 + t) * self.B + first % self.B) * 2
        return block * rows // (2 * HD)

    def hidden_blocks(self, t, u, c):
        half = self.B // 2
        return [
            ((a * 2 + t) * self.B + c * half + b) * 2 + u
            for a in range(self.A)
            for b in range(half)
        ]


SHIFTS = ((1, 1), (0, 1), (1, 0))


def pick(x, *index):
    lead = len(index)
    starts = list(index) + [0] * (x.ndim - lead)
    sizes = [1] * lead + list(x.shape[lead:])
    return lax.dynamic_slice(x, starts, sizes).reshape(x.shape[lead:])


def put(x, piece, *index):
    lead = len(index)
    starts = list(index) + [0] * (x.ndim - lead)
    return lax.dynamic_update_slice(x, piece.reshape((1,) * lead + x.shape[lead:]), starts)


def swap_halves(g, own, other):
    return jnp.where(g.c == 0, jnp.stack([own, other]), jnp.stack([other, own]))


def tokens_gather(g, x):
    out = jnp.zeros((2, 2, 2) + x.shape, x.dtype)
    near = {(0, 0): x}
    for dt, du in SHIFTS:
        near[dt, du] = g.pt(x, dt, du)
    for (dt, du), mine in near.items():
        theirs = g.pc(mine)
        out = put(out, mine, g.t ^ dt, g.u ^ du, g.c)
        out = put(out, theirs, g.t ^ dt, g.u ^ du, 1 - g.c)
    return out


def tokens_scatter(g, partial):
    total = None
    got = []
    for dt, du in SHIFTS + ((0, 0),):
        tt, uu = g.t ^ dt, g.u ^ du
        theirs = g.pc(pick(partial, tt, uu, 1 - g.c).astype(BF16))
        both = pick(partial, tt, uu, g.c) + theirs.astype(F32)
        if (dt, du) == (0, 0):
            total = both
        else:
            got.append(g.pt(both.astype(BF16), dt, du))
    for piece in got:
        total = total + piece.astype(F32)
    return total


def shards_gather(g, x):
    out = jnp.zeros((g.A, g.B) + x.shape, x.dtype)
    held = {0: x}
    for d in range(1, g.A):
        held[d] = g.pa(x, d)
    for d, block in held.items():
        out = put(out, block, g.a ^ d, g.b)
        for e in range(1, g.B):
            out = put(out, g.pb(block, e), g.a ^ d, g.b ^ e)
    return out


def shards_scatter(g, x):
    over_b = [pick(x, d, g.b).astype(F32) for d in range(g.A)]
    rows = jnp.stack(over_b)
    for e in range(1, g.B):
        sent = jnp.stack([pick(x, d, g.b ^ e) for d in range(g.A)]).astype(BF16)
        rows = rows + g.pb(sent, e).astype(F32)
    total = pick(rows, g.a)
    for d in range(1, g.A):
        total = total + g.pa(pick(rows, g.a ^ d).astype(BF16), d).astype(F32)
    return total


def columns_fetch(g, slices):
    own = slices(g.t, g.u)
    block = put(jnp.zeros((2, 2) + own.shape, own.dtype), own, g.t, g.u)
    for dt, du in SHIFTS:
        block = put(block, g.pt(slices(g.t ^ dt, g.u ^ du), dt, du), g.t ^ dt, g.u ^ du)
    whole = shards_gather(g, block)
    return whole.transpose(0, 2, 1, 3, 4, 5).reshape(-1, own.shape[1])


def columns_return(g, grad, rows):
    parts = grad.reshape(g.A, 2, g.B, 2, rows, -1).transpose(0, 2, 1, 3, 4, 5)
    mine = shards_scatter(g, parts).astype(BF16)
    out = {}
    for dt, du in SHIFTS + ((0, 0),):
        piece = pick(mine, g.t ^ dt, g.u ^ du)
        if (dt, du) != (0, 0):
            piece = g.pt(piece, dt, du)
        out[dt, du] = (piece, g.pc(piece))
    return out


def per_device(
    g,
    tokens,
    segments,
    cotangent,
    w_query,
    w_key,
    w_value,
    w_output,
    w_gate,
    w_up,
    w_down,
    gain_in,
    gain_query,
    gain_key,
    gain_post,
):
    g.place()
    A, B, Q = g.A, g.B, g.Q
    _, span, width = tokens.shape
    seq_len = segments.shape[1]
    w_q, w_k, w_v, w_o, w_g, w_u, w_d = (
        w[0] for w in (w_query, w_key, w_value, w_output, w_gate, w_up, w_down)
    )
    rows_in, rows_o, rows_d = w_q.shape[0], w_o.shape[0], w_d.shape[0]
    q_width, kv_width, hidden_width = w_q.shape[1], w_k.shape[1], w_g.shape[1]
    g_in, g_q, g_k, g_post = gain_in[0], gain_query[0], gain_key[0], gain_post[0]

    x_own = tokens[0].astype(F32)
    d_out = cotangent[0].astype(F32)

    def attn_slice(t, u):
        kv = g.kv_head(t, u, g.c, rows_o)
        return jnp.concatenate(
            [
                lax.dynamic_slice(w_q, (0, kv * 2 * HD), (rows_in, 2 * HD)),
                lax.dynamic_slice(w_k, (0, kv * HD), (rows_in, HD)),
                lax.dynamic_slice(w_v, (0, kv * HD), (rows_in, HD)),
            ],
            axis=1,
        )

    w_qkv = columns_fetch(g, attn_slice)

    xn_own = rms_scale(x_own, g_in).astype(BF16)
    xn = tokens_gather(g, xn_own).reshape(4 * seq_len, width)

    seg_all = put(jnp.zeros((2, 2, seq_len), segments.dtype), segments[0], g.t, g.u)
    for dt, du in SHIFTS:
        seg_all = put(seg_all, g.pt(segments[0], dt, du), g.t ^ dt, g.u ^ du)
    seg_all = seg_all.reshape(4, seq_len)
    index = lax.broadcasted_iota(jnp.int32, (4, seq_len), 1)
    earlier = seg_all[:, None, :] < seg_all[:, :, None]
    doc_start = jnp.sum(earlier.astype(jnp.int32), axis=-1)
    pos = (index - doc_start).astype(F32)
    inv_freq = jnp.exp(jnp.arange(HD // 2, dtype=F32) * (-2.0 * math.log(ROPE_BASE) / HD))
    rotation = pos[:, :, None] * inv_freq
    rotation = jnp.concatenate([rotation, rotation], axis=-1)[:, :, None, :]
    cosines, sines = jnp.cos(rotation), jnp.sin(rotation)
    same_doc = (index[:, None, :] <= index[:, :, None]) & (
        seg_all[:, :, None] == seg_all[:, None, :]
    )
    same_doc = same_doc[:, None]

    half_o = lax.dynamic_slice(w_o, (g.c * (rows_o // 2), 0), (rows_o // 2, width))
    o_blocks = shards_gather(g, half_o).reshape(2, 2, Q, rows_o // 2, width)
    o_mine = pick(o_blocks, g.u)
    o_next = g.px(pick(o_blocks, 1 - g.u), g.umask)
    o_pair = jnp.where(g.u == 0, jnp.stack([o_mine, o_next]), jnp.stack([o_next, o_mine]))
    o_pair = o_pair.transpose(1, 2, 0, 3, 4)
    o_other = g.pc(pick(o_pair, 1 - g.c))
    w_o_all = swap_halves(g, pick(o_pair, g.c), o_other)
    w_o_all = w_o_all.transpose(1, 2, 0, 3, 4).reshape(-1, width)

    qkv = dot(xn, w_qkv)
    q_raw = qkv[:, : 2 * HD].reshape(4, seq_len, 2, HD)
    k_raw = qkv[:, 2 * HD : 3 * HD].reshape(4, seq_len, 1, HD)
    vals = qkv[:, 3 * HD :].astype(BF16).reshape(4, seq_len, HD)
    queries, q_back = jax.vjp(
        functools.partial(head_prep, cosines=cosines, sines=sines), q_raw, g_q
    )
    keys, k_back = jax.vjp(functools.partial(head_prep, cosines=cosines, sines=sines), k_raw, g_k)
    queries = queries.astype(BF16)
    keys = keys.astype(BF16).reshape(4, seq_len, HD)
    scale = 1.0 / math.sqrt(HD)
    scores = jnp.where(same_doc, contract("sqrd,skd->srqk", queries, keys) * scale, NEG_FILL)
    top = jnp.max(scores, axis=-1, keepdims=True)
    expo = jnp.exp(scores - top)
    probs = expo / jnp.sum(expo, axis=-1, keepdims=True)
    probs_low = probs.astype(BF16)
    att = contract("srqk,skd->sqrd", probs_low, vals).astype(BF16).reshape(4 * seq_len, 2 * HD)
    att_part = dot(att, w_o_all).reshape(2, 2, 2, span, width)
    mid = x_own + tokens_scatter(g, att_part)
    xn2_own, post_back = jax.vjp(rms_scale, mid, g_post)
    xn2_own = xn2_own.astype(BF16)
    xn2 = tokens_gather(g, xn2_own).reshape(4 * seq_len, width)

    def hidden_slice(w):
        def take(t, u):
            return jnp.concatenate(
                [
                    lax.dynamic_slice(w, (0, i * rows_d), (rows_in, rows_d))
                    for i in g.hidden_blocks(t, u, g.c)
                ],
                axis=1,
            )

        return take

    half_d = lax.dynamic_slice(w_d, (g.c * (rows_d // 2), 0), (rows_d // 2, width))
    d_blocks = shards_gather(g, half_d).reshape(A, 2, B // 2, rows_d // 2, width)
    d_blocks = d_blocks.transpose(1, 0, 2, 3, 4)
    d_other = g.pc(pick(d_blocks, 1 - g.c))
    w_d_all = swap_halves(g, pick(d_blocks, g.c), d_other)
    w_d_all = w_d_all.transpose(1, 2, 0, 3, 4).reshape(-1, width)
    w_g_all = columns_fetch(g, hidden_slice(w_g))
    w_u_all = columns_fetch(g, hidden_slice(w_u))

    dob = tokens_gather(g, cotangent[0]).reshape(4 * seq_len, width)

    d_hidden = dot_nt(dob, w_d_all)
    gate = dot(xn2, w_g_all)
    up = dot(xn2, w_u_all)
    sig = jax.nn.sigmoid(gate)
    hidden = (gate * sig * up).astype(BF16)
    d_up = (d_hidden * gate * sig).astype(BF16)
    d_gate = (d_hidden * up * sig * (1.0 + gate * (1.0 - sig))).astype(BF16)
    d_xn2 = dot_nt(d_gate, w_g_all) + dot_nt(d_up, w_u_all)
    d_xn2 = tokens_scatter(g, d_xn2.reshape(2, 2, 2, span, width))
    d_post, grad_post = post_back(d_xn2)
    d_mid = d_out + d_post
    dmb = tokens_gather(g, d_mid.astype(BF16)).reshape(4 * seq_len, width)
    out_part = dot(hidden, w_d_all).reshape(2, 2, 2, span, width)
    activations = (mid + tokens_scatter(g, out_part)).astype(BF16)

    grad_g = columns_return(g, dot_tn(xn2, d_gate), rows_in)
    grad_u = columns_return(g, dot_tn(xn2, d_up), rows_in)

    def down_return(grad):
        grad = grad.reshape(A, B // 2, 2, rows_d // 2, width)
        mine = pick(grad.transpose(2, 0, 1, 3, 4), g.c).astype(BF16)
        other = g.pc(pick(grad.transpose(2, 0, 1, 3, 4), 1 - g.c).astype(BF16))
        both = swap_halves(g, mine, other)
        both = both.transpose(1, 0, 2, 3, 4).reshape(A, B, rows_d // 2, width)
        half = shards_scatter(g, both).astype(BF16)
        return swap_halves(g, half, g.pc(half)).reshape(1, rows_d, width).astype(F32)

    grad_down = down_return(dot_tn(hidden, dob))

    d_att = dot_nt(dmb, w_o_all).astype(BF16).reshape(4, seq_len, 2, HD)
    d_vals = contract("srqk,sqrd->skd", probs_low, d_att)
    d_probs = contract("sqrd,skd->srqk", d_att, vals)
    d_scores = (
        probs * (d_probs - jnp.sum(probs * d_probs, axis=-1, keepdims=True)) * scale
    ).astype(BF16)
    d_queries = contract("srqk,skd->sqrd", d_scores, keys)
    d_keys = contract("srqk,sqrd->skd", d_scores, queries)
    d_q_raw, grad_qgain = q_back(d_queries)
    d_k_raw, grad_kgain = k_back(d_keys.reshape(4, seq_len, 1, HD))
    d_qkv = jnp.concatenate(
        [
            d_q_raw.astype(BF16).reshape(4 * seq_len, 2 * HD),
            d_k_raw.astype(BF16).reshape(4 * seq_len, HD),
            d_vals.astype(BF16).reshape(4 * seq_len, HD),
        ],
        axis=1,
    )
    d_xn = tokens_scatter(g, dot_nt(d_qkv, w_qkv).reshape(2, 2, 2, span, width))
    _, in_back = jax.vjp(rms_scale, x_own, g_in)
    d_x, grad_in = in_back(d_xn)
    d_tokens = (d_mid + d_x).astype(BF16)

    def output_return(grad):
        grad = grad.reshape(Q, 2, rows_o, width).transpose(1, 0, 2, 3)
        mine = pick(grad, g.u).astype(BF16)
        other = g.px(pick(grad, 1 - g.u).astype(BF16), g.umask)
        both = jnp.where(g.u == 0, jnp.stack([mine, other]), jnp.stack([other, mine]))
        both = both.reshape(2, Q, 2, rows_o // 2, width).transpose(2, 0, 1, 3, 4)
        swapped = swap_halves(g, pick(both, g.c), g.pc(pick(both, 1 - g.c)))
        swapped = swapped.transpose(1, 0, 2, 3, 4).reshape(A, B, rows_o // 2, width)
        half = shards_scatter(g, swapped).astype(BF16)
        return swap_halves(g, half, g.pc(half)).reshape(1, rows_o, width).astype(F32)

    grad_output = output_return(dot_tn(att, dmb))
    grad_qkv = columns_return(g, dot_tn(xn, d_qkv), rows_in)

    grad_query = jnp.zeros((rows_in, q_width), F32)
    grad_key = jnp.zeros((rows_in, kv_width), F32)
    grad_value = jnp.zeros((rows_in, kv_width), F32)
    for (dt, du), pair in grad_qkv.items():
        for k, piece in enumerate(pair):
            kv = g.kv_head(g.t ^ dt, g.u ^ du, g.c ^ k, rows_o)
            piece = piece.astype(F32)
            grad_query = lax.dynamic_update_slice(grad_query, piece[:, : 2 * HD], (0, kv * 2 * HD))
            grad_key = lax.dynamic_update_slice(
                grad_key, piece[:, 2 * HD : 3 * HD], (0, kv * HD)
            )
            grad_value = lax.dynamic_update_slice(grad_value, piece[:, 3 * HD :], (0, kv * HD))

    def hidden_place(grads):
        out = jnp.zeros((rows_in, hidden_width), F32)
        for (dt, du), pair in grads.items():
            for k, piece in enumerate(pair):
                blocks = g.hidden_blocks(g.t ^ dt, g.u ^ du, g.c ^ k)
                for j, i in enumerate(blocks):
                    part = piece[:, j * rows_d : (j + 1) * rows_d].astype(F32)
                    out = lax.dynamic_update_slice(out, part, (0, i * rows_d))
        return out[None]

    gains = jnp.concatenate([grad_in, grad_post, grad_qgain, grad_kgain])
    for bit in range(int(math.log2(g.n))):
        gains = gains + g.px(gains, 1 << bit)
    gains = (gains + g.pc(gains))[None]
    return (
        activations[None],
        d_tokens[None],
        grad_query[None],
        grad_key[None],
        grad_value[None],
        grad_output,
        hidden_place(grad_g),
        hidden_place(grad_u),
        grad_down,
        gains[:, :width],
        gains[:, 2 * width : 2 * width + HD],
        gains[:, 2 * width + HD :],
        gains[:, width : 2 * width],
    )


def solution(mesh):
    rows = P("fsdp", "rep", None)
    cut_rows = P(None, "fsdp", None)
    return jax.shard_map(
        functools.partial(per_device, Grid(mesh)),
        mesh=mesh,
        in_specs=(rows, P("fsdp", None), rows) + (cut_rows,) * 7 + (P(),) * 4,
        out_specs=(rows, rows) + (cut_rows,) * 7 + (P(),) * 4,
        check_vma=False,
    )
```

time: 4580 us -> 825 us (0.18)
  waiting for transfers between devices: 4250 us -> 465 us
  matrix products: 221 us -> 81.3 us
  starting transfers between devices: 1.47 us -> 93 us
  local copies, waits for them, and re-layouts: 27.3 us -> 115 us
  other arithmetic: 13.2 us -> 61.8 us
    reduce_scatter x9 -> x0, waiting for transfers between devices: 3100 us -> none  [the longest x1 711 us: per_device(): lax.psum_scatter(mlp_terms[2], 'fsdp', scatter_dimension=0, tiled=True)]
    all_gather x7 -> x0, waiting for transfers between devices: 1140 us -> none  [the longest x1 265 us: fetch_forward(): lax.all_gather(w_down[layer_idx], 'fsdp', axis=0, tiled=True)]
    ppermute x0 -> x127, waiting for transfers between devices: none -> 465 us  [the longest x76 459 us: px(): return lax.ppermute(x, 'fsdp', [(i, i ^ mask) for i in range(self.n)])]
    dot_general x26 -> x20, matrix products: 214 us -> 78 us  [the longest x5 21.8 us: dot_nt(): lax.dot_general(x, y, (((1,), (1,)), ((), ())), preferred_element_type=F32)]
    ppermute x0 -> x127, starting transfers between devices: none -> 93 us  [the longest x76 83.8 us: px(): return lax.ppermute(x, 'fsdp', [(i, i ^ mask) for i in range(self.n)])]
  transfers between devices with their start and end apart: 17 -> 127, of which waited for: 16 -> 53; matrix products, arithmetic and copies ran while one was open for 4% -> 23% of each run, Pallas kernels for 0% -> 0%
where the time goes in v1:
time: 825 us; the launch traced here: 820 us
  waiting for transfers between devices  465 us (56%)
  local copies, waits for them, and re-layouts  115 us (14%)
  starting transfers between devices  93 us (11%)
  matrix products  81.3 us (10%)
  other arithmetic  61.8 us (7%)
    ppermute x76, waiting for transfers between devices, px(): return lax.ppermute(x, 'fsdp', [(i, i ^ mask) for i in range(self.n)])  459 us
    ppermute x76, starting transfers between devices, px(): return lax.ppermute(x, 'fsdp', [(i, i ^ mask) for i in range(self.n)])  83.8 us
    dynamic_update_slice x62, local copies, waits for them, and re-layouts, put(): lax.dynamic_update_slice(x, piece.reshape((1,) * lead + x.shape[lead:]),...  33.9 us
    dot_general x5, matrix products, dot_nt(): lax.dot_general(x, y, (((1,), (1,)), ((), ())), preferred_element_type=F32)  21.8 us
    dot_general x5, matrix products, dot_tn(): lax.dot_general(x, y, (((0,), (0,)), ((), ())), preferred_element_type=F32)  20.8 us
    dot_general x5, matrix products, contract(): return jnp.einsum(form, x, y, preferred_element_type=F32)  18.7 us
    dot_general x5, matrix products, dot(): return jnp.dot(x, y, preferred_element_type=F32)  16.6 us
  transfers between devices with their start and end apart: 127, of which 53 were waited for; matrix products, arithmetic and copies ran while one was open for 23% of the time, Pallas kernels for 0%

profile of v1, /device:TPU:0, one launch (start us, length us, event | category | flops | bytes accessed | tf_op | source)
XLA Modules:
  0.0 819.7 jit_solution(7325368840725363954)
XLA Ops:
  36.7 11.9 %collective-permute-done.7 = bf16[128,512]{1,0:T(8,128)(2,1)S(1)} collective-permute-done((bf16[128,512]{1,0:T(8,128)(2,1)S(1)}, bf16[128,512]{1,0:T(8,128)(2,1)S(1)}, u32[]{:S(2)}, u32[]{:S(2)}) %collective-permute-start.7) | collective-permute-done | bytes 131104 | tf_op jit(solution)/shard_map/ppermute | solution.py:64
  55.1 5.1 collective-permute-done.9
  62.2 4.9 collective-permute-done.41
  67.8 5.2 collective-permute-done.42
  74.3 5.7 collective-permute-done.43
  82.8 4.0 collective-permute-done.35
  88.4 4.2 collective-permute-done.36
  94.0 4.3 collective-permute-done.37
  107.2 7.5 collective-permute-done.17
  121.1 8.9 %collective-permute-done.59 = bf16[128,2048]{1,0:T(8,128)(2,1)S(1)} collective-permute-done((bf16[128,2048]{1,0:T(8,128)(2,1)S(1)}, bf16[128,2048]{1,0:T(8,128)(2,1)S(1)}, u32[]{:S(2)}, u32[]{:S(2)}) %collective-permute-start.59) | collective-permute-done | bytes 524320 | tf_op jit(solution)/shard_map/ppermute | solution.py:64
  132.4 21.2 %collective-permute-done.18 = bf16[64,2048]{1,0:T(8,128)(2,1)S(1)} collective-permute-done((bf16[64,2048]{1,0:T(8,128)(2,1)S(1)}, bf16[64,2048]{1,0:T(8,128)(2,1)S(1)}, u32[]{:S(2)}, u32[]{:S(2)}) %collective-permute-start.18) | collective-permute-done | bytes 262176 | tf_op jit(solution)/shard_map/ppermute | solution.py:64
  157.2 40.3 %collective-permute-done.11 = bf16[2,2,128,512]{3,2,1,0:T(8,128)(2,1)S(1)} collective-permute-done((bf16[2,2,128,512]{3,2,1,0:T(8,128)(2,1)}, bf16[2,2,128,512]{3,2,1,0:T(8,128)(2,1)S(1)}, u32[]{:S(2)}, u32[]{:S(2)}) %collective-permute-start.11) | collective-permute-done | bytes 524320 | tf_op jit(solution)/shard_map/ppermute | solution.py:64
  200.1 31.2 %collective-permute-done.48 = bf16[192,2048]{1,0:T(8,128)(2,1)} collective-permute-done((bf16[192,2048]{1,0:T(8,128)(2,1)S(1)}, bf16[192,2048]{1,0:T(8,128)(2,1)}, u32[]{:S(2)}, u32[]{:S(2)}) %collective-permute-start.48) | collective-permute-done | bytes 786464 | tf_op jit(solution)/shard_map/ppermute | solution.py:64
  235.0 30.0 %collective-permute-done.45 = bf16[2,2,128,768]{3,2,1,0:T(8,128)(2,1)} collective-permute-done((bf16[2,2,128,768]{3,2,1,0:T(8,128)(2,1)S(1)}, bf16[2,2,128,768]{3,2,1,0:T(8,128)(2,1)}, u32[]{:S(2)}, u32[]{:S(2)}) %collective-permute-start.45) | collective-permute-done | bytes 786464 | tf_op jit(solution)/shard_map/ppermute | solution.py:64
  266.9 14.1 %collective-permute-done.39 = bf16[2,2,128,768]{3,2,1,0:T(8,128)(2,1)S(1)} collective-permute-done((bf16[2,2,128,768]{3,2,1,0:T(8,128)(2,1)}, bf16[2,2,128,768]{3,2,1,0:T(8,128)(2,1)S(1)}, u32[]{:S(2)}, u32[]{:S(2)}) %collective-permute-start.39) | collective-permute-done | bytes 786464 | tf_op jit(solution)/shard_map/ppermute | solution.py:64
  283.9 10.4 %collective-permute-done.63 = bf16[128,2048]{1,0:T(8,128)(2,1)} collective-permute-done((bf16[128,2048]{1,0:T(8,128)(2,1)S(1)}, bf16[128,2048]{1,0:T(8,128)(2,1)}, u32[]{:S(2)}, u32[]{:S(2)}) %collective-permute-start.63) | collective-permute-done | bytes 524320 | tf_op jit(solution)/shard_map/ppermute | solution.py:64
  305.5 5.3 collective-permute-done.12
  359.4 6.5 copy.259
  371.0 8.5 %collective-permute-done.25 = bf16[128,2048]{1,0:T(8,128)(2,1)} collective-permute-done((bf16[128,2048]{1,0:T(8,128)(2,1)}, bf16[128,2048]{1,0:T(8,128)(2,1)}, u32[]{:S(2)}, u32[]{:S(2)}) %collective-permute-start.25) | collective-permute-done | bytes 524320 | tf_op jit(solution)/shard_map/ppermute | solution.py:64
  392.8 5.8 collective-permute-done.29
  398.5 10.7 %collective-permute-done.31 = bf16[128,2048]{1,0:T(8,128)(2,1)S(1)} collective-permute-done((bf16[128,2048]{1,0:T(8,128)(2,1)S(1)}, bf16[128,2048]{1,0:T(8,128)(2,1)S(1)}, u32[]{:S(2)}, u32[]{:S(2)}) %collective-permute-start.31) | collective-permute-done | bytes 524320 | tf_op jit(solution)/shard_map/ppermute | solution.py:64
  415.4 4.8 fusion.3
  420.2 8.2 %multiply_convert_fusion.1 = (bf16[1024,768]{1,0:T(8,128)(2,1)}, bf16[1024,768]{1,0:T(8,128)(2,1)S(1)}, bf16[1024,768]{1,0:T(8,128)(2,1)}) fusion(f32[1024,768]{1,0:T(8,128)S(1)} %fusion.194, f32[1024,768]{1,0:T(8,128)S(1)} %get-tuple-element.173, bf16[1024,2048]{1,0:T(8,128)(2,1)} %bitcast.163, bf16[768,2048]{1,0:T(8,128)(2,1)S(1)} %bitcast.1044), kind=kOutput, calls=%fused_computation.19 | convolution fusion | flops 3233808384 | bytes 18350080 | tf_op jit(solution)/shard_map/dot_general | solution.py:26
  428.4 5.7 fusion.196
  434.1 6.3 copy.261
  440.5 5.8 fusion.12
  451.1 5.2 fusion.14
  468.1 6.1 fusion.198
  491.8 9.1 %collective-permute-done.67 = bf16[128,2048]{1,0:T(8,128)(2,1)S(1)} collective-permute-done((bf16[128,2048]{1,0:T(8,128)(2,1)S(1)}, bf16[128,2048]{1,0:T(8,128)(2,1)S(1)}, u32[]{:S(2)}, u32[]{:S(2)}) %collective-permute-start.67) | collective-permute-done | bytes 524320 | tf_op jit(solution)/shard_map/ppermute | solution.py:64
  500.9 10.4 %collective-permute-done.69 = bf16[128,2048]{1,0:T(8,128)(2,1)S(1)} collective-permute-done((bf16[128,2048]{1,0:T(8,128)(2,1)S(1)}, bf16[128,2048]{1,0:T(8,128)(2,1)S(1)}, u32[]{:S(2)}, u32[]{:S(2)}) %collective-permute-start.69) | collective-permute-done | bytes 524320 | tf_op jit(solution)/shard_map/ppermute | solution.py:64
  520.1 11.2 %collective-permute-done.73 = bf16[128,2048]{1,0:T(8,128)(2,1)S(1)} collective-permute-done((bf16[128,2048]{1,0:T(8,128)(2,1)S(1)}, bf16[128,2048]{1,0:T(8,128)(2,1)S(1)}, u32[]{:S(2)}, u32[]{:S(2)}) %collective-permute-start.73) | collective-permute-done | bytes 524320 | tf_op jit(solution)/shard_map/ppermute | solution.py:64
  532.6 9.8 %collective-permute-done.75 = bf16[128,2048]{1,0:T(8,128)(2,1)S(1)} collective-permute-done((bf16[128,2048]{1,0:T(8,128)(2,1)S(1)}, bf16[128,2048]{1,0:T(8,128)(2,1)S(1)}, u32[]{:S(2)}, u32[]{:S(2)}) %collective-permute-start.75) | collective-permute-done | bytes 524320 | tf_op jit(solution)/shard_map/ppermute | solution.py:64
  546.7 12.9 %collective-permute-done.100 = bf16[2,2,2,128,768]{4,3,2,1,0:T(8,128)(2,1)S(1)} collective-permute-done((bf16[2,2,2,128,768]{4,3,2,1,0:T(8,128)(2,1)S(1)}, bf16[2,2,2,128,768]{4,3,2,1,0:T(8,128)(2,1)S(1)}, u32[]{:S(2)}, u32[]{:S(2)}) %collective-permute-start.100) | collective-permute-done | bytes 1572896 | tf_op jit(solution)/shard_map/ppermute | solution.py:64
  577.0 5.8 broadcast_multiply_fusion
  582.8 5.2 convolution_bitcast_fusion.2
  616.7 12.4 %collective-permute-done.101 = bf16[2,2,128,768]{3,2,1,0:T(8,128)(2,1)} collective-permute-done((bf16[2,2,128,768]{3,2,1,0:T(8,128)(2,1)}, bf16[2,2,128,768]{3,2,1,0:T(8,128)(2,1)}, u32[]{:S(2)}, u32[]{:S(2)}) %collective-permute-start.101) | collective-permute-done | bytes 786464 | tf_op jit(solution)/shard_map/ppermute | solution.py:64
  630.6 5.6 collective-permute-done.111
  636.8 5.9 collective-permute-done.102
  647.9 4.6 collective-permute-done.113
  661.0 4.7 collective-permute-done.106
  671.4 11.7 %collective-permute-done.81 = bf16[128,2048]{1,0:T(8,128)(2,1)S(1)} collective-permute-done((bf16[128,2048]{1,0:T(8,128)(2,1)S(1)}, bf16[128,2048]{1,0:T(8,128)(2,1)S(1)}, u32[]{:S(2)}, u32[]{:S(2)}) %collective-permute-start.81) | collective-permute-done | bytes 524320 | tf_op jit(solution)/shard_map/ppermute | solution.py:64
  684.8 9.4 %collective-permute-done.83 = bf16[128,2048]{1,0:T(8,128)(2,1)S(1)} collective-permute-done((bf16[128,2048]{1,0:T(8,128)(2,1)S(1)}, bf16[128,2048]{1,0:T(8,128)(2,1)S(1)}, u32[]{:S(2)}, u32[]{:S(2)}) %collective-permute-start.83) | collective-permute-done | bytes 524320 | tf_op jit(solution)/shard_map/ppermute | solution.py:64
  698.4 18.4 %collective-permute-done.122 = f32[4352]{0:T(1024)S(1)} collective-permute-done((f32[4352]{0:T(1024)S(1)}, f32[4352]{0:T(1024)S(1)}, u32[]{:S(2)}, u32[]{:S(2)}) %collective-permute-start.122) | collective-permute-done | bytes 17440 | tf_op jit(solution)/shard_map/ppermute | solution.py:64
  717.3 15.8 %collective-permute-done.123 = f32[4352]{0:T(1024)S(1)} collective-permute-done((f32[4352]{0:T(1024)S(1)}, f32[4352]{0:T(1024)S(1)}, u32[]{:S(2)}, u32[]{:S(2)}) %collective-permute-start.123) | collective-permute-done | bytes 17440 | tf_op jit(solution)/shard_map/ppermute | solution.py:64
  738.0 19.0 %collective-permute-done.57 = bf16[128,2048]{1,0:T(8,128)(2,1)S(1)} collective-permute-done((bf16[128,2048]{1,0:T(8,128)(2,1)S(1)}, bf16[128,2048]{1,0:T(8,128)(2,1)S(1)}, u32[]{:S(2)}, u32[]{:S(2)}) %collective-permute-start.57) | collective-permute-done | bytes 524320 | tf_op jit(solution)/shard_map/ppermute | solution.py:64
  773.4 13.0 %collective-permute-done.88 = bf16[128,512]{1,0:T(8,128)(2,1)S(1)} collective-permute-done((bf16[128,512]{1,0:T(8,128)(2,1)S(1)}, bf16[128,512]{1,0:T(8,128)(2,1)S(1)}, u32[]{:S(2)}, u32[]{:S(2)}) %collective-permute-start.88) | collective-permute-done | bytes 131104 | tf_op jit(solution)/shard_map/ppermute | solution.py:64
  787.2 7.3 collective-permute-done.92
  795.2 18.7 %collective-permute-done.98 = bf16[64,2048]{1,0:T(8,128)(2,1)S(1)} collective-permute-done((bf16[64,2048]{1,0:T(8,128)(2,1)S(1)}, bf16[64,2048]{1,0:T(8,128)(2,1)S(1)}, u32[]{:S(2)}, u32[]{:S(2)}) %collective-permute-start.98) | collective-permute-done | bytes 262176 | tf_op jit(solution)/shard_map/ppermute | solution.py:64
  (699 shorter events, 317.1 us)
Async XLA Ops:
  4.1 110.6 %collective-permute-start = (bf16[128,2048]{1,0:T(8,128)(2,1)}, bf16[128,2048]{1,0:T(8,128)(2,1)}, u32[]{:S(2)}, u32[]{:S(2)}) collective-permute-start(bf16[128,2048]{1,0:T(8,128)(2,1)} %fusion.28), channel_id=1, source_target_pairs={{0,1},{1,0},{2,3},{3,2},{4,5},{5,4},{6,7},{7,6},{8,9},{9,8},{10,11... | collective-permute-start | bytes 1572872 | tf_op jit(solution)/shard_map/ppermute | solution.py:67
  4.6 112.4 %collective-permute-start.1 = (bf16[128,2048]{1,0:T(8,128)(2,1)}, bf16[128,2048]{1,0:T(8,128)(2,1)}, u32[]{:S(2)}, u32[]{:S(2)}) collective-permute-start(bf16[128,2048]{1,0:T(8,128)(2,1)} %fusion.28), channel_id=1, source_target_pairs={{0,10},{2,8},{4,14},{6,12},{8,2},{10,0},{12,6},{14,4},{16,26},{18,... | collective-permute-start | bytes 1572872 | tf_op jit(solution)/shard_map/ppermute | solution.py:64
  31.1 250.0 %collective-permute-start.3 = (bf16[128,2048]{1,0:T(8,128)(2,1)}, bf16[128,2048]{1,0:T(8,128)(2,1)}, u32[]{:S(2)}, u32[]{:S(2)}) collective-permute-start(bf16[128,2048]{1,0:T(8,128)(2,1)} %fusion.28), channel_id=1, source_target_pairs={{0,2},{2,0},{4,6},{6,4},{8,10},{10,8},{12,14},{14,12},{16,18},{18,... | collective-permute-start | bytes 1572872 | tf_op jit(solution)/shard_map/ppermute | solution.py:64
  31.7 251.5 %collective-permute-start.5 = (bf16[128,2048]{1,0:T(8,128)(2,1)}, bf16[128,2048]{1,0:T(8,128)(2,1)}, u32[]{:S(2)}, u32[]{:S(2)}) collective-permute-start(bf16[128,2048]{1,0:T(8,128)(2,1)} %fusion.28), channel_id=1, source_target_pairs={{0,8},{2,10},{4,12},{6,14},{8,0},{10,2},{12,4},{14,6},{16,24},{18,... | collective-permute-start | bytes 1572872 | tf_op jit(solution)/shard_map/ppermute | solution.py:64
  117.0 82.1 %collective-permute-start.47 = (bf16[192,2048]{1,0:T(8,128)(2,1)S(1)}, bf16[192,2048]{1,0:T(8,128)(2,1)S(1)}, u32[]{:S(2)}, u32[]{:S(2)}) collective-permute-start(bf16[192,2048]{1,0:T(8,128)(2,1)S(1)} %copy-done.60), channel_id=1, source_target_pairs={{0,4},{2,6},{4,0},{6,2},{8,12},{10,14},{12,8},{14,10},{16,20},{18,... | collective-permute-start | bytes 2359304 | tf_op jit(solution)/shard_map/ppermute | solution.py:64
  119.7 37.4 %collective-permute-start.10 = (bf16[2,2,128,512]{3,2,1,0:T(8,128)(2,1)}, bf16[2,2,128,512]{3,2,1,0:T(8,128)(2,1)S(1)}, u32[]{:S(2)}, u32[]{:S(2)}) collective-permute-start(bf16[2,2,128,512]{3,2,1,0:T(8,128)(2,1)} %bitcast_dynamic-update-slice_fusion.57), channel_id=1, source_target_pairs={{0,4},{2,6},{4,0},{6,2},{8,12},{10,14},{12,8},{14,10},{16,20},{18,... | collective-permute-start | bytes 1572872 | tf_op jit(solution)/shard_map/ppermute | solution.py:64
  153.5 43.9 %collective-permute-start.11 = (bf16[2,2,128,512]{3,2,1,0:T(8,128)(2,1)}, bf16[2,2,128,512]{3,2,1,0:T(8,128)(2,1)S(1)}, u32[]{:S(2)}, u32[]{:S(2)}) collective-permute-start(bf16[2,2,128,512]{3,2,1,0:T(8,128)(2,1)} %bitcast_dynamic-update-slice_fusion.57), channel_id=1, source_target_pairs={{0,16},{2,18},{4,20},{6,22},{8,24},{10,26},{12,28},{14,30},{16,0},... | collective-permute-start | bytes 1572872 | tf_op jit(solution)/shard_map/ppermute | solution.py:64
  157.1 74.2 %collective-permute-start.48 = (bf16[192,2048]{1,0:T(8,128)(2,1)S(1)}, bf16[192,2048]{1,0:T(8,128)(2,1)}, u32[]{:S(2)}, u32[]{:S(2)}) collective-permute-start(bf16[192,2048]{1,0:T(8,128)(2,1)S(1)} %copy-done.60), channel_id=1, source_target_pairs={{0,16},{2,18},{4,20},{6,22},{8,24},{10,26},{12,28},{14,30},{16,0},... | collective-permute-start | bytes 2359304 | tf_op jit(solution)/shard_map/ppermute | solution.py:64
  197.5 37.4 %collective-permute-start.44 = (bf16[2,2,128,768]{3,2,1,0:T(8,128)(2,1)S(1)}, bf16[2,2,128,768]{3,2,1,0:T(8,128)(2,1)S(1)}, u32[]{:S(2)}, u32[]{:S(2)}) collective-permute-start(bf16[2,2,128,768]{3,2,1,0:T(8,128)(2,1)S(1)} %copy-done.45), channel_id=1, source_target_pairs={{0,4},{2,6},{4,0},{6,2},{8,12},{10,14},{12,8},{14,10},{16,20},{18,... | collective-permute-start | bytes 2359304 | tf_op jit(solution)/shard_map/ppermute | solution.py:64
  199.0 65.9 %collective-permute-start.45 = (bf16[2,2,128,768]{3,2,1,0:T(8,128)(2,1)S(1)}, bf16[2,2,128,768]{3,2,1,0:T(8,128)(2,1)}, u32[]{:S(2)}, u32[]{:S(2)}) collective-permute-start(bf16[2,2,128,768]{3,2,1,0:T(8,128)(2,1)S(1)} %copy-done.45), channel_id=1, source_target_pairs={{0,16},{2,18},{4,20},{6,22},{8,24},{10,26},{12,28},{14,30},{16,0},... | collective-permute-start | bytes 2359304 | tf_op jit(solution)/shard_map/ppermute | solution.py:64
  231.3 35.4 %collective-permute-start.38 = (bf16[2,2,128,768]{3,2,1,0:T(8,128)(2,1)}, bf16[2,2,128,768]{3,2,1,0:T(8,128)(2,1)S(1)}, u32[]{:S(2)}, u32[]{:S(2)}) collective-permute-start(bf16[2,2,128,768]{3,2,1,0:T(8,128)(2,1)} %bitcast_dynamic-update-slice_fusion.54), channel_id=1, source_target_pairs={{0,4},{2,6},{4,0},{6,2},{8,12},{10,14},{12,8},{14,10},{16,20},{18,... | collective-permute-start | bytes 2359304 | tf_op jit(solution)/shard_map/ppermute | solution.py:64
  234.9 46.1 %collective-permute-start.39 = (bf16[2,2,128,768]{3,2,1,0:T(8,128)(2,1)}, bf16[2,2,128,768]{3,2,1,0:T(8,128)(2,1)S(1)}, u32[]{:S(2)}, u32[]{:S(2)}) collective-permute-start(bf16[2,2,128,768]{3,2,1,0:T(8,128)(2,1)} %bitcast_dynamic-update-slice_fusion.54), channel_id=1, source_target_pairs={{0,16},{2,18},{4,20},{6,22},{8,24},{10,26},{12,28},{14,30},{16,0},... | collective-permute-start | bytes 2359304 | tf_op jit(solution)/shard_map/ppermute | solution.py:64
  294.3 59.8 %collective-permute-start.64 = (bf16[128,2048]{1,0:T(8,128)(2,1)}, bf16[128,2048]{1,0:T(8,128)(2,1)}, u32[]{:S(2)}, u32[]{:S(2)}) collective-permute-start(bf16[128,2048]{1,0:T(8,128)(2,1)} %collective-permute-done.63), channel_id=1, source_target_pairs={{0,1},{1,0},{2,3},{3,2},{4,5},{5,4},{6,7},{7,6},{8,9},{9,8},{10,11... | collective-permute-start | bytes 1572872 | tf_op jit(solution)/shard_map/ppermute | solution.py:67
  299.2 46.2 %collective-permute-start.49 = (bf16[192,2048]{1,0:T(8,128)(2,1)}, bf16[192,2048]{1,0:T(8,128)(2,1)}, u32[]{:S(2)}, u32[]{:S(2)}) collective-permute-start(bf16[192,2048]{1,0:T(8,128)(2,1)} %collective-permute-done.48), channel_id=1, source_target_pairs={{0,4},{2,6},{4,0},{6,2},{8,12},{10,14},{12,8},{14,10},{16,20},{18,... | collective-permute-start | bytes 2359304 | tf_op jit(solution)/shard_map/ppermute | solution.py:64
  302.5 53.3 %collective-permute-start.46 = (bf16[2,2,128,768]{3,2,1,0:T(8,128)(2,1)}, bf16[2,2,128,768]{3,2,1,0:T(8,128)(2,1)}, u32[]{:S(2)}, u32[]{:S(2)}) collective-permute-start(bf16[2,2,128,768]{3,2,1,0:T(8,128)(2,1)} %collective-permute-done.45), channel_id=1, source_target_pairs={{0,4},{2,6},{4,0},{6,2},{8,12},{10,14},{12,8},{14,10},{16,20},{18,... | collective-permute-start | bytes 2359304 | tf_op jit(solution)/shard_map/ppermute | solution.py:64
  305.4 33.6 %collective-permute-start.20 = (bf16[1,2,64,2048]{3,2,1,0:T(8,128)(2,1)}, bf16[1,2,64,2048]{3,2,1,0:T(8,128)(2,1)}, u32[]{:S(2)}, u32[]{:S(2)}) collective-permute-start(bf16[1,2,64,2048]{3,2,1,0:T(8,128)(2,1)} %get-tuple-element.117), channel_id=1, source_target_pairs={{0,1},{1,0},{2,3},{3,2},{4,5},{5,4},{6,7},{7,6},{8,9},{9,8},{10,11... | collective-permute-start | bytes 1572872 | tf_op jit(solution)/shard_map/ppermute | solution.py:67
  352.1 36.6 %collective-permute-start.50 = (bf16[2,1,192,2048]{3,2,0,1:T(8,128)(2,1)}, bf16[2,1,192,2048]{3,2,0,1:T(8,128)(2,1)}, u32[]{:S(2)}, u32[]{:S(2)}) collective-permute-start(bf16[2,1,192,2048]{3,2,0,1:T(8,128)(2,1)} %get-tuple-element.83), channel_id=1, source_target_pairs={{0,1},{1,0},{2,3},{3,2},{4,5},{5,4},{6,7},{7,6},{8,9},{9,8},{10,11... | collective-permute-start | bytes 4718600 | tf_op jit(solution)/shard_map/ppermute | solution.py:67
  354.0 25.4 %collective-permute-start.25 = (bf16[128,2048]{1,0:T(8,128)(2,1)}, bf16[128,2048]{1,0:T(8,128)(2,1)}, u32[]{:S(2)}, u32[]{:S(2)}) collective-permute-start(bf16[128,2048]{1,0:T(8,128)(2,1)} %get-tuple-element.60), channel_id=1, source_target_pairs={{0,2},{2,0},{4,6},{6,4},{8,10},{10,8},{12,14},{14,12},{16,18},{18,... | collective-permute-start | bytes 1572872 | tf_op jit(solution)/shard_map/ppermute | solution.py:64
  355.8 23.7 %collective-permute-start.27 = (bf16[128,2048]{1,0:T(8,128)(2,1)}, bf16[128,2048]{1,0:T(8,128)(2,1)}, u32[]{:S(2)}, u32[]{:S(2)}) collective-permute-start(bf16[128,2048]{1,0:T(8,128)(2,1)} %get-tuple-element.59), channel_id=1, source_target_pairs={{0,8},{2,10},{4,12},{6,14},{8,0},{10,2},{12,4},{14,6},{16,24},{18,... | collective-permute-start | bytes 1572872 | tf_op jit(solution)/shard_map/ppermute | solution.py:64
  382.7 27.1 %collective-permute-start.28 = (bf16[128,2048]{1,0:T(8,128)(2,1)S(1)}, bf16[128,2048]{1,0:T(8,128)(2,1)S(1)}, u32[]{:S(2)}, u32[]{:S(2)}) collective-permute-start(bf16[128,2048]{1,0:T(8,128)(2,1)S(1)} %get-tuple-element.30), channel_id=1, source_target_pairs={{0,1},{1,0},{2,3},{3,2},{4,5},{5,4},{6,7},{7,6},{8,9},{9,8},{10,11... | collective-permute-start | bytes 1572872 | tf_op jit(solution)/shard_map/ppermute | solution.py:67
  384.1 25.2 %collective-permute-start.31 = (bf16[128,2048]{1,0:T(8,128)(2,1)S(1)}, bf16[128,2048]{1,0:T(8,128)(2,1)S(1)}, u32[]{:S(2)}, u32[]{:S(2)}) collective-permute-start(bf16[128,2048]{1,0:T(8,128)(2,1)S(1)} %get-tuple-element.30), channel_id=1, source_target_pairs={{0,2},{2,0},{4,6},{6,4},{8,10},{10,8},{12,14},{14,12},{16,18},{18,... | collective-permute-start | bytes 1572872 | tf_op jit(solution)/shard_map/ppermute | solution.py:64
  465.1 25.1 %collective-permute-start.65 = (bf16[128,2048]{1,0:T(8,128)(2,1)}, bf16[128,2048]{1,0:T(8,128)(2,1)S(1)}, u32[]{:S(2)}, u32[]{:S(2)}) collective-permute-start(bf16[128,2048]{1,0:T(8,128)(2,1)} %get-tuple-element.40), channel_id=1, source_target_pairs={{0,1},{1,0},{2,3},{3,2},{4,5},{5,4},{6,7},{7,6},{8,9},{9,8},{10,11... | collective-permute-start | bytes 1572872 | tf_op jit(solution)/shard_map/ppermute | solution.py:67
  474.6 88.0 %collective-permute-start.118 = (bf16[2,1,192,2048]{3,2,1,0:T(8,128)(2,1)S(1)}, bf16[2,1,192,2048]{3,2,1,0:T(8,128)(2,1)S(1)}, u32[]{:S(2)}, u32[]{:S(2)}) collective-permute-start(bf16[2,1,192,2048]{3,2,1,0:T(8,128)(2,1)S(1)} %get-tuple-element.81), channel_id=1, source_target_pairs={{0,1},{1,0},{2,3},{3,2},{4,5},{5,4},{6,7},{7,6},{8,9},{9,8},{10,11... | collective-permute-start | bytes 4718600 | tf_op jit(solution)/shard_map/ppermute | solution.py:67
  486.5 24.9 %collective-permute-start.69 = (bf16[128,2048]{1,0:T(8,128)(2,1)S(1)}, bf16[128,2048]{1,0:T(8,128)(2,1)S(1)}, u32[]{:S(2)}, u32[]{:S(2)}) collective-permute-start(bf16[128,2048]{1,0:T(8,128)(2,1)S(1)} %get-tuple-element.46), channel_id=1, source_target_pairs={{0,2},{2,0},{4,6},{6,4},{8,10},{10,8},{12,14},{14,12},{16,18},{18,... | collective-permute-start | bytes 1572872 | tf_op jit(solution)/shard_map/ppermute | solution.py:64
  490.3 54.5 %collective-permute-start.109 = (bf16[2,2,2,128,768]{4,3,2,1,0:T(8,128)(2,1)S(1)}, bf16[2,2,2,128,768]{4,3,2,1,0:T(8,128)(2,1)S(1)}, u32[]{:S(2)}, u32[]{:S(2)}) collective-permute-start(bf16[2,2,2,128,768]{4,3,2,1,0:T(8,128)(2,1)S(1)} %pad_maximum_fusion.1), channel_id=1, source_target_pairs={{0,4},{2,6},{4,0},{6,2},{8,12},{10,14},{12,8},{14,10},{16,20},{18,... | collective-permute-start | bytes 4718600 | tf_op jit(solution)/shard_map/ppermute | solution.py:64
  514.3 45.3 %collective-permute-start.100 = (bf16[2,2,2,128,768]{4,3,2,1,0:T(8,128)(2,1)S(1)}, bf16[2,2,2,128,768]{4,3,2,1,0:T(8,128)(2,1)S(1)}, u32[]{:S(2)}, u32[]{:S(2)}) collective-permute-start(bf16[2,2,2,128,768]{4,3,2,1,0:T(8,128)(2,1)S(1)} %pad_maximum_fusion), channel_id=1, source_target_pairs={{0,4},{2,6},{4,0},{6,2},{8,12},{10,14},{12,8},{14,10},{16,20},{18,... | collective-permute-start | bytes 4718600 | tf_op jit(solution)/shard_map/ppermute | solution.py:64
  518.6 23.8 %collective-permute-start.75 = (bf16[128,2048]{1,0:T(8,128)(2,1)S(1)}, bf16[128,2048]{1,0:T(8,128)(2,1)S(1)}, u32[]{:S(2)}, u32[]{:S(2)}) collective-permute-start(bf16[128,2048]{1,0:T(8,128)(2,1)S(1)} %get-tuple-element.27), channel_id=1, source_target_pairs={{0,2},{2,0},{4,6},{6,4},{8,10},{10,8},{12,14},{14,12},{16,18},{18,... | collective-permute-start | bytes 1572872 | tf_op jit(solution)/shard_map/ppermute | solution.py:64
  542.4 25.3 %collective-permute-start.74 = (bf16[128,2048]{1,0:T(8,128)(2,1)S(1)}, bf16[128,2048]{1,0:T(8,128)(2,1)S(1)}, u32[]{:S(2)}, u32[]{:S(2)}) collective-permute-start(bf16[128,2048]{1,0:T(8,128)(2,1)S(1)} %collective-permute-done.73), channel_id=1, source_target_pairs={{0,1},{1,0},{2,3},{3,2},{4,5},{5,4},{6,7},{7,6},{8,9},{9,8},{10,11... | collective-permute-start | bytes 1572872 | tf_op jit(solution)/shard_map/ppermute | solution.py:67
  559.6 54.2 %collective-permute-start.110 = (bf16[2,2,128,768]{3,2,1,0:T(8,128)(2,1)}, bf16[2,2,128,768]{3,2,1,0:T(8,128)(2,1)}, u32[]{:S(2)}, u32[]{:S(2)}) collective-permute-start(bf16[2,2,128,768]{3,2,1,0:T(8,128)(2,1)} %fusion.87), channel_id=1, source_target_pairs={{0,16},{2,18},{4,20},{6,22},{8,24},{10,26},{12,28},{14,30},{16,0},... | collective-permute-start | bytes 2359304 | tf_op jit(solution)/shard_map/ppermute | solution.py:64
  562.7 66.5 %collective-permute-start.101 = (bf16[2,2,128,768]{3,2,1,0:T(8,128)(2,1)}, bf16[2,2,128,768]{3,2,1,0:T(8,128)(2,1)}, u32[]{:S(2)}, u32[]{:S(2)}) collective-permute-start(bf16[2,2,128,768]{3,2,1,0:T(8,128)(2,1)} %fusion.85), channel_id=1, source_target_pairs={{0,16},{2,18},{4,20},{6,22},{8,24},{10,26},{12,28},{14,30},{16,0},... | collective-permute-start | bytes 2359304 | tf_op jit(solution)/shard_map/ppermute | solution.py:64
  607.6 37.3 %collective-permute-start.80 = (bf16[128,2048]{1,0:T(8,128)(2,1)S(1)}, bf16[128,2048]{1,0:T(8,128)(2,1)S(1)}, u32[]{:S(2)}, u32[]{:S(2)}) collective-permute-start(bf16[128,2048]{1,0:T(8,128)(2,1)S(1)} %get-tuple-element.36), channel_id=1, source_target_pairs={{0,1},{1,0},{2,3},{3,2},{4,5},{5,4},{6,7},{7,6},{8,9},{9,8},{10,11... | collective-permute-start | bytes 1572872 | tf_op jit(solution)/shard_map/ppermute | solution.py:67
  607.7 39.5 %collective-permute-start.82 = (bf16[128,2048]{1,0:T(8,128)(2,1)S(1)}, bf16[128,2048]{1,0:T(8,128)(2,1)S(1)}, u32[]{:S(2)}, u32[]{:S(2)}) collective-permute-start(bf16[128,2048]{1,0:T(8,128)(2,1)S(1)} %get-tuple-element.35), channel_id=1, source_target_pairs={{0,1},{1,0},{2,3},{3,2},{4,5},{5,4},{6,7},{7,6},{8,9},{9,8},{10,11... | collective-permute-start | bytes 1572872 | tf_op jit(solution)/shard_map/ppermute | solution.py:67
  608.2 39.0 %collective-permute-start.84 = (bf16[128,2048]{1,0:T(8,128)(2,1)S(1)}, bf16[128,2048]{1,0:T(8,128)(2,1)S(1)}, u32[]{:S(2)}, u32[]{:S(2)}) collective-permute-start(bf16[128,2048]{1,0:T(8,128)(2,1)S(1)} %get-tuple-element.34), channel_id=1, source_target_pairs={{0,1},{1,0},{2,3},{3,2},{4,5},{5,4},{6,7},{7,6},{8,9},{9,8},{10,11... | collective-permute-start | bytes 1572872 | tf_op jit(solution)/shard_map/ppermute | solution.py:67
  613.8 29.3 %collective-permute-start.95 = (bf16[1,128,2048]{2,1,0:T(8,128)(2,1)S(1)}, bf16[1,128,2048]{2,1,0:T(8,128)(2,1)S(1)}, u32[]{:S(2)}, u32[]{:S(2)}) collective-permute-start(bf16[1,128,2048]{2,1,0:T(8,128)(2,1)S(1)} %get-tuple-element.109), channel_id=1, source_target_pairs={{0,2},{2,0},{4,6},{6,4},{8,10},{10,8},{12,14},{14,12},{16,18},{18,... | collective-permute-start | bytes 1572872 | tf_op jit(solution)/shard_map/ppermute | solution.py:64
  642.7 28.5 %collective-permute-start.79 = (bf16[128,2048]{1,0:T(8,128)(2,1)S(1)}, bf16[128,2048]{1,0:T(8,128)(2,1)S(1)}, u32[]{:S(2)}, u32[]{:S(2)}) collective-permute-start(bf16[128,2048]{1,0:T(8,128)(2,1)S(1)} %get-tuple-element.33), channel_id=1, source_target_pairs={{0,1},{1,0},{2,3},{3,2},{4,5},{5,4},{6,7},{7,6},{8,9},{9,8},{10,11... | collective-permute-start | bytes 1572872 | tf_op jit(solution)/shard_map/ppermute | solution.py:67
  643.1 52.7 %collective-permute-start.86 = (bf16[2,2,2,128,512]{4,3,2,1,0:T(8,128)(2,1)S(1)}, bf16[2,2,2,128,512]{4,3,2,1,0:T(8,128)(2,1)S(1)}, u32[]{:S(2)}, u32[]{:S(2)}) collective-permute-start(bf16[2,2,2,128,512]{4,3,2,1,0:T(8,128)(2,1)S(1)} %pad_maximum_fusion.4), channel_id=1, source_target_pairs={{0,4},{2,6},{4,0},{6,2},{8,12},{10,14},{12,8},{14,10},{16,20},{18,... | collective-permute-start | bytes 3145736 | tf_op jit(solution)/shard_map/ppermute | solution.py:64
  669.3 25.0 %collective-permute-start.83 = (bf16[128,2048]{1,0:T(8,128)(2,1)S(1)}, bf16[128,2048]{1,0:T(8,128)(2,1)S(1)}, u32[]{:S(2)}, u32[]{:S(2)}) collective-permute-start(bf16[128,2048]{1,0:T(8,128)(2,1)S(1)} %get-tuple-element.39), channel_id=1, source_target_pairs={{0,2},{2,0},{4,6},{6,4},{8,10},{10,8},{12,14},{14,12},{16,18},{18,... | collective-permute-start | bytes 1572872 | tf_op jit(solution)/shard_map/ppermute | solution.py:64
  670.0 25.1 %collective-permute-start.85 = (bf16[128,2048]{1,0:T(8,128)(2,1)S(1)}, bf16[128,2048]{1,0:T(8,128)(2,1)S(1)}, u32[]{:S(2)}, u32[]{:S(2)}) collective-permute-start(bf16[128,2048]{1,0:T(8,128)(2,1)S(1)} %get-tuple-element.38), channel_id=1, source_target_pairs={{0,8},{2,10},{4,12},{6,14},{8,0},{10,2},{12,4},{14,6},{16,24},{18,... | collective-permute-start | bytes 1572872 | tf_op jit(solution)/shard_map/ppermute | solution.py:64
  671.3 63.6 %collective-permute-start.51 = (bf16[128,2048]{1,0:T(8,128)(2,1)S(1)}, bf16[128,2048]{1,0:T(8,128)(2,1)S(1)}, u32[]{:S(2)}, u32[]{:S(2)}) collective-permute-start(bf16[128,2048]{1,0:T(8,128)(2,1)S(1)} %copy-done.70), channel_id=1, source_target_pairs={{0,1},{1,0},{2,3},{3,2},{4,5},{5,4},{6,7},{7,6},{8,9},{9,8},{10,11... | collective-permute-start | bytes 1572872 | tf_op jit(solution)/shard_map/ppermute | solution.py:67
  683.1 52.4 %collective-permute-start.53 = (bf16[128,2048]{1,0:T(8,128)(2,1)S(1)}, bf16[128,2048]{1,0:T(8,128)(2,1)S(1)}, u32[]{:S(2)}, u32[]{:S(2)}) collective-permute-start(bf16[128,2048]{1,0:T(8,128)(2,1)S(1)} %copy-done.64), channel_id=1, source_target_pairs={{0,10},{2,8},{4,14},{6,12},{8,2},{10,0},{12,6},{14,4},{16,26},{18,... | collective-permute-start | bytes 1572872 | tf_op jit(solution)/shard_map/ppermute | solution.py:64
  694.2 42.8 %collective-permute-start.55 = (bf16[128,2048]{1,0:T(8,128)(2,1)S(1)}, bf16[128,2048]{1,0:T(8,128)(2,1)S(1)}, u32[]{:S(2)}, u32[]{:S(2)}) collective-permute-start(bf16[128,2048]{1,0:T(8,128)(2,1)S(1)} %copy-done.63), channel_id=1, source_target_pairs={{0,2},{2,0},{4,6},{6,4},{8,10},{10,8},{12,14},{14,12},{16,18},{18,... | collective-permute-start | bytes 1572872 | tf_op jit(solution)/shard_map/ppermute | solution.py:64
  695.9 64.9 %collective-permute-start.119 = (bf16[2,192,2048]{2,1,0:T(8,128)(2,1)S(1)}, bf16[2,192,2048]{2,1,0:T(8,128)(2,1)S(1)}, u32[]{:S(2)}, u32[]{:S(2)}) collective-permute-start(bf16[2,192,2048]{2,1,0:T(8,128)(2,1)S(1)} %copy-done.56), channel_id=1, source_target_pairs={{0,4},{2,6},{4,0},{6,2},{8,12},{10,14},{12,8},{14,10},{16,20},{18,... | collective-permute-start | bytes 4718600 | tf_op jit(solution)/shard_map/ppermute | solution.py:64
  733.2 23.8 %collective-permute-start.57 = (bf16[128,2048]{1,0:T(8,128)(2,1)S(1)}, bf16[128,2048]{1,0:T(8,128)(2,1)S(1)}, u32[]{:S(2)}, u32[]{:S(2)}) collective-permute-start(bf16[128,2048]{1,0:T(8,128)(2,1)S(1)} %copy-done.62), channel_id=1, source_target_pairs={{0,8},{2,10},{4,12},{6,14},{8,0},{10,2},{12,4},{14,6},{16,24},{18,... | collective-permute-start | bytes 1572872 | tf_op jit(solution)/shard_map/ppermute | solution.py:64
  734.9 34.4 %collective-permute-start.97 = (bf16[2,64,2048]{2,1,0:T(8,128)(2,1)S(1)}, bf16[2,64,2048]{2,1,0:T(8,128)(2,1)S(1)}, u32[]{:S(2)}, u32[]{:S(2)}) collective-permute-start(bf16[2,64,2048]{2,1,0:T(8,128)(2,1)S(1)} %pad_maximum_fusion.6), channel_id=1, source_target_pairs={{0,4},{2,6},{4,0},{6,2},{8,12},{10,14},{12,8},{14,10},{16,20},{18,... | collective-permute-start | bytes 1572872 | tf_op jit(solution)/shard_map/ppermute | solution.py:64
  735.5 32.0 %collective-permute-start.87 = (bf16[2,2,128,512]{3,2,1,0:T(8,128)(2,1)S(1)}, bf16[2,2,128,512]{3,2,1,0:T(8,128)(2,1)S(1)}, u32[]{:S(2)}, u32[]{:S(2)}) collective-permute-start(bf16[2,2,128,512]{3,2,1,0:T(8,128)(2,1)S(1)} %fusion.109), channel_id=1, source_target_pairs={{0,16},{2,18},{4,20},{6,22},{8,24},{10,26},{12,28},{14,30},{16,0},... | collective-permute-start | bytes 1572872 | tf_op jit(solution)/shard_map/ppermute | solution.py:64
  765.2 49.3 %collective-permute-start.120 = (bf16[192,2048]{1,0:T(8,128)(2,1)S(1)}, bf16[192,2048]{1,0:T(8,128)(2,1)S(1)}, u32[]{:S(2)}, u32[]{:S(2)}) collective-permute-start(bf16[192,2048]{1,0:T(8,128)(2,1)S(1)} %fusion.88), channel_id=1, source_target_pairs={{0,16},{2,18},{4,20},{6,22},{8,24},{10,26},{12,28},{14,30},{16,0},... | collective-permute-start | bytes 2359304 | tf_op jit(solution)/shard_map/ppermute | solution.py:64
  769.5 44.4 %collective-permute-start.98 = (bf16[64,2048]{1,0:T(8,128)(2,1)S(1)}, bf16[64,2048]{1,0:T(8,128)(2,1)S(1)}, u32[]{:S(2)}, u32[]{:S(2)}) collective-permute-start(bf16[64,2048]{1,0:T(8,128)(2,1)S(1)} %fusion.128), channel_id=1, source_target_pairs={{0,16},{2,18},{4,20},{6,22},{8,24},{10,26},{12,28},{14,30},{16,0},... | collective-permute-start | bytes 786440 | tf_op jit(solution)/shard_map/ppermute | solution.py:64
  786.6 27.5 %collective-permute-start.89 = (bf16[128,512]{1,0:T(8,128)(2,1)S(1)}, bf16[128,512]{1,0:T(8,128)(2,1)S(1)}, u32[]{:S(2)}, u32[]{:S(2)}) collective-permute-start(bf16[128,512]{1,0:T(8,128)(2,1)S(1)} %collective-permute-done.88), channel_id=1, source_target_pairs={{0,1},{1,0},{2,3},{3,2},{4,5},{5,4},{6,7},{7,6},{8,9},{9,8},{10,11... | collective-permute-start | bytes 393224 | tf_op jit(solution)/shard_map/ppermute | solution.py:67
  (174 other events, 1952.9 us)

commit v2 on v1

v2 whole, which is shorter than its diff:
```python
import functools
import math

import jax
import jax.numpy as jnp
from jax import lax
from jax.experimental import pallas as pl
from jax.experimental.pallas import tpu as pltpu
from jax.sharding import PartitionSpec as P

HD = 128
NORM_EPS = 1e-06
NEG_FILL = -1e30
ROPE_BASE = 1000000.0
BF16 = jnp.bfloat16
F32 = jnp.float32


def dot(x, y):
    return jnp.dot(x, y, preferred_element_type=F32)


def dot_tn(x, y):
    return lax.dot_general(x, y, (((0,), (0,)), ((), ())), preferred_element_type=F32)


def dot_nt(x, y):
    return lax.dot_general(x, y, (((1,), (1,)), ((), ())), preferred_element_type=F32)


def rms_scale(v, gain):
    return v * lax.rsqrt(jnp.mean(v * v, axis=-1, keepdims=True) + NORM_EPS) * gain


class Grid:
    def __init__(self, mesh):
        n = mesh.shape["fsdp"]
        assert mesh.shape["rep"] == 2 and n % 16 == 0 and n & (n - 1) == 0
        self.n = n
        self.F = n // 4
        self.B = 2 ** (int(math.log2(self.F)) // 2)
        self.A = self.F // self.B
        self.Q = self.F // 4
        self.tmask, self.umask = 2 * self.B, 1

    def place(self):
        i = lax.axis_index("fsdp")
        self.u = i % 2
        self.b = (i // 2) % self.B
        self.t = (i // (2 * self.B)) % 2
        self.a = i // (4 * self.B)
        self.c = lax.axis_index("rep")

    def px(self, x, mask):
        return lax.ppermute(x, "fsdp", [(i, i ^ mask) for i in range(self.n)])

    def pc(self, x):
        return lax.ppermute(x, "rep", [(0, 1), (1, 0)])

    def pa(self, x, delta):
        return self.px(x, 4 * self.B * delta)

    def pb(self, x, delta):
        return self.px(x, 2 * delta)

    def pt(self, x, dt, du):
        return self.px(x, dt * self.tmask + du * self.umask)

    def kv_head(self, t, u, c, rows):
        first = (u * 2 + c) * self.Q
        block = ((first // self.B * 2 + t) * self.B + first % self.B) * 2
        return block * rows // (2 * HD)

    def hidden_blocks(self, t, u, c):
        half = self.B // 2
        return [
            ((a * 2 + t) * self.B + c * half + b) * 2 + u
            for a in range(self.A)
            for b in range(half)
        ]


SHIFTS = ((1, 1), (0, 1), (1, 0))


def pick(x, *index):
    lead = len(index)
    starts = list(index) + [0] * (x.ndim - lead)
    sizes = [1] * lead + list(x.shape[lead:])
    return lax.dynamic_slice(x, starts, sizes).reshape(x.shape[lead:])


def put(x, piece, *index):
    lead = len(index)
    starts = list(index) + [0] * (x.ndim - lead)
    return lax.dynamic_update_slice(x, piece.reshape((1,) * lead + x.shape[lead:]), starts)


def swap_halves(g, own, other):
    return jnp.where(g.c == 0, jnp.stack([own, other]), jnp.stack([other, own]))


class Live(dict):
    __getattr__ = dict.__getitem__
    __setattr__ = dict.__setitem__


ORDER = ((0, 0),) + SHIFTS
LANES = 128


def cut_columns(sources, pieces):
    rows = sources[0].shape[0]
    cuts = [cut for piece in pieces for cut in piece]
    if any(c[2] % LANES for c in cuts) or rows % 16:
        return [
            jnp.concatenate(
                [lax.dynamic_slice(sources[k], (0, at), (rows, w)) for k, at, w in piece], axis=1
            )
            for piece in pieces
        ]

    def kernel(at_ref, *refs):
        ins, outs = refs[: len(sources)], refs[len(sources) :]
        j = 0
        for out, piece in zip(outs, pieces):
            to = 0
            for k, _, w in piece:
                start = pl.multiple_of(at_ref[j] * LANES, LANES)
                out[:, to : to + w] = ins[k][:, pl.ds(start, w)]
                to += w
                j += 1

    vmem = pl.BlockSpec(memory_space=pltpu.VMEM)
    return pl.pallas_call(
        kernel,
        in_specs=[pl.BlockSpec(memory_space=pltpu.SMEM)] + [vmem] * len(sources),
        out_specs=[vmem] * len(pieces),
        out_shape=[
            jax.ShapeDtypeStruct((rows, sum(w for _, _, w in piece)), sources[0].dtype)
            for piece in pieces
        ],
        compiler_params=pltpu.CompilerParams(vmem_limit_bytes=24 << 20),
        name="cut_columns",
    )(jnp.stack([jnp.asarray(at // LANES, jnp.int32) for _, at, _ in cuts]), *sources)


def place_columns(pieces, widths, places):
    rows = pieces[0].shape[0]
    if any(p[2] % LANES or p[1] % LANES for p in places) or rows % 16:
        outs = [jnp.zeros((rows, w), F32) for w in widths]
        for k, at, w, o, to in places:
            part = pieces[k][:, at : at + w].astype(F32)
            outs[o] = lax.dynamic_update_slice(outs[o], part, (0, to))
        return outs

    def kernel(to_ref, *refs):
        ins, outs = refs[: len(pieces)], refs[len(pieces) :]
        for j, (k, at, w, o, _) in enumerate(places):
            start = pl.multiple_of(to_ref[j] * LANES, LANES)
            outs[o][:, pl.ds(start, w)] = ins[k][:, at : at + w].astype(F32)

    vmem = pl.BlockSpec(memory_space=pltpu.VMEM)
    return pl.pallas_call(
        kernel,
        in_specs=[pl.BlockSpec(memory_space=pltpu.SMEM)] + [vmem] * len(pieces),
        out_specs=[vmem] * len(widths),
        out_shape=[jax.ShapeDtypeStruct((rows, w), F32) for w in widths],
        compiler_params=pltpu.CompilerParams(vmem_limit_bytes=24 << 20),
        name="place_columns",
    )(jnp.stack([jnp.asarray(to // LANES, jnp.int32) for *_, to in places]), *pieces)


def chips_swap(g, pieces):
    return [pieces[0]] + [g.pt(x, dt, du) for x, (dt, du) in zip(pieces[1:], SHIFTS)]


def gather_one(g, x):
    return x, g.pt(x, 0, 1), g.pt(x, 1, 0)


def gather_two(g, near):
    own, along_u, along_t = near
    return [own, g.pt(along_t, 0, 1), along_u, along_t]


def scatter_one(g, blocks):
    own, far, to_u, to_t = blocks
    return own, to_u, to_t, g.pt(far.astype(BF16), 0, 1)


def scatter_two(g, state):
    own, to_u, to_t, relayed = state
    return (
        own,
        g.pt(to_u.astype(BF16), 0, 1),
        g.pt((to_t + relayed.astype(F32)).astype(BF16), 1, 0),
    )


def add_all(pieces):
    total = pieces[0]
    for x in pieces[1:]:
        total = total + x.astype(F32)
    return total


def permute_joined(permute, arrays):
    out = [None] * len(arrays)
    for n in sorted({x.shape[-1] for x in arrays}):
        which = [k for k, x in enumerate(arrays) if x.shape[-1] == n]
        flat = [arrays[k].reshape(-1, n) for k in which]
        got = permute(jnp.concatenate(flat) if len(flat) > 1 else flat[0])
        at = 0
        for k, x in zip(which, flat):
            out[k] = got[at : at + x.shape[0]].reshape(arrays[k].shape)
            at += x.shape[0]
    return out


class Shards:
    def __init__(self, g, live):
        self.g, self.live = g, live

    def fetch(self, name, parts):
        self.live[name] = {(p, 0, 0): x for p, x in enumerate(parts)}

    def fetch_a(self, *jobs):
        for d in range(1, self.g.A):
            got = permute_joined(
                lambda x, d=d: self.g.pa(x, d), [self.live[n][p, 0, 0] for n, p in jobs]
            )
            for (n, p), x in zip(jobs, got):
                self.live[n] = {**self.live[n], (p, d, 0): x}

    def fetch_b(self, *jobs):
        jobs = [
            (n, p, d) for n, p, rest in jobs for d in (range(1, self.g.A) if rest else (0,))
        ]
        for e in range(1, self.g.B):
            got = permute_joined(
                lambda x, e=e: self.g.pb(x, e), [self.live[n][p, d, 0] for n, p, d in jobs]
            )
            for (n, p, d), x in zip(jobs, got):
                self.live[n] = {**self.live[n], (p, d, e): x}

    def total(self, name, parts):
        g = self.g
        self.live[name] = {}
        for p, x in enumerate(parts):
            by_b = x.swapaxes(0, 1)
            sent = [pick(by_b, g.b ^ e).astype(BF16) for e in range(1, g.B)]
            self.live[name][p] = (pick(by_b, g.b), sent)

    def total_b(self, *jobs):
        g = self.g
        got = [
            permute_joined(lambda x, e=e: g.pb(x, e), [self.live[n][p][1][e - 1] for n, p in jobs])
            for e in range(1, g.B)
        ]
        for k, (n, p) in enumerate(jobs):
            self.live[n] = {**self.live[n], p: (self.live[n][p][0], [x[k] for x in got])}

    def prepare_a(self, *jobs):
        g = self.g
        for n, p in jobs:
            kept, got = self.live[n][p]
            rows = add_all([kept.astype(F32)] + got)
            sent = [pick(rows, g.a ^ d).astype(BF16) for d in range(1, g.A)]
            self.live[n] = {**self.live[n], p: (pick(rows, g.a), sent)}

    def total_a(self, *jobs):
        g = self.g
        got = [
            permute_joined(lambda x, d=d: g.pa(x, d), [self.live[n][p][1][d - 1] for n, p in jobs])
            for d in range(1, g.A)
        ]
        for k, (n, p) in enumerate(jobs):
            self.live[n] = {**self.live[n], p: (self.live[n][p][0], [x[k] for x in got])}

    def finish(self, *names):
        for n in names:
            self.live[n] = {
                p: add_all([kept] + got).astype(BF16) for p, (kept, got) in self.live[n].items()
            }

    def rows(self, name):
        g, state = self.g, self.live[name]
        parts = 1 + max(p for p, _, _ in state)
        height = [state[p, 0, 0].shape[0] for p in range(parts)]
        out = jnp.zeros((g.A, g.B, sum(height)) + state[0, 0, 0].shape[1:], BF16)
        for (p, d, e), x in state.items():
            starts = [g.a ^ d, g.b ^ e, sum(height[:p])] + [0] * (x.ndim - 1)
            out = lax.dynamic_update_slice(out, x[None, None], starts)
        return out

    def columns(self, name):
        g, state = self.g, self.live[name]
        pieces, rows = [], []
        for (p, d, e), x in state.items():
            pieces.append(x)
            for k in range(2):
                dt, du = ORDER[2 * p + k]
                rows.append(
                    (((g.a ^ d) * 2 + (g.t ^ dt)) * g.B + (g.b ^ e)) * 2 + (g.u ^ du)
                )
        return jnp.stack(rows).astype(jnp.int32), pieces

    def total_rows(self):
        g = self.g
        return jnp.stack(
            [
                (a * 2 + t) * g.B + (g.b ^ e)
                for t in range(2)
                for e in range(g.B)
                for a in range(g.A)
            ]
        ).astype(jnp.int32)

    def total_split(self, name, arrays):
        n = self.g.B
        self.live[name] = {p: (arrays[p * n], arrays[p * n + 1 : (p + 1) * n]) for p in range(2)}


def columns_pieces(g, state):
    both = jnp.stack([state[0], state[1]])
    return [pick(both, g.t ^ dt, g.u ^ du) for dt, du in ORDER]


def kernel_call(kernel, ins, outs, scratch, name):
    vmem = pl.BlockSpec(memory_space=pltpu.VMEM)
    smem = pl.BlockSpec(memory_space=pltpu.SMEM)
    return pl.pallas_call(
        kernel,
        in_specs=[smem if x.dtype == jnp.int32 else vmem for x in ins],
        out_specs=[vmem] * len(outs),
        out_shape=[jax.ShapeDtypeStruct(shape, dtype) for shape, dtype in outs],
        scratch_shapes=[pltpu.VMEM(shape, dtype) for shape, dtype in scratch],
        compiler_params=pltpu.CompilerParams(vmem_limit_bytes=20 << 20),
        cost_estimate=pl.CostEstimate(flops=1 << 20, bytes_accessed=1 << 16, transcendentals=0),
        name=name,
    )(*ins)


def join_rows(rows_ref, pieces, whole):
    height = pieces[0].shape[1]
    for j, piece in enumerate(pieces):
        for k in range(2):
            at = pl.multiple_of(rows_ref[2 * j + k] * height, height)
            whole[pl.ds(at, height), :] = piece[k]


def split_rows(rows_ref, whole, outs):
    j = 0
    for out in outs:
        count, height = out.shape[0], out.shape[1] * out.shape[2]
        for k in range(count):
            at = pl.multiple_of(rows_ref[j] * height, height)
            out[k] = whole[pl.ds(at, height), :].reshape(out.shape[1:])
            j += 1


BLOCK = 512


def over_rows(near, far, body):
    for part, ref in enumerate((near, far)):

        @pl.loop(0, ref.shape[0] // BLOCK)
        def _(j, part=part, ref=ref):
            at = pl.multiple_of(j * BLOCK, BLOCK)
            body(part, at, pl.multiple_of(part * ref.shape[0] + at, BLOCK), ref[pl.ds(at, BLOCK), :])


def grad_rows(near, far, right, whole):
    half = near.shape[0]

    @pl.loop(0, near.shape[1] // BLOCK)
    def _(j):
        at = pl.multiple_of(j * BLOCK, BLOCK)
        cols = pl.ds(at, BLOCK)
        whole[cols, :] = (
            dot_tn(near[:, cols], right[:half, :]) + dot_tn(far[:, cols], right[half:, :])
        ).astype(BF16)


def turn_half(x):
    return pltpu.roll(x, HD // 2, 1)


SCALE = 1.0 / math.sqrt(HD)


def attend(rows, pieces, near, far, cosines, sines, mask, g_q, g_k):
    many, span = 2 * near.shape[0], near.shape[0] // 4
    width = near.shape[1]

    def kernel(rows_ref, *refs):
        ws, refs = refs[: len(pieces)], refs[len(pieces) :]
        near, far, cos_ref, sin_ref, mask_ref, gq_ref, gk_ref = refs[:7]
        w_ref, raw_ref, q_ref, k_ref, v_ref, p_ref, att_ref, qkv_ref = refs[7:]
        join_rows(rows_ref, ws, w_ref)

        def project(part, at, row, x):
            qkv_ref[pl.ds(row, BLOCK), :] = dot(x, w_ref[...])

        over_rows(near, far, project)
        raw_ref[...] = qkv_ref[:, : 3 * HD]

        @pl.loop(0, 4)
        def _(k):
            own = pl.ds(pl.multiple_of(k * span, span), span)
            other = pl.ds(pl.multiple_of(4 * span + k * span, span), span)
            x = jnp.concatenate([qkv_ref[own, :], qkv_ref[other, :]])
            cos, sin = cos_ref[k], sin_ref[k]

            def head(u, gain):
                u = u * lax.rsqrt(jnp.mean(u * u, axis=-1, keepdims=True) + NORM_EPS) * gain
                return (u * cos + turn_half(u) * sin).astype(BF16)

            key = head(x[:, 2 * HD : 3 * HD], gk_ref[...])
            val = x[:, 3 * HD :].astype(BF16)
            k_ref[k] = key
            v_ref[k] = val
            for h in range(2):
                cols = slice(h * HD, (h + 1) * HD)
                query = head(x[:, cols], gq_ref[...])
                q_ref[k, :, cols] = query
                scores = jnp.where(mask_ref[k] > 0, dot_nt(query, key) * SCALE, NEG_FILL)
                expo = jnp.exp(scores - jnp.max(scores, axis=-1, keepdims=True))
                probs = expo / jnp.sum(expo, axis=-1, keepdims=True)
                p_ref[k, h] = probs
                att = dot(probs.astype(BF16), val).astype(BF16)
                att_ref[own, cols] = att[:span]
                att_ref[other, cols] = att[span:]

    seq = 2 * span
    outs = [
        ((width, 4 * HD), BF16), ((many, 3 * HD), F32), ((4, seq, 2 * HD), BF16),
        ((4, seq, HD), BF16), ((4, seq, HD), BF16), ((4, 2, seq, seq), F32), ((many, 2 * HD), BF16),
    ]
    ins = [rows, *pieces, near, far, cosines, sines, mask, g_q, g_k]
    return kernel_call(kernel, ins, outs, [((many, 4 * HD), F32)], "attend")


def attend_back(g, rows_out, near_d, far_d, w_o, att, saved, cosines, sines, g_q, g_k, near, far, rows_in):
    w_qkv, raw, q, k, v, probs = saved
    many, span = 2 * near.shape[0], near.shape[0] // 4
    width = near.shape[1]
    parts = 2 * g.B

    def kernel(rows_ref, *refs):
        near_d, far_d, wo_ref, att_ref, w_ref, raw_ref, q_ref, k_ref, v_ref, p_ref = refs[:10]
        cos_ref, sin_ref, gq_ref, gk_ref, near, far = refs[10:16]
        own_ref, sent_ref, go_ref, gain_ref, in_ref = refs[16:21]
        outs, (datt_ref, dqkv_ref, whole_ref) = refs[21 : 21 + parts], refs[21 + parts :]

        def project(part, at, row, x):
            datt_ref[pl.ds(row, BLOCK), :] = dot_nt(x, wo_ref[...]).astype(BF16)

        over_rows(near_d, far_d, project)
        gain_ref[...] = jnp.zeros_like(gain_ref)

        @pl.loop(0, 4)
        def _(s):
            own = pl.ds(pl.multiple_of(s * span, span), span)
            other = pl.ds(pl.multiple_of(4 * span + s * span, span), span)
            cos, sin = cos_ref[s], sin_ref[s]
            key, val = k_ref[s], v_ref[s]
            d_val = d_key = None

            def put_back(cols, x):
                x = x.astype(BF16)
                dqkv_ref[own, cols] = x[:span]
                dqkv_ref[other, cols] = x[span:]

            def head_back(cot, cols, gain, which):
                x = jnp.concatenate([raw_ref[own, cols], raw_ref[other, cols]])
                r = lax.rsqrt(jnp.mean(x * x, axis=-1, keepdims=True) + NORM_EPS)
                d_norm = cot * cos + turn_half(cot * sin)
                x = x * r
                gain_ref[which : which + 1, :] += jnp.sum(d_norm * x, axis=0, keepdims=True)
                d_norm = d_norm * gain
                put_back(cols, r * (d_norm - x * jnp.mean(d_norm * x, axis=-1, keepdims=True)))

            for h in range(2):
                cols = slice(h * HD, (h + 1) * HD)
                d_att = jnp.concatenate([datt_ref[own, cols], datt_ref[other, cols]])
                probs = p_ref[s, h]
                query = q_ref[s, :, cols]
                dv = dot_tn(probs.astype(BF16), d_att)
                dp = dot_nt(d_att, val)
                ds = probs * (dp - jnp.sum(probs * dp, axis=-1, keepdims=True)) * SCALE
                ds = ds.astype(BF16)
                dk = dot_tn(ds, query)
                d_val = dv if d_val is None else d_val + dv
                d_key = dk if d_key is None else d_key + dk
                head_back(dot(ds, key), cols, gq_ref[...], 0)
            head_back(d_key, slice(2 * HD, 3 * HD), gk_ref[...], 1)
            put_back(slice(3 * HD, 4 * HD), d_val)

        half = many // 2

        in_ref[...] = jnp.zeros_like(in_ref)

        def inward(part, at, row, x):
            d_xn = dot_nt(dqkv_ref[pl.ds(row, BLOCK), :], w_ref[...])
            in_ref[...] += jnp.sum(d_xn * x.astype(F32), axis=0, keepdims=True)
            out = sent_ref if part else own_ref
            out[pl.ds(at, BLOCK), :] = d_xn.astype(out.dtype)

        over_rows(near, far, inward)
        grad_rows(near, far, dqkv_ref, whole_ref)
        split_rows(rows_ref, whole_ref, outs)

        @pl.loop(0, width // BLOCK)
        def _(j):
            cols = pl.ds(pl.multiple_of(j * BLOCK, BLOCK), BLOCK)
            go_ref[:, cols] = (
                dot_tn(att_ref[:half, :], near_d[:, cols])
                + dot_tn(att_ref[half:, :], far_d[:, cols])
            ).astype(BF16)

    outs = [
        ((many // 2, width), F32), ((many // 2, width), BF16), ((2 * HD, width), BF16), ((2, HD), F32),
        ((1, width), F32),
    ]
    outs += [((g.A, 2, rows_in, 4 * HD), BF16)] * parts
    scratch = [((many, 2 * HD), BF16), ((many, 4 * HD), BF16), ((width, 4 * HD), BF16)]
    ins = [rows_out, near_d, far_d, w_o, att, w_qkv, raw, q, k, v, probs]
    ins += [cosines, sines, g_q, g_k, near, far]
    return kernel_call(kernel, ins, outs, scratch, "attend_back")


def feed(g, rows, rows_out, pieces, near, far, near_d, far_d, w_d, before, last):
    many, width = 2 * near.shape[0], near.shape[1]
    pw, rows_in = w_d.shape[0], pieces[0].shape[1]
    parts = 2 * g.B
    half = many // 2

    def kernel(rows_ref, rows_out_ref, *refs):
        ws, refs = refs[: len(pieces)], refs[len(pieces) :]
        near, far, near_d, far_d, wd_ref = refs[:5]
        given, refs = refs[5 : 5 + len(before)], refs[5 + len(before) :]
        hid_ref, gd_ref = refs[:2]
        outs, refs = refs[2 : 2 + parts], refs[2 + parts :]
        if len(before) == 0:
            (dgu_ref, w_ref), refs = refs[:2], refs[2:]
            dx = None
        else:
            dx, refs = refs[:2], refs[2:]
            (dgu_ref, w_ref), refs = refs[-2:], refs[:-2]
        (whole_ref,) = refs
        join_rows(rows_ref, ws, w_ref)

        def one(part, at, row, x):
            both = dot(x, w_ref[...])
            gate, up = both[:, :pw], both[:, pw:]
            d_ref = far_d if part else near_d
            dh = dot_nt(d_ref[pl.ds(at, BLOCK), :], wd_ref[...])
            sig = jax.nn.sigmoid(gate)
            lit = gate * sig
            rows = pl.ds(row, BLOCK)
            hid_ref[rows, :] = (lit * up).astype(BF16)
            dgu_ref[rows, pw:] = (dh * lit).astype(BF16)
            dgu_ref[rows, :pw] = (dh * up * sig * (1.0 + gate * (1.0 - sig))).astype(BF16)
            if dx is not None:
                total = dot_nt(dgu_ref[rows, :], w_ref[...])
                if last:
                    total = total + given[part][pl.ds(at, BLOCK), :]
                else:
                    total = total + dot_nt(given[0][rows, :], given[1][...])
                dx[part][pl.ds(at, BLOCK), :] = total.astype(dx[part].dtype)

        over_rows(near, far, one)
        grad_rows(near, far, dgu_ref, whole_ref)
        split_rows(rows_out_ref, whole_ref, outs)

        @pl.loop(0, width // BLOCK)
        def _(j):
            cols = pl.ds(pl.multiple_of(j * BLOCK, BLOCK), BLOCK)
            gd_ref[:, cols] = (
                dot_tn(hid_ref[:half, :], near_d[:, cols])
                + dot_tn(hid_ref[half:, :], far_d[:, cols])
            ).astype(BF16)

    outs = [((many, pw), BF16), ((pw, width), BF16)]
    outs += [((g.A, 2, rows_in, 2 * pw), BF16)] * parts
    local = [((many, 2 * pw), BF16), ((width, 2 * pw), BF16)]
    whole = [((width, 2 * pw), BF16)]
    if len(before) == 0:
        outs, scratch = outs + local, whole
    else:
        outs += [((half, width), F32), ((half, width), BF16 if last else F32)]
        scratch = whole + local
    ins = [rows, rows_out, *pieces, near, far, near_d, far_d, w_d, *before]
    got = kernel_call(kernel, ins, outs, scratch, "feed")
    return got[0], got[1], got[2 : 2 + parts], got[2 + parts :]


def project_out(x, w):
    half, width = x.shape[0] // 2, w.shape[1]

    def kernel(x_ref, w_ref, own_ref, sent_ref):
        @pl.loop(0, half // BLOCK)
        def _(j):
            at = pl.ds(pl.multiple_of(j * BLOCK, BLOCK), BLOCK)
            own_ref[at, :] = dot(x_ref[at, :], w_ref[...])
            low = pl.ds(pl.multiple_of(half + j * BLOCK, BLOCK), BLOCK)
            sent_ref[at, :] = dot(x_ref[low, :], w_ref[...]).astype(BF16)

    outs = [((half, width), F32), ((half, width), BF16)]
    return kernel_call(kernel, [x, w], outs, [], "project_out")


PARTS = 3


def per_device(
    g,
    tokens,
    segments,
    cotangent,
    w_query,
    w_key,
    w_value,
    w_output,
    w_gate,
    w_up,
    w_down,
    gain_in,
    gain_query,
    gain_key,
    gain_post,
):
    g.place()
    A, B, Q = g.A, g.B, g.Q
    _, span, width = tokens.shape
    seq_len = segments.shape[1]
    w_q, w_k, w_v, w_o, w_g, w_u, w_d = (
        w[0] for w in (w_query, w_key, w_value, w_output, w_gate, w_up, w_down)
    )
    rows_in, rows_o, rows_d = w_q.shape[0], w_o.shape[0], w_d.shape[0]
    q_width, kv_width, hidden_width = w_q.shape[1], w_k.shape[1], w_g.shape[1]
    g_in, g_q, g_k, g_post = gain_in[0], gain_query[0], gain_key[0], gain_post[0]
    many = 8 * span
    units = hidden_width // 8
    pw = units // PARTS
    hd2 = 2 * HD

    def hidden_cuts(t, u, c, part):
        out = []
        for j, i in enumerate(g.hidden_blocks(t, u, c)):
            lo, hi = max(j * rows_d, part * pw), min((j + 1) * rows_d, (part + 1) * pw)
            if lo < hi:
                out.append((i * rows_d + lo - j * rows_d, hi - lo))
        return out

    x_own = tokens[0].astype(F32)
    xn_own = rms_scale(x_own, g_in).astype(BF16)
    half_o = lax.dynamic_slice(w_o, (g.c * (rows_o // 2), 0), (rows_o // 2, width))
    half_d = lax.dynamic_slice(w_d, (g.c * (rows_d // 2), 0), (rows_d // 2, width))
    third = rows_d // 6
    seg_low = segments[0].astype(BF16)[None]
    seg_low = jnp.pad(seg_low, ((0, 15), (0, width - seq_len)))
    first, later = [], []
    for dt, du in ORDER:
        t, u = g.t ^ dt, g.u ^ du
        kv = g.kv_head(t, u, g.c, rows_o)
        first.append([(0, kv * hd2, hd2), (1, kv * HD, HD), (2, kv * HD, HD)])
        later.append(
            [
                (k, at, w)
                for part in range(PARTS)
                for k in (0, 1)
                for at, w in hidden_cuts(t, u, g.c, part)
            ]
        )
    first = cut_columns([w_q, w_k, w_v], first)
    later = cut_columns([w_g, w_u], later)
    L = Live(qkv=first)
    S = Shards(g, L)
    S.fetch("o", [half_o])
    S.fetch("d", [half_d[k * third : (k + 1) * third] for k in range(3)])

    def done(*floating):
        new = lax.optimization_barrier({k: v for k, v in L.items() if k not in floating})
        L.update(new)

    def pairs(x):
        return [jnp.stack(x[:2]), jnp.stack(x[2:])]

    done()

    L.qkv = chips_swap(g, L.qkv)
    S.fetch_a(("o", 0))
    S.fetch_b(("o", 0, False))
    L.xn, L.cot = jnp.concatenate([xn_own, seg_low]), cotangent[0]
    L.gu = (later[0], later[2], jnp.concatenate([later[1], later[3]], axis=1))
    done()

    L.xn = gather_one(g, L.xn)
    S.fetch("qkv", pairs(L.qkv))
    S.fetch_a(("qkv", 0))
    S.fetch_b(("qkv", 0, False), ("qkv", 1, False))
    done()
    L.xn = gather_two(g, L.xn)
    S.fetch_a(("qkv", 1))
    S.fetch_b(("qkv", 0, True), ("o", 0, True))
    L.gu_t = g.pt(L.gu[2], 1, 0)
    done("gu_t")

    near = jnp.concatenate([x[:span] for x in L.xn])
    L.seg = [x[span, :seq_len] for x in L.xn]
    L.xn = (near, g.pc(near))
    S.fetch_a(("d", 0))
    S.fetch_b(("qkv", 1, True))
    o_blocks = S.rows("o").reshape(2, 2, Q, rows_o // 2, width)
    o_mine = pick(o_blocks, g.u)
    o_next = g.px(pick(o_blocks, 1 - g.u), g.umask)
    L.gu_u = g.pt(L.gu[1], 0, 1)
    seg_all = jnp.stack(L.seg)
    index = lax.broadcasted_iota(jnp.int32, (4, seq_len), 1)
    earlier = seg_all[:, None, :] < seg_all[:, :, None]
    pos = index - jnp.sum(earlier.astype(jnp.int32), axis=-1)
    turn = lambda v: lax.dynamic_slice(
        jnp.concatenate([v, v], axis=1), (0, g.c * span), (4, seq_len)
    )
    index, pos, seg_own = turn(index), turn(pos).astype(F32), turn(seg_all)
    inv_freq = jnp.exp(jnp.arange(HD // 2, dtype=F32) * (-2.0 * math.log(ROPE_BASE) / HD))
    rotation = pos[:, :, None] * inv_freq
    cosines, sines = jnp.cos(rotation), jnp.sin(rotation)
    L.cosines = jnp.concatenate([cosines, cosines], axis=-1)
    L.sines = jnp.concatenate([-sines, sines], axis=-1)
    same_doc = (index[:, None, :] <= index[:, :, None]) & (
        seg_own[:, :, None] == seg_own[:, None, :]
    )
    L.mask = same_doc.astype(F32)
    L.o = (o_mine, o_next)
    done("gu_u", "o")

    def core_sum(own, sent):
        return own + g.pc(sent).astype(F32)

    def chip_blocks(x):
        return [x[k * span : (k + 1) * span] for k in range(4)]

    L.cot = gather_one(g, L.cot)
    pass_on, along_t = L.gu_t[:, : 2 * units], L.gu_t[:, 2 * units :]
    L.gu = [L.gu[0], g.pt(pass_on, 0, 1), L.gu_u, along_t]
    del L["gu_t"], L["gu_u"]
    S.fetch_a(("d", 1), ("d", 2))
    S.fetch_b(("d", 0, False), ("d", 1, False), ("d", 2, False))
    o_mine, o_next = L.o
    o_pair = jnp.where(g.u == 0, jnp.stack([o_mine, o_next]), jnp.stack([o_next, o_mine]))
    o_pair = o_pair.transpose(1, 2, 0, 3, 4)
    w_o_all = swap_halves(g, pick(o_pair, g.c), g.pc(pick(o_pair, 1 - g.c)))
    w_o_all = w_o_all.transpose(1, 2, 0, 3, 4).reshape(-1, width)
    rows, pieces = S.columns("qkv")
    *saved, att = attend(rows, pieces, *L.xn, L.cosines, L.sines, L.mask, gain_query, gain_key)
    L.part = project_out(att, w_o_all)
    done()

    L.part = core_sum(*L.part)
    L.cot = gather_two(g, L.cot)
    for k in range(PARTS):
        S.fetch(f"gu{k + 1}", pairs([x[:, 2 * pw * k : 2 * pw * (k + 1)] for x in L.gu]))
    del L["gu"]
    S.fetch_a(("gu1", 0))
    S.fetch_b(("d", 0, True), ("d", 1, True))
    done()

    L.part = scatter_one(g, chip_blocks(L.part))
    S.fetch_a(("gu1", 1))
    S.fetch_b(("d", 2, True), ("gu1", 0, False), ("gu1", 1, False))
    cot_near = jnp.concatenate(L.cot)
    L.cot = (cot_near, g.pc(cot_near))
    done()
    L.part = scatter_two(g, L.part)
    S.fetch_a(("gu2", 0))
    S.fetch_b(("gu1", 0, True), ("gu1", 1, True))
    d_blocks = S.rows("d").reshape(A, 2, B // 2, rows_d // 2, width).transpose(1, 0, 2, 3, 4)
    L.d = (pick(d_blocks, g.c), g.pc(pick(d_blocks, 1 - g.c)))
    done()

    mid = x_own + add_all(L.part)
    xn2_own, post_back = jax.vjp(rms_scale, mid, g_post)
    L.xn2 = gather_one(g, xn2_own.astype(BF16))
    S.fetch_a(("gu2", 1))
    S.fetch_b(("gu2", 0, False), ("gu2", 1, False))
    done()
    L.xn2 = gather_two(g, L.xn2)
    S.fetch_a(("gu3", 0))
    S.fetch_b(("gu2", 0, True), ("gu2", 1, True))
    w_d_all = swap_halves(g, *L.d)
    L.w_d_all = w_d_all.transpose(1, 2, 0, 3, 4).reshape(-1, width)
    done()

    near = jnp.concatenate(L.xn2)
    L.xn2 = (near, g.pc(near))
    S.fetch_a(("gu3", 1))
    S.fetch_b(("gu3", 0, False), ("gu3", 1, False))
    done()
    w_d_all = L.w_d_all

    rows_out = S.total_rows()

    def feed_part(part, before):
        name = f"gu{part + 1}"
        rows, pieces = S.columns(name)
        w_d_part = w_d_all[part * pw : (part + 1) * pw]
        hid, grad_d, grads, rest = feed(
            g, rows, rows_out, pieces, *L.xn2, *L.cot, w_d_part, before, part == PARTS - 1
        )
        S.total_split(name, grads)
        return (hid, grad_d), rest

    S.fetch_b(("gu3", 0, True), ("gu3", 1, True))
    L.one, L.rest = feed_part(0, ())
    done()

    S.total_b(("gu1", 0))
    S.prepare_a(("gu1", 0))
    L.two, L.rest = feed_part(1, L.rest)
    done()

    S.total_b(("gu1", 1))
    S.prepare_a(("gu1", 1))
    S.total_a(("gu1", 0))
    L.three, L.part = feed_part(2, L.rest)
    done()

    L.part = core_sum(*L.part)
    S.total_b(("gu2", 0))
    S.prepare_a(("gu2", 0))
    S.total_a(("gu1", 1))
    grad_d = jnp.concatenate([L.one[1], L.two[1], L.three[1]])
    grad_d = grad_d.reshape(A, B // 2, 2, rows_d // 2, width)
    grad_d = grad_d.transpose(2, 0, 1, 3, 4)
    L.d = (pick(grad_d, g.c), pick(grad_d, 1 - g.c))
    done()

    L.part = scatter_one(g, chip_blocks(L.part))
    S.total_b(("gu2", 1))
    S.prepare_a(("gu2", 1))
    S.total_a(("gu2", 0))
    S.finish("gu1")
    L.d = (L.d[0], g.pc(L.d[1]))
    L.hidden = jnp.concatenate([L.one[0], L.two[0], L.three[0]], axis=1)
    done()
    L.part = scatter_two(g, L.part)
    S.total_b(("gu3", 0))
    S.prepare_a(("gu3", 0))
    S.total_a(("gu2", 1))
    grad_d = swap_halves(g, *L.d).transpose(1, 0, 2, 3, 4).reshape(A, B, rows_d // 2, width)
    S.total("d", [grad_d[:, :, k * third : (k + 1) * third] for k in range(3)])
    L.out = project_out(L.hidden, w_d_all)
    done()

    d_post, grad_post = post_back(add_all(L.part))
    d_mid = cotangent[0].astype(F32) + d_post
    L.dmb = gather_one(g, d_mid.astype(BF16))
    S.total_b(("gu3", 1))
    S.prepare_a(("gu3", 1))
    S.total_a(("gu3", 0))
    S.finish("gu2")
    done()
    L.dmb = gather_two(g, L.dmb)
    S.total_b(("d", 0))
    S.prepare_a(("d", 0))
    S.total_a(("gu3", 1))
    L.out = core_sum(*L.out)
    done()

    near = jnp.concatenate(L.dmb)
    L.dmb = (near, g.pc(near))
    S.total_b(("d", 1))
    S.prepare_a(("d", 1))
    S.total_a(("d", 0))
    S.finish("gu3")
    L.out = scatter_one(g, chip_blocks(L.out))
    grads = [columns_pieces(g, L[f"gu{k + 1}"]) for k in range(PARTS)]
    L.gu = [jnp.concatenate(x, axis=1) for x in zip(*grads)]
    done()

    S.total_b(("d", 2))
    S.prepare_a(("d", 2))
    S.total_a(("d", 1))
    L.gu = chips_swap(g, L.gu)
    own, sent, grad_o, head_gains, grad_in, *grads = attend_back(
        g, rows_out, *L.dmb, w_o_all, att, saved, L.cosines, L.sines, gain_query, gain_key, *L.xn,
        rows_in,
    )
    L.part = (own, sent)
    L.gains = jnp.concatenate([grad_in[0] / g_in, grad_post, head_gains.reshape(-1)])
    grad_o = grad_o.reshape(Q, 2, rows_o, width).transpose(1, 0, 2, 3)
    L.o = (pick(grad_o, g.u), pick(grad_o, 1 - g.u))
    S.total_split("qkv", grads)
    done()

    L.part = core_sum(*L.part)
    S.total_b(("qkv", 0))
    S.prepare_a(("qkv", 0))
    S.total_a(("d", 2))
    L.o = (L.o[0], g.px(L.o[1], g.umask))
    L.gu = (L.gu, g.pc(jnp.stack(L.gu)))
    L.gains = L.gains + g.pc(L.gains)
    done()

    L.part = scatter_one(g, chip_blocks(L.part))
    S.total_b(("qkv", 1))
    S.total_a(("qkv", 0))
    S.finish("d")
    mine, other = L.o
    grad_o = jnp.where(g.u == 0, jnp.stack([mine, other]), jnp.stack([other, mine]))
    grad_o = grad_o.reshape(2, Q, 2, rows_o // 2, width).transpose(2, 0, 1, 3, 4)
    grad_o = swap_halves(g, pick(grad_o, g.c), g.pc(pick(grad_o, 1 - g.c)))
    grad_o = grad_o.transpose(1, 0, 2, 3, 4).reshape(A, B, rows_o // 2, width)
    S.total("o", [grad_o])
    S.prepare_a(("qkv", 1))
    bits = int(math.log2(g.n))
    for bit in range(bits // 2):
        L.gains = L.gains + g.px(L.gains, 1 << bit)
    done()
    L.part = scatter_two(g, L.part)
    for bit in range(bits // 2, bits):
        L.gains = L.gains + g.px(L.gains, 1 << bit)
    S.total_b(("o", 0))
    S.total_a(("qkv", 1))
    S.prepare_a(("o", 0))
    S.finish("qkv")
    d_sum = jnp.concatenate([L.d[k] for k in range(3)])
    L.d = (d_sum, g.pc(d_sum))
    done()

    S.total_a(("o", 0))
    L.qkv = chips_swap(g, columns_pieces(g, L.qkv))
    _, in_back = jax.vjp(lambda x: rms_scale(x, g_in), x_own)
    L.d_tokens = (d_mid + in_back(add_all(L.part))[0]).astype(BF16)
    grad_down = swap_halves(g, *L.d).reshape(1, rows_d, width).astype(F32)
    done()

    gains = L.gains[None]
    S.finish("o")
    L.out = scatter_two(g, L.out)
    L.qkv = (L.qkv, g.pc(jnp.stack(L.qkv)))
    grad_output = swap_halves(g, L.o[0], g.pc(L.o[0])).reshape(1, rows_o, width).astype(F32)
    activations = (mid + add_all(L.out)).astype(BF16)
    d_tokens = L.d_tokens

    def both_cores(pair):
        near, far = pair
        return list(near) + [far[k] for k in range(4)]

    pieces = both_cores(L.qkv)
    places = []
    for j, piece in enumerate(pieces):
        dt, du = ORDER[j % 4]
        kv = g.kv_head(g.t ^ dt, g.u ^ du, g.c ^ (j // 4), rows_o)
        places += [
            (j, 0, hd2, 0, kv * hd2),
            (j, hd2, HD, 1, kv * HD),
            (j, hd2 + HD, HD, 2, kv * HD),
        ]
    grad_query, grad_key, grad_value = place_columns(pieces, [q_width, kv_width, kv_width], places)

    pieces, places = both_cores(L.gu), []
    for part in range(PARTS):
        for j, piece in enumerate(pieces):
            dt, du = ORDER[j % 4]
            at = 2 * pw * part
            for to, w in hidden_cuts(g.t ^ dt, g.u ^ du, g.c ^ (j // 4), part):
                places += [
                    (j, at, w, 0, to),
                    (j, pw + at, w, 1, to),
                ]
                at += w
    grad_gate, grad_up = place_columns(pieces, [hidden_width, hidden_width], places)

    return (
        activations[None],
        d_tokens[None],
        grad_query[None],
        grad_key[None],
        grad_value[None],
        grad_output,
        grad_gate[None],
        grad_up[None],
        grad_down,
        gains[:, :width],
        gains[:, 2 * width : 2 * width + HD],
        gains[:, 2 * width + HD :],
        gains[:, width : 2 * width],
    )


def solution(mesh):
    rows = P("fsdp", "rep", None)
    cut_rows = P(None, "fsdp", None)
    return jax.shard_map(
        functools.partial(per_device, Grid(mesh)),
        mesh=mesh,
        in_specs=(rows, P("fsdp", None), rows) + (cut_rows,) * 7 + (P(),) * 4,
        out_specs=(rows, rows) + (cut_rows,) * 7 + (P(),) * 4,
        check_vma=False,
    )
```

time: 825 us -> 543 us (0.66)
  waiting for transfers between devices: 465 us -> 238 us
  matrix products: 81.3 us -> 0 us
  Pallas kernels: 0 us -> 79.6 us
  local copies, waits for them, and re-layouts: 115 us -> 53.6 us
  starting transfers between devices: 93 us -> 114 us
  other arithmetic: 61.8 us -> 45.2 us
    ppermute x76 -> x91, waiting for transfers between devices: 459 us -> 237 us  [px(): return lax.ppermute(x, 'fsdp', [(i, i ^ mask) for i in range(self.n)])]
    pallas_call x0 -> x11, Pallas kernels: none -> 79.6 us  [the longest x7 71.6 us: kernel_call(): pl.pallas_call(kernel, in_specs=[smem if x.dtype == jnp.int32 else vmem f...]
    dot_general x20 -> x0, matrix products: 78 us -> none  [the longest x5 21.8 us: dot_nt(): lax.dot_general(x, y, (((1,), (1,)), ((), ())), preferred_element_type=F32)]
    dynamic_update_slice x79 -> x16, local copies, waits for them, and re-layouts: 34.1 us -> 4.41 us  [rows(): out = lax.dynamic_update_slice(out, x[None, None], starts)]
    ppermute x76 -> x91, starting transfers between devices: 83.8 us -> 112 us  [px(): return lax.ppermute(x, 'fsdp', [(i, i ^ mask) for i in range(self.n)])]
    slice x2 -> x31, local copies, waits for them, and re-layouts: 1.36 us -> 15.6 us  [the longest x10 4.68 us: permute_joined(): out[k] = got[at:at + x.shape[0]].reshape(arrays[k].shape)]
    dot_general x3 -> x0, local copies, waits for them, and re-layouts: 13.7 us -> none  [the longest x2 12.8 us: dot_tn(): lax.dot_general(x, y, (((0,), (0,)), ((), ())), preferred_element_type=F32)]
    convert_element_type x15 -> x12, local copies, waits for them, and re-layouts: 13.3 us -> 1.18 us  [prepare_a(): sent = [pick(rows, g.a ^ d).astype(BF16) for d in range(1, g.A)]]
  transfers between devices with their start and end apart: 127 -> 108, of which waited for: 53 -> 44; matrix products, arithmetic and copies ran while one was open for 23% -> 13% of each run, Pallas kernels for 0% -> 15%
where the time goes in v2:
time: 543 us; the launch traced here: 535 us
  waiting for transfers between devices  238 us (44%)
  starting transfers between devices  114 us (21%)
  Pallas kernels  79.6 us (15%)
  local copies, waits for them, and re-layouts  53.6 us (10%)
  other arithmetic  45.2 us (8%)
    ppermute x91, waiting for transfers between devices, px(): return lax.ppermute(x, 'fsdp', [(i, i ^ mask) for i in range(self.n)])  237 us
    ppermute x91, starting transfers between devices, px(): return lax.ppermute(x, 'fsdp', [(i, i ^ mask) for i in range(self.n)])  112 us
    pallas_call x7, Pallas kernels, kernel_call(): pl.pallas_call(kernel, in_specs=[smem if x.dtype == jnp.int32 else vmem f...  71.6 us
    unnamed x247, local copies, waits for them, and re-layouts  18.7 us
  transfers between devices with their start and end apart: 108, of which 44 were waited for; matrix products, arithmetic and copies ran while one was open for 13% of the time, Pallas kernels for 15%

profile of v2, /device:TPU:0, one launch (start us, length us, event | category | flops | bytes accessed | tf_op | source)
XLA Modules:
  0.0 534.9 jit_solution(7865484378307445736)
XLA Ops:
  6.1 2.3 dynamic-slice_bitcast_fusion.31
  8.4 4.0 collective-permute-start.1
  14.0 2.5 collective-permute-start.2
  22.9 4.4 collective-permute-done.4
  31.6 2.3 collective-permute-start.6
  33.9 7.6 %collective-permute-done.5 = bf16[512,512]{1,0:T(8,128)(2,1)S(1)} collective-permute-done((bf16[512,512]{1,0:T(8,128)(2,1)S(1)}, bf16[512,512]{1,0:T(8,128)(2,1)S(1)}, u32[]{:S(2)}, u32[]{:S(2)}) %collective-permute-start.5) | collective-permute-done | bytes 524320 | tf_op jit(solution)/shard_map/ppermute | solution.py:55
  41.5 5.6 %collective-permute-done.6 = bf16[256,512]{1,0:T(8,128)(2,1)S(1)} collective-permute-done((bf16[256,512]{1,0:T(8,128)(2,1)S(1)}, bf16[256,512]{1,0:T(8,128)(2,1)S(1)}, u32[]{:S(2)}, u32[]{:S(2)}) %collective-permute-start.6) | collective-permute-done | bytes 262176 | tf_op jit(solution)/shard_map/ppermute | solution.py:55
  54.2 2.6 collective-permute-start.14
  56.8 6.4 %collective-permute-done.11 = bf16[256,512]{1,0:T(8,128)(2,1)S(1)} collective-permute-done((bf16[256,512]{1,0:T(8,128)(2,1)S(1)}, bf16[256,512]{1,0:T(8,128)(2,1)S(1)}, u32[]{:S(2)}, u32[]{:S(2)}) %collective-permute-start.11) | collective-permute-done | bytes 262176 | tf_op jit(solution)/shard_map/ppermute | solution.py:55
  78.2 13.3 %collective-permute-done.23 = bf16[2,1,64,2048]{3,2,0,1:T(8,128)(2,1)S(1)} collective-permute-done((bf16[2,1,64,2048]{3,2,0,1:T(8,128)(2,1)S(1)}, bf16[2,1,64,2048]{3,2,0,1:T(8,128)(2,1)S(1)}, u32[]{:S(2)}, u32[]{:S(2)}) %collective-permute-start.23) | collective-permute-done | bytes 524320 | tf_op jit(solution)/shard_map/ppermute | solution.py:55
  102.1 9.0 %attend.1 = (bf16[2048,512]{1,0:T(8,128)(2,1)S(1)}, f32[1024,384]{1,0:T(8,128)S(1)}, bf16[4,256,256]{2,1,0:T(8,128)(2,1)S(1)}, bf16[4,256,128]{2,1,0:T(8,128)(2,...) custom-call(s32[16]{0:T(128)S(1)} %stack.663.rows_ref, ...), custom_call_target="tpu_custom_call" | custom-call | flops 1048576 | bytes 65536 | tf_op jit(solution)/shard_map/attend/pallas_call | solution.py:333
  117.2 7.2 %collective-permute-done.20 = bf16[128,2048]{1,0:T(8,128)(2,1)S(1)} collective-permute-done((bf16[128,2048]{1,0:T(8,128)(2,1)S(1)}, bf16[128,2048]{1,0:T(8,128)(2,1)S(1)}, u32[]{:S(2)}, u32[]{:S(2)}) %collective-permute-start.20) | collective-permute-done | bytes 524320 | tf_op jit(solution)/shard_map/ppermute | solution.py:55
  125.5 8.7 %collective-permute-done.21 = bf16[128,1536]{1,0:T(8,128)(2,1)S(1)} collective-permute-done((bf16[128,1536]{1,0:T(8,128)(2,1)S(1)}, bf16[128,1536]{1,0:T(8,128)(2,1)S(1)}, u32[]{:S(2)}, u32[]{:S(2)}) %collective-permute-start.21) | collective-permute-done | bytes 393248 | tf_op jit(solution)/shard_map/ppermute | solution.py:55
  138.4 10.5 %collective-permute-done.26 = bf16[128,2048]{1,0:T(8,128)(2,1)S(1)} collective-permute-done((bf16[128,2048]{1,0:T(8,128)(2,1)S(1)}, bf16[128,2048]{1,0:T(8,128)(2,1)S(1)}, u32[]{:S(2)}, u32[]{:S(2)}) %collective-permute-start.26) | collective-permute-done | bytes 524320 | tf_op jit(solution)/shard_map/ppermute | solution.py:55
  152.0 2.6 collective-permute-start.32
  156.6 14.1 %collective-permute-done.31 = bf16[512,512]{1,0:T(8,128)(2,1)S(1)} collective-permute-done((bf16[512,512]{1,0:T(8,128)(2,1)S(1)}, bf16[512,512]{1,0:T(8,128)(2,1)S(1)}, u32[]{:S(2)}, u32[]{:S(2)}) %collective-permute-start.31) | collective-permute-done | bytes 524320 | tf_op jit(solution)/shard_map/ppermute | solution.py:55
  179.6 9.5 %collective-permute-done.35 = bf16[512,512]{1,0:T(8,128)(2,1)S(1)} collective-permute-done((bf16[512,512]{1,0:T(8,128)(2,1)S(1)}, bf16[512,512]{1,0:T(8,128)(2,1)S(1)}, u32[]{:S(2)}, u32[]{:S(2)}) %collective-permute-start.35) | collective-permute-done | bytes 524320 | tf_op jit(solution)/shard_map/ppermute | solution.py:55
  189.9 5.3 collective-permute-done.36
  197.5 2.6 collective-permute-start.42
  201.0 8.4 %collective-permute-done.39 = bf16[512,512]{1,0:T(8,128)(2,1)S(1)} collective-permute-done((bf16[512,512]{1,0:T(8,128)(2,1)S(1)}, bf16[512,512]{1,0:T(8,128)(2,1)S(1)}, u32[]{:S(2)}, u32[]{:S(2)}) %collective-permute-start.39) | collective-permute-done | bytes 524320 | tf_op jit(solution)/shard_map/ppermute | solution.py:55
  210.2 5.9 %collective-permute-done.40 = bf16[256,512]{1,0:T(8,128)(2,1)S(1)} collective-permute-done((bf16[256,512]{1,0:T(8,128)(2,1)S(1)}, bf16[256,512]{1,0:T(8,128)(2,1)S(1)}, u32[]{:S(2)}, u32[]{:S(2)}) %collective-permute-start.40) | collective-permute-done | bytes 262176 | tf_op jit(solution)/shard_map/ppermute | solution.py:55
  218.2 2.7 collective-permute-start.44
  222.1 7.2 %collective-permute-done.43 = bf16[512,512]{1,0:T(8,128)(2,1)S(1)} collective-permute-done((bf16[512,512]{1,0:T(8,128)(2,1)S(1)}, bf16[512,512]{1,0:T(8,128)(2,1)S(1)}, u32[]{:S(2)}, u32[]{:S(2)}) %collective-permute-start.43) | collective-permute-done | bytes 524320 | tf_op jit(solution)/shard_map/ppermute | solution.py:55
  239.0 13.1 %collective-permute-done.46 = bf16[512,512]{1,0:T(8,128)(2,1)} collective-permute-done((bf16[512,512]{1,0:T(8,128)(2,1)}, bf16[512,512]{1,0:T(8,128)(2,1)}, u32[]{:S(2)}, u32[]{:S(2)}) %collective-permute-start.46) | collective-permute-done | bytes 524320 | tf_op jit(solution)/shard_map/ppermute | solution.py:55
  257.1 11.6 %feed.3 = (bf16[1024,256]{1,0:T(8,128)(2,1)S(1)}, bf16[256,2048]{1,0:T(8,128)(2,1)S(1)}, bf16[2,2,128,512]{3,2,1,0:T(8,128)(2,1)S(1)}, bf16[2,2,128,512]{3,2,1,0...) custom-call(s32[16]{0:T(128)S(1)} %stack.663.rows_ref, ...), custom_call_target="tpu_custom_call" | custom-call | flops 1048576 | bytes 65536 | tf_op jit(solution)/shard_map/feed/pallas_call | solution.py:333
  269.9 15.5 %feed.4 = (bf16[1024,256]{1,0:T(8,128)(2,1)S(1)}, bf16[256,2048]{1,0:T(8,128)(2,1)S(1)}, bf16[2,2,128,512]{3,2,1,0:T(8,128)(2,1)S(1)}, bf16[2,2,128,512]{3,2,1,0...) custom-call(s32[16]{0:T(128)S(1)} %stack.663.rows_ref, ...), custom_call_target="tpu_custom_call" | custom-call | flops 1048576 | bytes 65536 | tf_op jit(solution)/shard_map/feed/pallas_call | solution.py:333
  287.3 14.4 %feed.5 = (bf16[1024,256]{1,0:T(8,128)(2,1)S(1)}, bf16[256,2048]{1,0:T(8,128)(2,1)S(1)}, bf16[2,2,128,512]{3,2,1,0:T(8,128)(2,1)S(1)}, bf16[2,2,128,512]{3,2,1,0...) custom-call(s32[16]{0:T(128)S(1)} %stack.663.rows_ref, ...), custom_call_target="tpu_custom_call" | custom-call | flops 1048576 | bytes 65536 | tf_op jit(solution)/shard_map/feed/pallas_call | solution.py:333
  302.1 2.4 collective-permute-start.53
  306.1 12.4 %collective-permute-done.54 = bf16[512,512]{1,0:T(8,128)(2,1)S(1)} collective-permute-done((bf16[512,512]{1,0:T(8,128)(2,1)S(1)}, bf16[512,512]{1,0:T(8,128)(2,1)S(1)}, u32[]{:S(2)}, u32[]{:S(2)}) %collective-permute-start.54) | collective-permute-done | bytes 524320 | tf_op jit(solution)/shard_map/ppermute | solution.py:55
  324.0 9.2 %collective-permute-done.58 = bf16[512,512]{1,0:T(8,128)(2,1)S(1)} collective-permute-done((bf16[512,512]{1,0:T(8,128)(2,1)S(1)}, bf16[512,512]{1,0:T(8,128)(2,1)S(1)}, u32[]{:S(2)}, u32[]{:S(2)}) %collective-permute-start.58) | collective-permute-done | bytes 524320 | tf_op jit(solution)/shard_map/ppermute | solution.py:55
  336.3 2.5 collective-permute-start.60
  342.9 4.8 project_out.3
  347.7 2.4 collective-permute-done.61
  350.4 6.1 %collective-permute-done.63 = bf16[128,2048]{1,0:T(8,128)(2,1)S(1)} collective-permute-done((bf16[128,2048]{1,0:T(8,128)(2,1)S(1)}, bf16[128,2048]{1,0:T(8,128)(2,1)S(1)}, u32[]{:S(2)}, u32[]{:S(2)}) %collective-permute-start.63) | collective-permute-done | bytes 524320 | tf_op jit(solution)/shard_map/ppermute | solution.py:55
  364.7 4.0 collective-permute-done.67
  370.4 4.1 collective-permute-done.66
  381.3 11.6 %collective-permute-done.68 = bf16[128,2048]{1,0:T(8,128)(2,1)} collective-permute-done((bf16[128,2048]{1,0:T(8,128)(2,1)}, bf16[128,2048]{1,0:T(8,128)(2,1)}, u32[]{:S(2)}, u32[]{:S(2)}) %collective-permute-start.68) | collective-permute-done | bytes 524320 | tf_op jit(solution)/shard_map/ppermute | solution.py:55
  395.2 3.1 convert_add_fusion.1
  406.1 6.8 %collective-permute-done.73 = bf16[128,2048]{1,0:T(8,128)(2,1)S(1)} collective-permute-done((bf16[128,2048]{1,0:T(8,128)(2,1)S(1)}, bf16[128,2048]{1,0:T(8,128)(2,1)S(1)}, u32[]{:S(2)}, u32[]{:S(2)}) %collective-permute-start.73) | collective-permute-done | bytes 524320 | tf_op jit(solution)/shard_map/ppermute | solution.py:55
  421.0 15.0 %attend_back.1 = (f32[512,2048]{1,0:T(8,128)S(1)}, bf16[512,2048]{1,0:T(8,128)(2,1)}, bf16[256,2048]{1,0:T(8,128)(2,1)S(1)}, f32[2,128]{1,0:T(2,128)S(1)}, f32[1...) custom-call(s32[8]{0:T(128)S(1)} %stack.701.rows_out_ref.rows_ref, ...), custom_call_target="tpu_custom_call" | custom-call | flops 1048576 | bytes 65536 | tf_op jit(solution)/shard_map/attend_back/pallas_call | solution.py:333
  445.5 8.9 %collective-permute-done.86 = bf16[512,512]{1,0:T(8,128)(2,1)} collective-permute-done((bf16[512,512]{1,0:T(8,128)(2,1)}, bf16[512,512]{1,0:T(8,128)(2,1)}, u32[]{:S(2)}, u32[]{:S(2)}) %collective-permute-start.86) | collective-permute-done | bytes 524320 | tf_op jit(solution)/shard_map/ppermute | solution.py:55
  455.8 3.5 convert_add_fusion
  465.8 9.4 %collective-permute-done.88 = f32[4352]{0:T(1024)S(1)} collective-permute-done((f32[4352]{0:T(1024)S(1)}, f32[4352]{0:T(1024)S(1)}, u32[]{:S(2)}, u32[]{:S(2)}) %collective-permute-start.88) | collective-permute-done | bytes 17440 | tf_op jit(solution)/shard_map/ppermute | solution.py:55
  485.1 12.0 %collective-permute-done.95 = f32[4352]{0:T(1024)S(1)} collective-permute-done((f32[4352]{0:T(1024)S(1)}, f32[4352]{0:T(1024)S(1)}, u32[]{:S(2)}, u32[]{:S(2)}) %collective-permute-start.95) | collective-permute-done | bytes 17440 | tf_op jit(solution)/shard_map/ppermute | solution.py:55
  499.9 3.4 collective-permute-start.100
  512.8 3.8 collective-permute-done.101.refs_1_
  521.8 3.8 place_columns.3
  529.4 2.7 collective-permute-done.105
  (634 shorter events, 199.7 us)
Async XLA Ops:
  8.4 18.9 %collective-permute-start.1 = (bf16[64,2048]{1,0:T(8,128)(2,1)}, bf16[64,2048]{1,0:T(8,128)(2,1)}, u32[]{:S(2)}, u32[]{:S(2)}) collective-permute-start(bf16[64,2048]{1,0:T(8,128)(2,1)} %get-tuple-element.789), channel_id=1, source_target_pairs={{0,16},{2,18},{4,20},{6,22},{8,24},{10,26},{12,28},{14,30},{16,0},... | collective-permute-start | bytes 786440 | tf_op jit(solution)/shard_map/ppermute | solution.py:55
  29.9 18.7 %collective-permute-start.8 = (bf16[144,2048]{1,0:T(8,128)(2,1)S(1)}, bf16[144,2048]{1,0:T(8,128)(2,1)}, u32[]{:S(2)}, u32[]{:S(2)}) collective-permute-start(bf16[144,2048]{1,0:T(8,128)(2,1)S(1)} %fusion.9), channel_id=1, source_target_pairs={{0,8},{2,10},{4,12},{6,14},{8,0},{10,2},{12,4},{14,6},{16,24},{18,... | collective-permute-start | bytes 1769480 | tf_op jit(solution)/shard_map/ppermute | solution.py:55
  30.1 18.6 %collective-permute-start.7 = (bf16[144,2048]{1,0:T(8,128)(2,1)S(1)}, bf16[144,2048]{1,0:T(8,128)(2,1)S(1)}, u32[]{:S(2)}, u32[]{:S(2)}) collective-permute-start(bf16[144,2048]{1,0:T(8,128)(2,1)S(1)} %fusion.9), channel_id=1, source_target_pairs={{0,2},{2,0},{4,6},{6,4},{8,10},{10,8},{12,14},{14,12},{16,18},{18,... | collective-permute-start | bytes 1769480 | tf_op jit(solution)/shard_map/ppermute | solution.py:55
  31.6 15.6 %collective-permute-start.6 = (bf16[256,512]{1,0:T(8,128)(2,1)S(1)}, bf16[256,512]{1,0:T(8,128)(2,1)S(1)}, u32[]{:S(2)}, u32[]{:S(2)}) collective-permute-start(bf16[256,512]{1,0:T(8,128)(2,1)S(1)} %bitcast.456), channel_id=1, source_target_pairs={{0,16},{2,18},{4,20},{6,22},{8,24},{10,26},{12,28},{14,30},{16,0},... | collective-permute-start | bytes 786440 | tf_op jit(solution)/shard_map/ppermute | solution.py:55
  54.2 41.0 %collective-permute-start.14 = (bf16[128,3072]{1,0:T(8,128)(2,1)}, bf16[128,3072]{1,0:T(8,128)(2,1)S(1)}, u32[]{:S(2)}, u32[]{:S(2)}) collective-permute-start(bf16[128,3072]{1,0:T(8,128)(2,1)} %pad_maximum_fusion.4), channel_id=1, source_target_pairs={{0,8},{2,10},{4,12},{6,14},{8,0},{10,2},{12,4},{14,6},{16,24},{18,... | collective-permute-start | bytes 2359304 | tf_op jit(solution)/shard_map/ppermute | solution.py:55
  68.8 26.5 %collective-permute-start.15 = (bf16[256,512]{1,0:T(8,128)(2,1)S(1)}, bf16[256,512]{1,0:T(8,128)(2,1)S(1)}, u32[]{:S(2)}, u32[]{:S(2)}) collective-permute-start(bf16[256,512]{1,0:T(8,128)(2,1)S(1)} %collective-permute-done.11), channel_id=1, source_target_pairs={{0,4},{2,6},{4,0},{6,2},{8,12},{10,14},{12,8},{14,10},{16,20},{18,... | collective-permute-start | bytes 786440 | tf_op jit(solution)/shard_map/ppermute | solution.py:55
  69.9 25.4 %collective-permute-start.13 = (bf16[64,2048]{1,0:T(8,128)(2,1)S(1)}, bf16[64,2048]{1,0:T(8,128)(2,1)S(1)}, u32[]{:S(2)}, u32[]{:S(2)}) collective-permute-start(bf16[64,2048]{1,0:T(8,128)(2,1)S(1)} %copy-done.77), channel_id=1, source_target_pairs={{0,16},{2,18},{4,20},{6,22},{8,24},{10,26},{12,28},{14,30},{16,0},... | collective-permute-start | bytes 786440 | tf_op jit(solution)/shard_map/ppermute | solution.py:55
  72.9 22.4 %collective-permute-start.16 = (bf16[512,2048]{1,0:T(8,128)(2,1)S(1)}, bf16[512,2048]{1,0:T(8,128)(2,1)S(1)}, u32[]{:S(2)}, u32[]{:S(2)}) collective-permute-start(bf16[512,2048]{1,0:T(8,128)(2,1)S(1)} %pad_maximum_fusion.1.refs_8_.refs_14_), channel_id=1, source_target_pairs={{0,1},{1,0},{2,3},{3,2},{4,5},{5,4},{6,7},{7,6},{8,9},{9,8},{10,11... | collective-permute-start | bytes 6291464 | tf_op jit(solution)/shard_map/ppermute | solution.py:58
  94.7 30.7 %collective-permute-start.22 = (bf16[128,1536]{1,0:T(8,128)(2,1)S(1)}, bf16[128,1536]{1,0:T(8,128)(2,1)S(1)}, u32[]{:S(2)}, u32[]{:S(2)}) collective-permute-start(bf16[128,1536]{1,0:T(8,128)(2,1)S(1)} %copy-done.66), channel_id=1, source_target_pairs={{0,2},{2,0},{4,6},{6,4},{8,10},{10,8},{12,14},{14,12},{16,18},{18,... | collective-permute-start | bytes 1179656 | tf_op jit(solution)/shard_map/ppermute | solution.py:55
  95.4 38.8 %collective-permute-start.18 = (bf16[128,2048]{1,0:T(8,128)(2,1)S(1)}, bf16[128,2048]{1,0:T(8,128)(2,1)S(1)}, u32[]{:S(2)}, u32[]{:S(2)}) collective-permute-start(bf16[128,2048]{1,0:T(8,128)(2,1)S(1)} %bitcast.517), channel_id=1, source_target_pairs={{0,8},{2,10},{4,12},{6,14},{8,0},{10,2},{12,4},{14,6},{16,24},{18,... | collective-permute-start | bytes 1572872 | tf_op jit(solution)/shard_map/ppermute | solution.py:55
  97.5 36.7 %collective-permute-start.17 = (bf16[128,2048]{1,0:T(8,128)(2,1)S(1)}, bf16[128,2048]{1,0:T(8,128)(2,1)S(1)}, u32[]{:S(2)}, u32[]{:S(2)}) collective-permute-start(bf16[128,2048]{1,0:T(8,128)(2,1)S(1)} %bitcast.518), channel_id=1, source_target_pairs={{0,2},{2,0},{4,6},{6,4},{8,10},{10,8},{12,14},{14,12},{16,18},{18,... | collective-permute-start | bytes 1572872 | tf_op jit(solution)/shard_map/ppermute | solution.py:55
  98.7 25.7 %collective-permute-start.20 = (bf16[128,2048]{1,0:T(8,128)(2,1)S(1)}, bf16[128,2048]{1,0:T(8,128)(2,1)S(1)}, u32[]{:S(2)}, u32[]{:S(2)}) collective-permute-start(bf16[128,2048]{1,0:T(8,128)(2,1)S(1)} %pad_maximum_fusion.9), channel_id=1, source_target_pairs={{0,16},{2,18},{4,20},{6,22},{8,24},{10,26},{12,28},{14,30},{16,0},... | collective-permute-start | bytes 1572872 | tf_op jit(solution)/shard_map/ppermute | solution.py:55
  100.5 24.9 %collective-permute-start.19 = (bf16[192,2048]{1,0:T(8,128)(2,1)S(1)}, bf16[192,2048]{1,0:T(8,128)(2,1)S(1)}, u32[]{:S(2)}, u32[]{:S(2)}) collective-permute-start(bf16[192,2048]{1,0:T(8,128)(2,1)S(1)} %pad_maximum_fusion.5), channel_id=1, source_target_pairs={{0,4},{2,6},{4,0},{6,2},{8,12},{10,14},{12,8},{14,10},{16,20},{18,... | collective-permute-start | bytes 2359304 | tf_op jit(solution)/shard_map/ppermute | solution.py:55
  150.6 20.9 %collective-permute-start.29 = (bf16[512,2048]{1,0:T(8,128)(2,1)S(1)}, bf16[512,2048]{1,0:T(8,128)(2,1)S(1)}, u32[]{:S(2)}, u32[]{:S(2)}) collective-permute-start(bf16[512,2048]{1,0:T(8,128)(2,1)S(1)} %constant_dynamic-update-slice_fusion.refs_10_), channel_id=1, source_target_pairs={{0,1},{1,0},{2,3},{3,2},{4,5},{5,4},{6,7},{7,6},{8,9},{9,8},{10,11... | collective-permute-start | bytes 6291464 | tf_op jit(solution)/shard_map/ppermute | solution.py:58
  150.7 20.8 %collective-permute-start.30 = (bf16[64,2048]{1,0:T(8,128)(2,1)S(1)}, bf16[64,2048]{1,0:T(8,128)(2,1)S(1)}, u32[]{:S(2)}, u32[]{:S(2)}) collective-permute-start(bf16[64,2048]{1,0:T(8,128)(2,1)S(1)} %get-tuple-element.893), channel_id=1, source_target_pairs={{0,4},{2,6},{4,0},{6,2},{8,12},{10,14},{12,8},{14,10},{16,20},{18,... | collective-permute-start | bytes 786440 | tf_op jit(solution)/shard_map/ppermute | solution.py:55
  152.0 19.5 %collective-permute-start.32 = (bf16[256,512]{1,0:T(8,128)(2,1)S(1)}, bf16[256,512]{1,0:T(8,128)(2,1)S(1)}, u32[]{:S(2)}, u32[]{:S(2)}) collective-permute-start(bf16[256,512]{1,0:T(8,128)(2,1)S(1)} %bitcast.461), channel_id=1, source_target_pairs={{0,16},{2,18},{4,20},{6,22},{8,24},{10,26},{12,28},{14,30},{16,0},... | collective-permute-start | bytes 786440 | tf_op jit(solution)/shard_map/ppermute | solution.py:55
  154.7 16.0 %collective-permute-start.31 = (bf16[512,512]{1,0:T(8,128)(2,1)S(1)}, bf16[512,512]{1,0:T(8,128)(2,1)S(1)}, u32[]{:S(2)}, u32[]{:S(2)}) collective-permute-start(bf16[512,512]{1,0:T(8,128)(2,1)S(1)} %pad_maximum_fusion.11), channel_id=1, source_target_pairs={{0,4},{2,6},{4,0},{6,2},{8,12},{10,14},{12,8},{14,10},{16,20},{18,... | collective-permute-start | bytes 1572872 | tf_op jit(solution)/shard_map/ppermute | solution.py:55
  155.6 15.9 %collective-permute-start.33 = (bf16[128,2048]{1,0:T(8,128)(2,1)S(1)}, bf16[128,2048]{1,0:T(8,128)(2,1)S(1)}, u32[]{:S(2)}, u32[]{:S(2)}) collective-permute-start(bf16[128,2048]{1,0:T(8,128)(2,1)S(1)} %get-tuple-element.1433), channel_id=1, source_target_pairs={{0,2},{2,0},{4,6},{6,4},{8,10},{10,8},{12,14},{14,12},{16,18},{18,... | collective-permute-start | bytes 1572872 | tf_op jit(solution)/shard_map/ppermute | solution.py:55
  173.9 22.1 %collective-permute-start.34 = (bf16[2,1,192,2048]{3,2,0,1:T(8,128)(2,1)S(1)}, bf16[2,1,192,2048]{3,2,0,1:T(8,128)(2,1)S(1)}, u32[]{:S(2)}, u32[]{:S(2)}) collective-permute-start(bf16[2,1,192,2048]{3,2,0,1:T(8,128)(2,1)S(1)} %get-tuple-element.1445), channel_id=1, source_target_pairs={{0,1},{1,0},{2,3},{3,2},{4,5},{5,4},{6,7},{7,6},{8,9},{9,8},{10,11... | collective-permute-start | bytes 4718600 | tf_op jit(solution)/shard_map/ppermute | solution.py:58
  176.1 19.8 %collective-permute-start.38 = (bf16[128,2048]{1,0:T(8,128)(2,1)S(1)}, bf16[128,2048]{1,0:T(8,128)(2,1)S(1)}, u32[]{:S(2)}, u32[]{:S(2)}) collective-permute-start(bf16[128,2048]{1,0:T(8,128)(2,1)S(1)} %add_convert_fusion.4), channel_id=1, source_target_pairs={{0,8},{2,10},{4,12},{6,14},{8,0},{10,2},{12,4},{14,6},{16,24},{18,... | collective-permute-start | bytes 1572872 | tf_op jit(solution)/shard_map/ppermute | solution.py:55
  178.0 17.9 %collective-permute-start.37 = (bf16[128,2048]{1,0:T(8,128)(2,1)S(1)}, bf16[128,2048]{1,0:T(8,128)(2,1)S(1)}, u32[]{:S(2)}, u32[]{:S(2)}) collective-permute-start(bf16[128,2048]{1,0:T(8,128)(2,1)S(1)} %get-tuple-element.907), channel_id=1, source_target_pairs={{0,2},{2,0},{4,6},{6,4},{8,10},{10,8},{12,14},{14,12},{16,18},{18,... | collective-permute-start | bytes 1572872 | tf_op jit(solution)/shard_map/ppermute | solution.py:55
  178.3 16.9 %collective-permute-start.36 = (bf16[256,512]{1,0:T(8,128)(2,1)S(1)}, bf16[256,512]{1,0:T(8,128)(2,1)S(1)}, u32[]{:S(2)}, u32[]{:S(2)}) collective-permute-start(bf16[256,512]{1,0:T(8,128)(2,1)S(1)} %bitcast.463), channel_id=1, source_target_pairs={{0,16},{2,18},{4,20},{6,22},{8,24},{10,26},{12,28},{14,30},{16,0},... | collective-permute-start | bytes 786440 | tf_op jit(solution)/shard_map/ppermute | solution.py:55
  197.5 19.4 %collective-permute-start.42 = (bf16[128,2048]{1,0:T(8,128)(2,1)S(1)}, bf16[128,2048]{1,0:T(8,128)(2,1)S(1)}, u32[]{:S(2)}, u32[]{:S(2)}) collective-permute-start(bf16[128,2048]{1,0:T(8,128)(2,1)S(1)} %multiply_convert_fusion), channel_id=1, source_target_pairs={{0,8},{2,10},{4,12},{6,14},{8,0},{10,2},{12,4},{14,6},{16,24},{18,... | collective-permute-start | bytes 1572872 | tf_op jit(solution)/shard_map/ppermute | solution.py:55
  200.1 16.8 %collective-permute-start.41 = (bf16[128,2048]{1,0:T(8,128)(2,1)S(1)}, bf16[128,2048]{1,0:T(8,128)(2,1)S(1)}, u32[]{:S(2)}, u32[]{:S(2)}) collective-permute-start(bf16[128,2048]{1,0:T(8,128)(2,1)S(1)} %multiply_convert_fusion), channel_id=1, source_target_pairs={{0,2},{2,0},{4,6},{6,4},{8,10},{10,8},{12,14},{14,12},{16,18},{18,... | collective-permute-start | bytes 1572872 | tf_op jit(solution)/shard_map/ppermute | solution.py:55
  235.7 17.5 %collective-permute-start.48 = (bf16[512,2048]{1,0:T(8,128)(2,1)}, bf16[512,2048]{1,0:T(8,128)(2,1)}, u32[]{:S(2)}, u32[]{:S(2)}) collective-permute-start(bf16[512,2048]{1,0:T(8,128)(2,1)} %constant_dynamic-update-slice_fusion.4.refs_8_), channel_id=1, source_target_pairs={{0,1},{1,0},{2,3},{3,2},{4,5},{5,4},{6,7},{7,6},{8,9},{9,8},{10,11... | collective-permute-start | bytes 6291464 | tf_op jit(solution)/shard_map/ppermute | solution.py:58
  268.8 16.6 %collective-permute-start.50 = (bf16[512,512]{1,0:T(8,128)(2,1)S(1)}, bf16[512,512]{1,0:T(8,128)(2,1)S(1)}, u32[]{:S(2)}, u32[]{:S(2)}) collective-permute-start(bf16[512,512]{1,0:T(8,128)(2,1)S(1)} %bitcast.512), channel_id=1, source_target_pairs={{0,4},{2,6},{4,0},{6,2},{8,12},{10,14},{12,8},{14,10},{16,20},{18,... | collective-permute-start | bytes 1572872 | tf_op jit(solution)/shard_map/ppermute | solution.py:55
  285.7 16.1 %collective-permute-start.52 = (bf16[512,512]{1,0:T(8,128)(2,1)S(1)}, bf16[512,512]{1,0:T(8,128)(2,1)S(1)}, u32[]{:S(2)}, u32[]{:S(2)}) collective-permute-start(bf16[512,512]{1,0:T(8,128)(2,1)S(1)} %bitcast.511), channel_id=1, source_target_pairs={{0,4},{2,6},{4,0},{6,2},{8,12},{10,14},{12,8},{14,10},{16,20},{18,... | collective-permute-start | bytes 1572872 | tf_op jit(solution)/shard_map/ppermute | solution.py:55
  302.0 16.8 %collective-permute-start.55 = (bf16[512,2048]{1,0:T(8,128)(2,1)S(1)}, bf16[512,2048]{1,0:T(8,128)(2,1)S(1)}, u32[]{:S(2)}, u32[]{:S(2)}) collective-permute-start(bf16[512,2048]{1,0:T(8,128)(2,1)S(1)} %get-tuple-element.1148), channel_id=1, source_target_pairs={{0,1},{1,0},{2,3},{3,2},{4,5},{5,4},{6,7},{7,6},{8,9},{9,8},{10,11... | collective-permute-start | bytes 6291464 | tf_op jit(solution)/shard_map/ppermute | solution.py:58
  302.1 17.6 %collective-permute-start.53 = (bf16[256,512]{1,0:T(8,128)(2,1)S(1)}, bf16[256,512]{1,0:T(8,128)(2,1)S(1)}, u32[]{:S(2)}, u32[]{:S(2)}) collective-permute-start(bf16[256,512]{1,0:T(8,128)(2,1)S(1)} %bitcast.560), channel_id=1, source_target_pairs={{0,16},{2,18},{4,20},{6,22},{8,24},{10,26},{12,28},{14,30},{16,0},... | collective-permute-start | bytes 786440 | tf_op jit(solution)/shard_map/ppermute | solution.py:55
  339.9 16.6 %collective-permute-start.63 = (bf16[128,2048]{1,0:T(8,128)(2,1)S(1)}, bf16[128,2048]{1,0:T(8,128)(2,1)S(1)}, u32[]{:S(2)}, u32[]{:S(2)}) collective-permute-start(bf16[128,2048]{1,0:T(8,128)(2,1)S(1)} %add_convert_fusion.3), channel_id=1, source_target_pairs={{0,8},{2,10},{4,12},{6,14},{8,0},{10,2},{12,4},{14,6},{16,24},{18,... | collective-permute-start | bytes 1572872 | tf_op jit(solution)/shard_map/ppermute | solution.py:55
  340.0 16.5 %collective-permute-start.62 = (bf16[128,2048]{1,0:T(8,128)(2,1)S(1)}, bf16[128,2048]{1,0:T(8,128)(2,1)S(1)}, u32[]{:S(2)}, u32[]{:S(2)}) collective-permute-start(bf16[128,2048]{1,0:T(8,128)(2,1)S(1)} %get-tuple-element.1193), channel_id=1, source_target_pairs={{0,2},{2,0},{4,6},{6,4},{8,10},{10,8},{12,14},{14,12},{16,18},{18,... | collective-permute-start | bytes 1572872 | tf_op jit(solution)/shard_map/ppermute | solution.py:55
  360.2 16.5 %collective-permute-start.65 = (bf16[128,2048]{1,0:T(8,128)(2,1)S(1)}, bf16[128,2048]{1,0:T(8,128)(2,1)S(1)}, u32[]{:S(2)}, u32[]{:S(2)}) collective-permute-start(bf16[128,2048]{1,0:T(8,128)(2,1)S(1)} %get-tuple-element.1254), channel_id=1, source_target_pairs={{0,8},{2,10},{4,12},{6,14},{8,0},{10,2},{12,4},{14,6},{16,24},{18,... | collective-permute-start | bytes 1572872 | tf_op jit(solution)/shard_map/ppermute | solution.py:55
  360.2 16.5 %collective-permute-start.64 = (bf16[128,2048]{1,0:T(8,128)(2,1)S(1)}, bf16[128,2048]{1,0:T(8,128)(2,1)S(1)}, u32[]{:S(2)}, u32[]{:S(2)}) collective-permute-start(bf16[128,2048]{1,0:T(8,128)(2,1)S(1)} %get-tuple-element.1254), channel_id=1, source_target_pairs={{0,2},{2,0},{4,6},{6,4},{8,10},{10,8},{12,14},{14,12},{16,18},{18,... | collective-permute-start | bytes 1572872 | tf_op jit(solution)/shard_map/ppermute | solution.py:55
  378.3 16.9 %collective-permute-start.71 = (bf16[512,2048]{1,0:T(8,128)(2,1)}, bf16[512,2048]{1,0:T(8,128)(2,1)S(1)}, u32[]{:S(2)}, u32[]{:S(2)}) collective-permute-start(bf16[512,2048]{1,0:T(8,128)(2,1)} %get-tuple-element.1243), channel_id=1, source_target_pairs={{0,1},{1,0},{2,3},{3,2},{4,5},{5,4},{6,7},{7,6},{8,9},{9,8},{10,11... | collective-permute-start | bytes 6291464 | tf_op jit(solution)/shard_map/ppermute | solution.py:58
  379.1 19.2 %collective-permute-start.70 = (bf16[256,512]{1,0:T(8,128)(2,1)}, bf16[256,512]{1,0:T(8,128)(2,1)S(1)}, u32[]{:S(2)}, u32[]{:S(2)}) collective-permute-start(bf16[256,512]{1,0:T(8,128)(2,1)} %bitcast.557), channel_id=1, source_target_pairs={{0,16},{2,18},{4,20},{6,22},{8,24},{10,26},{12,28},{14,30},{16,0},... | collective-permute-start | bytes 786440 | tf_op jit(solution)/shard_map/ppermute | solution.py:55
  380.3 18.0 %collective-permute-start.69 = (bf16[128,2048]{1,0:T(8,128)(2,1)}, bf16[128,2048]{1,0:T(8,128)(2,1)S(1)}, u32[]{:S(2)}, u32[]{:S(2)}) collective-permute-start(bf16[128,2048]{1,0:T(8,128)(2,1)} %copy-done.94), channel_id=1, source_target_pairs={{0,2},{2,0},{4,6},{6,4},{8,10},{10,8},{12,14},{14,12},{16,18},{18,... | collective-permute-start | bytes 1572872 | tf_op jit(solution)/shard_map/ppermute | solution.py:55
  398.3 15.6 %collective-permute-start.72 = (bf16[64,2048]{1,0:T(8,128)(2,1)S(1)}, bf16[64,2048]{1,0:T(8,128)(2,1)S(1)}, u32[]{:S(2)}, u32[]{:S(2)}) collective-permute-start(bf16[64,2048]{1,0:T(8,128)(2,1)S(1)} %fusion.18), channel_id=1, source_target_pairs={{0,16},{2,18},{4,20},{6,22},{8,24},{10,26},{12,28},{14,30},{16,0},... | collective-permute-start | bytes 786440 | tf_op jit(solution)/shard_map/ppermute | solution.py:55
  414.4 22.7 %collective-permute-start.77 = (bf16[128,2048]{1,0:T(8,128)(2,1)S(1)}, bf16[128,2048]{1,0:T(8,128)(2,1)S(1)}, u32[]{:S(2)}, u32[]{:S(2)}) collective-permute-start(bf16[128,2048]{1,0:T(8,128)(2,1)S(1)} %bitcast.540), channel_id=1, source_target_pairs={{0,4},{2,6},{4,0},{6,2},{8,12},{10,14},{12,8},{14,10},{16,20},{18,... | collective-permute-start | bytes 1572872 | tf_op jit(solution)/shard_map/ppermute | solution.py:55
  415.7 23.5 %collective-permute-start.76 = (bf16[64,2048]{1,0:T(8,128)(2,1)S(1)}, bf16[64,2048]{1,0:T(8,128)(2,1)S(1)}, u32[]{:S(2)}, u32[]{:S(2)}) collective-permute-start(bf16[64,2048]{1,0:T(8,128)(2,1)S(1)} %fusion.19), channel_id=1, source_target_pairs={{0,16},{2,18},{4,20},{6,22},{8,24},{10,26},{12,28},{14,30},{16,0},... | collective-permute-start | bytes 786440 | tf_op jit(solution)/shard_map/ppermute | solution.py:55
  417.4 21.8 %collective-permute-start.78 = (bf16[128,1536]{1,0:T(8,128)(2,1)S(1)}, bf16[128,1536]{1,0:T(8,128)(2,1)S(1)}, u32[]{:S(2)}, u32[]{:S(2)}) collective-permute-start(bf16[128,1536]{1,0:T(8,128)(2,1)S(1)} %pad_maximum_fusion.19), channel_id=1, source_target_pairs={{0,10},{2,8},{4,14},{6,12},{8,2},{10,0},{12,6},{14,4},{16,26},{18,... | collective-permute-start | bytes 1179656 | tf_op jit(solution)/shard_map/ppermute | solution.py:55
  417.9 21.2 %collective-permute-start.79 = (bf16[128,1536]{1,0:T(8,128)(2,1)S(1)}, bf16[128,1536]{1,0:T(8,128)(2,1)S(1)}, u32[]{:S(2)}, u32[]{:S(2)}) collective-permute-start(bf16[128,1536]{1,0:T(8,128)(2,1)S(1)} %pad_maximum_fusion.20), channel_id=1, source_target_pairs={{0,2},{2,0},{4,6},{6,4},{8,10},{10,8},{12,14},{14,12},{16,18},{18,... | collective-permute-start | bytes 1179656 | tf_op jit(solution)/shard_map/ppermute | solution.py:55
  419.6 20.0 %collective-permute-start.80 = (bf16[128,1536]{1,0:T(8,128)(2,1)S(1)}, bf16[128,1536]{1,0:T(8,128)(2,1)S(1)}, u32[]{:S(2)}, u32[]{:S(2)}) collective-permute-start(bf16[128,1536]{1,0:T(8,128)(2,1)S(1)} %pad_maximum_fusion.21), channel_id=1, source_target_pairs={{0,8},{2,10},{4,12},{6,14},{8,0},{10,2},{12,4},{14,6},{16,24},{18,... | collective-permute-start | bytes 1179656 | tf_op jit(solution)/shard_map/ppermute | solution.py:55
  439.8 15.9 %collective-permute-start.85 = (bf16[512,2048]{1,0:T(8,128)(2,1)}, bf16[512,2048]{1,0:T(8,128)(2,1)}, u32[]{:S(2)}, u32[]{:S(2)}) collective-permute-start(bf16[512,2048]{1,0:T(8,128)(2,1)} %get-tuple-element.1323), channel_id=1, source_target_pairs={{0,1},{1,0},{2,3},{3,2},{4,5},{5,4},{6,7},{7,6},{8,9},{9,8},{10,11... | collective-permute-start | bytes 6291464 | tf_op jit(solution)/shard_map/ppermute | solution.py:58
  442.0 17.3 %collective-permute-start.83 = (bf16[4,128,1536]{2,1,0:T(8,128)(2,1)}, bf16[4,128,1536]{2,1,0:T(8,128)(2,1)}, u32[]{:S(2)}, u32[]{:S(2)}) collective-permute-start(bf16[4,128,1536]{2,1,0:T(8,128)(2,1)} %pad_maximum_fusion.3), channel_id=1, source_target_pairs={{0,1},{1,0},{2,3},{3,2},{4,5},{5,4},{6,7},{7,6},{8,9},{9,8},{10,11... | collective-permute-start | bytes 4718600 | tf_op jit(solution)/shard_map/ppermute | solution.py:58
  442.8 16.5 %collective-permute-start.81 = (bf16[64,2048]{1,0:T(8,128)(2,1)S(1)}, bf16[64,2048]{1,0:T(8,128)(2,1)S(1)}, u32[]{:S(2)}, u32[]{:S(2)}) collective-permute-start(bf16[64,2048]{1,0:T(8,128)(2,1)S(1)} %fusion.20), channel_id=1, source_target_pairs={{0,16},{2,18},{4,20},{6,22},{8,24},{10,26},{12,28},{14,30},{16,0},... | collective-permute-start | bytes 786440 | tf_op jit(solution)/shard_map/ppermute | solution.py:55
  478.6 18.6 %collective-permute-start.99 = (bf16[256,512]{1,0:T(8,128)(2,1)S(1)}, bf16[256,512]{1,0:T(8,128)(2,1)S(1)}, u32[]{:S(2)}, u32[]{:S(2)}) collective-permute-start(bf16[256,512]{1,0:T(8,128)(2,1)S(1)} %bitcast.554), channel_id=1, source_target_pairs={{0,16},{2,18},{4,20},{6,22},{8,24},{10,26},{12,28},{14,30},{16,0},... | collective-permute-start | bytes 786440 | tf_op jit(solution)/shard_map/ppermute | solution.py:55
  480.0 18.7 %collective-permute-start.98 = (bf16[128,2048]{1,0:T(8,128)(2,1)S(1)}, bf16[128,2048]{1,0:T(8,128)(2,1)S(1)}, u32[]{:S(2)}, u32[]{:S(2)}) collective-permute-start(bf16[128,2048]{1,0:T(8,128)(2,1)S(1)} %add_convert_fusion.2), channel_id=1, source_target_pairs={{0,8},{2,10},{4,12},{6,14},{8,0},{10,2},{12,4},{14,6},{16,24},{18,... | collective-permute-start | bytes 1572872 | tf_op jit(solution)/shard_map/ppermute | solution.py:55
  499.9 16.8 %collective-permute-start.100 = (bf16[64,2048]{1,0:T(8,128)(2,1)S(1)}, bf16[64,2048]{1,0:T(8,128)(2,1)S(1)}, u32[]{:S(2)}, u32[]{:S(2)}) collective-permute-start(bf16[64,2048]{1,0:T(8,128)(2,1)S(1)} %fusion.23), channel_id=1, source_target_pairs={{0,16},{2,18},{4,20},{6,22},{8,24},{10,26},{12,28},{14,30},{16,0},... | collective-permute-start | bytes 786440 | tf_op jit(solution)/shard_map/ppermute | solution.py:55
  (179 other events, 1712.8 us)

commit v3 on v2

--- a/solution.py
+++ b/solution.py
@@ -184,6 +184,11 @@
     return [own, g.pt(along_t, 0, 1), along_u, along_t]
 
 
+def gather_two_along_t(g, near):
+    own, along_u, along_t = near
+    return [own, g.pt(along_u, 1, 0), along_u, along_t]
+
+
 def scatter_one(g, blocks):
     own, far, to_u, to_t = blocks
     return own, to_u, to_t, g.pt(far.astype(BF16), 0, 1)
@@ -336,7 +341,7 @@
         out_specs=[vmem] * len(outs),
         out_shape=[jax.ShapeDtypeStruct(shape, dtype) for shape, dtype in outs],
         scratch_shapes=[pltpu.VMEM(shape, dtype) for shape, dtype in scratch],
-        compiler_params=pltpu.CompilerParams(vmem_limit_bytes=20 << 20),
+        compiler_params=pltpu.CompilerParams(vmem_limit_bytes=16 << 20),
         cost_estimate=pl.CostEstimate(flops=1 << 20, bytes_accessed=1 << 16, transcendentals=0),
         name=name,
     )(*ins)
@@ -663,12 +668,12 @@
     third = rows_d // 6
     seg_low = segments[0].astype(BF16)[None]
     seg_low = jnp.pad(seg_low, ((0, 15), (0, width - seq_len)))
-    first, later = [], []
+    qkv_cuts, gu_cuts = [], []
     for dt, du in ORDER:
         t, u = g.t ^ dt, g.u ^ du
         kv = g.kv_head(t, u, g.c, rows_o)
-        first.append([(0, kv * hd2, hd2), (1, kv * HD, HD), (2, kv * HD, HD)])
-        later.append(
+        qkv_cuts.append([(2, kv * hd2, hd2), (3, kv * HD, HD), (4, kv * HD, HD)])
+        gu_cuts.append(
             [
                 (k, at, w)
                 for part in range(PARTS)
@@ -676,9 +681,10 @@
                 for at, w in hidden_cuts(t, u, g.c, part)
             ]
         )
-    first = cut_columns([w_q, w_k, w_v], first)
-    later = cut_columns([w_g, w_u], later)
-    L = Live(qkv=first)
+    cuts = [qkv_cuts[0], qkv_cuts[1], qkv_cuts[2] + gu_cuts[2], qkv_cuts[3]]
+    cuts += [gu_cuts[0], gu_cuts[3] + gu_cuts[1]]
+    cut = cut_columns([w_g, w_u, w_q, w_k, w_v], cuts)
+    L = Live(qkv=cut[:4])
     S = Shards(g, L)
     S.fetch("o", [half_o])
     S.fetch("d", [half_d[k * third : (k + 1) * third] for k in range(3)])
@@ -696,29 +702,34 @@
     S.fetch_a(("o", 0))
     S.fetch_b(("o", 0, False))
     L.xn, L.cot = jnp.concatenate([xn_own, seg_low]), cotangent[0]
-    L.gu = (later[0], later[2], jnp.concatenate([later[1], later[3]], axis=1))
+    L.gu, L.gu_t, L.gu_f = cut[4], cut[5][:, : 2 * units], cut[5][:, 2 * units :]
     done()
 
     L.xn = gather_one(g, L.xn)
+    L.gu_u = L.qkv[2][:, 4 * HD :]
+    L.qkv[2] = L.qkv[2][:, : 4 * HD]
     S.fetch("qkv", pairs(L.qkv))
     S.fetch_a(("qkv", 0))
-    S.fetch_b(("qkv", 0, False), ("qkv", 1, False))
+    S.fetch_b(("qkv", 0, False), ("qkv", 1, False), ("o", 0, True))
     done()
     L.xn = gather_two(g, L.xn)
     S.fetch_a(("qkv", 1))
-    S.fetch_b(("qkv", 0, True), ("o", 0, True))
-    L.gu_t = g.pt(L.gu[2], 1, 0)
-    done("gu_t")
+    S.fetch_b(("qkv", 0, True))
+    L.gu_f = g.pt(L.gu_f, 1, 0)
+    o_blocks = S.rows("o").reshape(2, 2, Q, rows_o // 2, width)
+    L.o = (pick(o_blocks, g.u), pick(o_blocks, 1 - g.u))
+    done()
 
     near = jnp.concatenate([x[:span] for x in L.xn])
     L.seg = [x[span, :seq_len] for x in L.xn]
     L.xn = (near, g.pc(near))
+    L.gu_t = g.pt(L.gu_t, 1, 0)
+    joined = rows_in == span
+    if joined:
+        L.gu_f = jnp.concatenate([L.cot, L.gu_f], axis=1)
     S.fetch_a(("d", 0))
     S.fetch_b(("qkv", 1, True))
-    o_blocks = S.rows("o").reshape(2, 2, Q, rows_o // 2, width)
-    o_mine = pick(o_blocks, g.u)
-    o_next = g.px(pick(o_blocks, 1 - g.u), g.umask)
-    L.gu_u = g.pt(L.gu[1], 0, 1)
+    L.o = (L.o[0], g.px(L.o[1], g.umask))
     seg_all = jnp.stack(L.seg)
     index = lax.broadcasted_iota(jnp.int32, (4, seq_len), 1)
     earlier = seg_all[:, None, :] < seg_all[:, :, None]
@@ -736,8 +747,7 @@
         seg_own[:, :, None] == seg_own[:, None, :]
     )
     L.mask = same_doc.astype(F32)
-    L.o = (o_mine, o_next)
-    done("gu_u", "o")
+    done()
 
     def core_sum(own, sent):
         return own + g.pc(sent).astype(F32)
@@ -745,10 +755,14 @@
     def chip_blocks(x):
         return [x[k * span : (k + 1) * span] for k in range(4)]
 
-    L.cot = gather_one(g, L.cot)
-    pass_on, along_t = L.gu_t[:, : 2 * units], L.gu_t[:, 2 * units :]
-    L.gu = [L.gu[0], g.pt(pass_on, 0, 1), L.gu_u, along_t]
-    del L["gu_t"], L["gu_u"]
+    if joined:
+        both = g.pt(L.gu_f, 0, 1)
+        L.cot = (L.cot, both[:, :width], g.pt(L.cot, 1, 0))
+        L.gu_f = both[:, width:]
+    else:
+        L.cot, L.gu_f = gather_one(g, L.cot), g.pt(L.gu_f, 0, 1)
+    L.gu = [L.gu, L.gu_f, L.gu_u, L.gu_t]
+    del L["gu_t"], L["gu_u"], L["gu_f"]
     S.fetch_a(("d", 1), ("d", 2))
     S.fetch_b(("d", 0, False), ("d", 1, False), ("d", 2, False))
     o_mine, o_next = L.o
@@ -762,7 +776,6 @@
     done()
 
     L.part = core_sum(*L.part)
-    L.cot = gather_two(g, L.cot)
     for k in range(PARTS):
         S.fetch(f"gu{k + 1}", pairs([x[:, 2 * pw * k : 2 * pw * (k + 1)] for x in L.gu]))
     del L["gu"]
@@ -773,14 +786,15 @@
     L.part = scatter_one(g, chip_blocks(L.part))
     S.fetch_a(("gu1", 1))
     S.fetch_b(("d", 2, True), ("gu1", 0, False), ("gu1", 1, False))
-    cot_near = jnp.concatenate(L.cot)
-    L.cot = (cot_near, g.pc(cot_near))
+    L.cot = gather_two_along_t(g, L.cot)
     done()
     L.part = scatter_two(g, L.part)
     S.fetch_a(("gu2", 0))
     S.fetch_b(("gu1", 0, True), ("gu1", 1, True))
+    cot_near = jnp.concatenate(L.cot)
+    L.cot = (cot_near, g.pc(cot_near))
     d_blocks = S.rows("d").reshape(A, 2, B // 2, rows_d // 2, width).transpose(1, 0, 2, 3, 4)
-    L.d = (pick(d_blocks, g.c), g.pc(pick(d_blocks, 1 - g.c)))
+    L.d = (pick(d_blocks, g.c), pick(d_blocks, 1 - g.c))
     done()
 
     mid = x_own + add_all(L.part)
@@ -788,6 +802,7 @@
     L.xn2 = gather_one(g, xn2_own.astype(BF16))
     S.fetch_a(("gu2", 1))
     S.fetch_b(("gu2", 0, False), ("gu2", 1, False))
+    L.d = (L.d[0], g.pc(L.d[1]))
     done()
     L.xn2 = gather_two(g, L.xn2)
     S.fetch_a(("gu3", 0))
@@ -878,7 +893,8 @@
     S.prepare_a(("d", 1))
     S.total_a(("d", 0))
     S.finish("gu3")
-    L.out = scatter_one(g, chip_blocks(L.out))
+    out = chip_blocks(L.out)
+    L.out = scatter_one(g, out)
     grads = [columns_pieces(g, L[f"gu{k + 1}"]) for k in range(PARTS)]
     L.gu = [jnp.concatenate(x, axis=1) for x in zip(*grads)]
     done()
@@ -903,7 +919,8 @@
     S.prepare_a(("qkv", 0))
     S.total_a(("d", 2))
     L.o = (L.o[0], g.px(L.o[1], g.umask))
-    L.gu = (L.gu, g.pc(jnp.stack(L.gu)))
+    own, to_u, to_t, relayed = L.out
+    L.out = (own, to_u, g.pt((to_t + relayed.astype(F32)).astype(BF16), 1, 0))
     L.gains = L.gains + g.pc(L.gains)
     done()
 
@@ -923,34 +940,48 @@
         L.gains = L.gains + g.px(L.gains, 1 << bit)
     done()
     L.part = scatter_two(g, L.part)
-    for bit in range(bits // 2, bits):
+    for bit in range(bits // 2, bits - 1):
         L.gains = L.gains + g.px(L.gains, 1 << bit)
     S.total_b(("o", 0))
     S.total_a(("qkv", 1))
     S.prepare_a(("o", 0))
     S.finish("qkv")
+    L.gu = (L.gu, g.pc(jnp.stack(L.gu)))
     d_sum = jnp.concatenate([L.d[k] for k in range(3)])
-    L.d = (d_sum, g.pc(d_sum))
-    done()
-
+    L.d = d_sum
+    done()
+
+    def both_cores(pair):
+        near, far = pair
+        return list(near) + [far[k] for k in range(4)]
+
+    pieces, places = both_cores(L.gu), []
+    for part in range(PARTS):
+        for j, piece in enumerate(pieces):
+            dt, du = ORDER[j % 4]
+            at = 2 * pw * part
+            for to, w in hidden_cuts(g.t ^ dt, g.u ^ du, g.c ^ (j // 4), part):
+                places += [
+                    (j, at, w, 0, to),
+                    (j, pw + at, w, 1, to),
+                ]
+                at += w
+    L.gate, L.up = place_columns(pieces, [hidden_width, hidden_width], places)
     S.total_a(("o", 0))
     L.qkv = chips_swap(g, columns_pieces(g, L.qkv))
+    own, to_u, from_t = L.out
+    L.out = (own, g.pt(to_u.astype(BF16), 0, 1), from_t)
     _, in_back = jax.vjp(lambda x: rms_scale(x, g_in), x_own)
     L.d_tokens = (d_mid + in_back(add_all(L.part))[0]).astype(BF16)
-    grad_down = swap_halves(g, *L.d).reshape(1, rows_d, width).astype(F32)
-    done()
-
-    gains = L.gains[None]
+    done("out")
+
+    L.d = swap_halves(g, L.d, g.pc(L.d)).reshape(1, rows_d, width).astype(F32)
+    gains = (L.gains + g.px(L.gains, 1 << (bits - 1)))[None]
     S.finish("o")
-    L.out = scatter_two(g, L.out)
     L.qkv = (L.qkv, g.pc(jnp.stack(L.qkv)))
     grad_output = swap_halves(g, L.o[0], g.pc(L.o[0])).reshape(1, rows_o, width).astype(F32)
     activations = (mid + add_all(L.out)).astype(BF16)
     d_tokens = L.d_tokens
-
-    def both_cores(pair):
-        near, far = pair
-        return list(near) + [far[k] for k in range(4)]
 
     pieces = both_cores(L.qkv)
     places = []
@@ -964,19 +995,6 @@
         ]
     grad_query, grad_key, grad_value = place_columns(pieces, [q_width, kv_width, kv_width], places)
 
-    pieces, places = both_cores(L.gu), []
-    for part in range(PARTS):
-        for j, piece in enumerate(pieces):
-            dt, du = ORDER[j % 4]
-            at = 2 * pw * part
-            for to, w in hidden_cuts(g.t ^ dt, g.u ^ du, g.c ^ (j // 4), part):
-                places += [
-                    (j, at, w, 0, to),
-                    (j, pw + at, w, 1, to),
-                ]
-                at += w
-    grad_gate, grad_up = place_columns(pieces, [hidden_width, hidden_width], places)
-
     return (
         activations[None],
         d_tokens[None],
@@ -984,9 +1002,9 @@
         grad_key[None],
         grad_value[None],
         grad_output,
-        grad_gate[None],
-        grad_up[None],
-        grad_down,
+        L.gate[None],
+        L.up[None],
+        L.d,
         gains[:, :width],
         gains[:, 2 * width : 2 * width + HD],
         gains[:, 2 * width + HD :],

time: 543 us -> 527 us (0.971)
  waiting for transfers between devices: 238 us -> 219 us
  local copies, waits for them, and re-layouts: 53.6 us -> 63.8 us
  starting transfers between devices: 114 us -> 106 us
    ppermute x91 -> x90, waiting for transfers between devices: 237 us -> 219 us  [px(): return lax.ppermute(x, 'fsdp', [(i, i ^ mask) for i in range(self.n)])]
    ppermute x91 -> x90, starting transfers between devices: 112 us -> 105 us  [px(): return lax.ppermute(x, 'fsdp', [(i, i ^ mask) for i in range(self.n)])]
    unnamed x247 -> x271, local copies, waits for them, and re-layouts: 18.7 us -> 24.6 us
  transfers between devices with their start and end apart: 108 -> 107, of which waited for: 44 -> 42; matrix products, arithmetic and copies ran while one was open for 13% -> 13% of each run, Pallas kernels for 15% -> 15%
where the time goes in v3:
time: 527 us; the launch traced here: 519 us
  waiting for transfers between devices  219 us (42%)
  starting transfers between devices  106 us (20%)
  Pallas kernels  80.6 us (15%)
  local copies, waits for them, and re-layouts  63.8 us (12%)
  other arithmetic  43.9 us (8%)
    ppermute x90, waiting for transfers between devices, px(): return lax.ppermute(x, 'fsdp', [(i, i ^ mask) for i in range(self.n)])  219 us
    ppermute x90, starting transfers between devices, px(): return lax.ppermute(x, 'fsdp', [(i, i ^ mask) for i in range(self.n)])  105 us
    pallas_call x7, Pallas kernels, kernel_call(): pl.pallas_call(kernel, in_specs=[smem if x.dtype == jnp.int32 else vmem f...  73.9 us
    unnamed x271, local copies, waits for them, and re-layouts  24.6 us
  transfers between devices with their start and end apart: 107, of which 42 were waited for; matrix products, arithmetic and copies ran while one was open for 13% of the time, Pallas kernels for 15%

profile of v3, /device:TPU:0, one launch (start us, length us, event | category | flops | bytes accessed | tf_op | source)
XLA Modules:
  0.0 518.6 jit_solution(12323644137084221042)
XLA Ops:
  7.9 4.1 collective-permute-start.1
  13.5 2.5 collective-permute-start.2
  18.3 3.5 collective-permute-done.2
  21.8 4.6 collective-permute-done.4
  26.4 4.0 collective-permute-done.3
  31.1 3.0 collective-permute-start.9
  36.2 9.3 %collective-permute-done.6 = bf16[512,512]{1,0:T(8,128)(2,1)S(1)} collective-permute-done((bf16[512,512]{1,0:T(8,128)(2,1)S(1)}, bf16[512,512]{1,0:T(8,128)(2,1)S(1)}, u32[]{:S(2)}, u32[]{:S(2)}) %collective-permute-start.6) | collective-permute-done | bytes 524320 | tf_op jit(solution)/shard_map/ppermute | solution.py:55
  46.3 4.3 collective-permute-done.7
  51.5 2.7 collective-permute-start.12
  60.4 3.2 collective-permute-done.12
  63.7 5.4 %collective-permute-done.10 = bf16[128,1536]{1,0:T(8,128)(2,1)S(1)} collective-permute-done((bf16[128,1536]{1,0:T(8,128)(2,1)S(1)}, bf16[128,1536]{1,0:T(8,128)(2,1)S(1)}, u32[]{:S(2)}, u32[]{:S(2)}) %collective-permute-start.10) | collective-permute-done | bytes 393248 | tf_op jit(solution)/shard_map/ppermute | solution.py:55
  83.6 5.9 %collective-permute-done.14 = bf16[64,2048]{1,0:T(8,128)(2,1)S(1)} collective-permute-done((bf16[64,2048]{1,0:T(8,128)(2,1)}, bf16[64,2048]{1,0:T(8,128)(2,1)S(1)}, u32[]{:S(2)}, u32[]{:S(2)}) %collective-permute-start.14) | collective-permute-done | bytes 262176 | tf_op jit(solution)/shard_map/ppermute | solution.py:55
  107.4 10.2 %attend.1 = (bf16[2048,512]{1,0:T(8,128)(2,1)S(1)}, f32[1024,384]{1,0:T(8,128)S(1)}, bf16[4,256,256]{2,1,0:T(8,128)(2,1)S(1)}, bf16[4,256,128]{2,1,0:T(8,128)(2,...) custom-call(s32[16]{0:T(128)S(1)} %stack.663.rows_ref, ...), custom_call_target="tpu_custom_call" | custom-call | flops 1048576 | bytes 65536 | tf_op jit(solution)/shard_map/attend/pallas_call | solution.py:338
  128.7 12.3 %collective-permute-done.24 = bf16[128,2048]{1,0:T(8,128)(2,1)S(1)} collective-permute-done((bf16[128,2048]{1,0:T(8,128)(2,1)S(1)}, bf16[128,2048]{1,0:T(8,128)(2,1)S(1)}, u32[]{:S(2)}, u32[]{:S(2)}) %collective-permute-start.24) | collective-permute-done | bytes 524320 | tf_op jit(solution)/shard_map/ppermute | solution.py:55
  142.5 2.6 collective-permute-start.30
  149.3 11.6 %collective-permute-done.29 = bf16[512,512]{1,0:T(8,128)(2,1)S(1)} collective-permute-done((bf16[512,512]{1,0:T(8,128)(2,1)S(1)}, bf16[512,512]{1,0:T(8,128)(2,1)S(1)}, u32[]{:S(2)}, u32[]{:S(2)}) %collective-permute-start.29) | collective-permute-done | bytes 524320 | tf_op jit(solution)/shard_map/ppermute | solution.py:55
  171.1 5.2 collective-permute-done.33
  177.1 5.3 %collective-permute-done.36 = bf16[128,2048]{1,0:T(8,128)(2,1)S(1)} collective-permute-done((bf16[128,2048]{1,0:T(8,128)(2,1)S(1)}, bf16[128,2048]{1,0:T(8,128)(2,1)S(1)}, u32[]{:S(2)}, u32[]{:S(2)}) %collective-permute-start.36) | collective-permute-done | bytes 524320 | tf_op jit(solution)/shard_map/ppermute | solution.py:55
  185.7 2.5 collective-permute-start.39
  188.2 8.8 %collective-permute-done.38 = bf16[512,512]{1,0:T(8,128)(2,1)S(1)} collective-permute-done((bf16[512,512]{1,0:T(8,128)(2,1)S(1)}, bf16[512,512]{1,0:T(8,128)(2,1)S(1)}, u32[]{:S(2)}, u32[]{:S(2)}) %collective-permute-start.38) | collective-permute-done | bytes 524320 | tf_op jit(solution)/shard_map/ppermute | solution.py:55
  197.8 3.5 collective-permute-done.39
  207.8 8.8 %collective-permute-done.42 = bf16[512,512]{1,0:T(8,128)(2,1)S(1)} collective-permute-done((bf16[512,512]{1,0:T(8,128)(2,1)S(1)}, bf16[512,512]{1,0:T(8,128)(2,1)S(1)}, u32[]{:S(2)}, u32[]{:S(2)}) %collective-permute-start.42) | collective-permute-done | bytes 524320 | tf_op jit(solution)/shard_map/ppermute | solution.py:55
  226.3 12.8 %collective-permute-done.45 = bf16[512,512]{1,0:T(8,128)(2,1)} collective-permute-done((bf16[512,512]{1,0:T(8,128)(2,1)}, bf16[512,512]{1,0:T(8,128)(2,1)}, u32[]{:S(2)}, u32[]{:S(2)}) %collective-permute-start.45) | collective-permute-done | bytes 524320 | tf_op jit(solution)/shard_map/ppermute | solution.py:55
  244.1 11.6 %feed.3 = (bf16[1024,256]{1,0:T(8,128)(2,1)S(1)}, bf16[256,2048]{1,0:T(8,128)(2,1)S(1)}, bf16[2,2,128,512]{3,2,1,0:T(8,128)(2,1)S(1)}, bf16[2,2,128,512]{3,2,1,0...) custom-call(s32[16]{0:T(128)S(1)} %stack.663.rows_ref, ...), custom_call_target="tpu_custom_call" | custom-call | flops 1048576 | bytes 65536 | tf_op jit(solution)/shard_map/feed/pallas_call | solution.py:338
  257.4 15.5 %feed.4 = (bf16[1024,256]{1,0:T(8,128)(2,1)S(1)}, bf16[256,2048]{1,0:T(8,128)(2,1)S(1)}, bf16[2,2,128,512]{3,2,1,0:T(8,128)(2,1)S(1)}, bf16[2,2,128,512]{3,2,1,0...) custom-call(s32[16]{0:T(128)S(1)} %stack.663.rows_ref, ...), custom_call_target="tpu_custom_call" | custom-call | flops 1048576 | bytes 65536 | tf_op jit(solution)/shard_map/feed/pallas_call | solution.py:338
  275.1 14.4 %feed.5 = (bf16[1024,256]{1,0:T(8,128)(2,1)S(1)}, bf16[256,2048]{1,0:T(8,128)(2,1)S(1)}, bf16[2,2,128,512]{3,2,1,0:T(8,128)(2,1)S(1)}, bf16[2,2,128,512]{3,2,1,0...) custom-call(s32[16]{0:T(128)S(1)} %stack.663.rows_ref, ...), custom_call_target="tpu_custom_call" | custom-call | flops 1048576 | bytes 65536 | tf_op jit(solution)/shard_map/feed/pallas_call | solution.py:338
  293.7 11.8 %collective-permute-done.53 = bf16[512,512]{1,0:T(8,128)(2,1)S(1)} collective-permute-done((bf16[512,512]{1,0:T(8,128)(2,1)S(1)}, bf16[512,512]{1,0:T(8,128)(2,1)S(1)}, u32[]{:S(2)}, u32[]{:S(2)}) %collective-permute-start.53) | collective-permute-done | bytes 524320 | tf_op jit(solution)/shard_map/ppermute | solution.py:55
  311.7 9.2 %collective-permute-done.57 = bf16[512,512]{1,0:T(8,128)(2,1)S(1)} collective-permute-done((bf16[512,512]{1,0:T(8,128)(2,1)S(1)}, bf16[512,512]{1,0:T(8,128)(2,1)S(1)}, u32[]{:S(2)}, u32[]{:S(2)}) %collective-permute-start.57) | collective-permute-done | bytes 524320 | tf_op jit(solution)/shard_map/ppermute | solution.py:55
  323.5 2.5 collective-permute-start.59
  331.5 4.8 project_out.3
  338.6 4.6 collective-permute-done.62
  348.1 2.7 collective-permute-start.65
  352.4 2.7 collective-permute-done.66
  356.9 4.6 collective-permute-done.65
  367.6 12.3 %collective-permute-done.67 = bf16[128,2048]{1,0:T(8,128)(2,1)} collective-permute-done((bf16[128,2048]{1,0:T(8,128)(2,1)}, bf16[128,2048]{1,0:T(8,128)(2,1)}, u32[]{:S(2)}, u32[]{:S(2)}) %collective-permute-start.67) | collective-permute-done | bytes 524320 | tf_op jit(solution)/shard_map/ppermute | solution.py:55
  382.1 2.8 convert_add_fusion.1
  392.2 7.4 %collective-permute-done.72 = bf16[128,2048]{1,0:T(8,128)(2,1)S(1)} collective-permute-done((bf16[128,2048]{1,0:T(8,128)(2,1)S(1)}, bf16[128,2048]{1,0:T(8,128)(2,1)S(1)}, u32[]{:S(2)}, u32[]{:S(2)}) %collective-permute-start.72) | collective-permute-done | bytes 524320 | tf_op jit(solution)/shard_map/ppermute | solution.py:55
  407.6 16.1 %attend_back.1 = (f32[512,2048]{1,0:T(8,128)S(1)}, bf16[512,2048]{1,0:T(8,128)(2,1)}, bf16[256,2048]{1,0:T(8,128)(2,1)S(1)}, f32[2,128]{1,0:T(2,128)S(1)}, f32[1...) custom-call(s32[8]{0:T(128)S(1)} %stack.702.rows_out_ref.rows_ref, ...), custom_call_target="tpu_custom_call" | custom-call | flops 1048576 | bytes 65536 | tf_op jit(solution)/shard_map/attend_back/pallas_call | solution.py:338
  434.5 7.8 %collective-permute-done.85 = bf16[512,512]{1,0:T(8,128)(2,1)} collective-permute-done((bf16[512,512]{1,0:T(8,128)(2,1)}, bf16[512,512]{1,0:T(8,128)(2,1)}, u32[]{:S(2)}, u32[]{:S(2)}) %collective-permute-start.85) | collective-permute-done | bytes 524320 | tf_op jit(solution)/shard_map/ppermute | solution.py:55
  443.6 2.5 convert_add_fusion
  446.1 4.8 collective-permute-done.83
  456.7 9.1 %collective-permute-done.87 = f32[4352]{0:T(1024)S(1)} collective-permute-done((f32[4352]{0:T(1024)S(1)}, f32[4352]{0:T(1024)S(1)}, u32[]{:S(2)}, u32[]{:S(2)}) %collective-permute-start.87) | collective-permute-done | bytes 17440 | tf_op jit(solution)/shard_map/ppermute | solution.py:55
  466.4 2.6 collective-permute-done.89
  475.8 9.7 %collective-permute-done.97 = bf16[256,512]{1,0:T(8,128)(2,1)S(1)} collective-permute-done((bf16[256,512]{1,0:T(8,128)(2,1)S(1)}, bf16[256,512]{1,0:T(8,128)(2,1)S(1)}, u32[]{:S(2)}, u32[]{:S(2)}) %collective-permute-start.97) | collective-permute-done | bytes 262176 | tf_op jit(solution)/shard_map/ppermute | solution.py:55
  486.0 4.5 collective-permute-done.96
  497.8 3.8 place_columns.2
  501.8 3.9 collective-permute-done.100.refs_1_
  506.6 3.8 collective-permute-done.106
  (658 shorter events, 202.0 us)
Async XLA Ops:
  7.9 18.5 %collective-permute-start.1 = (bf16[64,2048]{1,0:T(8,128)(2,1)}, bf16[64,2048]{1,0:T(8,128)(2,1)}, u32[]{:S(2)}, u32[]{:S(2)}) collective-permute-start(bf16[64,2048]{1,0:T(8,128)(2,1)} %get-tuple-element.744), channel_id=1, source_target_pairs={{0,16},{2,18},{4,20},{6,22},{8,24},{10,26},{12,28},{14,30},{16,0},... | collective-permute-start | bytes 786440 | tf_op jit(solution)/shard_map/ppermute | solution.py:55
  31.1 20.3 %collective-permute-start.9 = (bf16[144,2048]{1,0:T(8,128)(2,1)S(1)}, bf16[144,2048]{1,0:T(8,128)(2,1)}, u32[]{:S(2)}, u32[]{:S(2)}) collective-permute-start(bf16[144,2048]{1,0:T(8,128)(2,1)S(1)} %fusion.9), channel_id=1, source_target_pairs={{0,8},{2,10},{4,12},{6,14},{8,0},{10,2},{12,4},{14,6},{16,24},{18,... | collective-permute-start | bytes 1769480 | tf_op jit(solution)/shard_map/ppermute | solution.py:55
  34.1 17.4 %collective-permute-start.8 = (bf16[144,2048]{1,0:T(8,128)(2,1)S(1)}, bf16[144,2048]{1,0:T(8,128)(2,1)}, u32[]{:S(2)}, u32[]{:S(2)}) collective-permute-start(bf16[144,2048]{1,0:T(8,128)(2,1)S(1)} %fusion.9), channel_id=1, source_target_pairs={{0,2},{2,0},{4,6},{6,4},{8,10},{10,8},{12,14},{14,12},{16,18},{18,... | collective-permute-start | bytes 1769480 | tf_op jit(solution)/shard_map/ppermute | solution.py:55
  34.6 16.0 %collective-permute-start.7 = (bf16[256,512]{1,0:T(8,128)(2,1)S(1)}, bf16[256,512]{1,0:T(8,128)(2,1)S(1)}, u32[]{:S(2)}, u32[]{:S(2)}) collective-permute-start(bf16[256,512]{1,0:T(8,128)(2,1)S(1)} %bitcast.462), channel_id=1, source_target_pairs={{0,16},{2,18},{4,20},{6,22},{8,24},{10,26},{12,28},{14,30},{16,0},... | collective-permute-start | bytes 786440 | tf_op jit(solution)/shard_map/ppermute | solution.py:55
  34.6 16.0 %collective-permute-start.5 = (bf16[64,2048]{1,0:T(8,128)(2,1)}, bf16[64,2048]{1,0:T(8,128)(2,1)}, u32[]{:S(2)}, u32[]{:S(2)}) collective-permute-start(bf16[64,2048]{1,0:T(8,128)(2,1)} %collective-permute-done.1), channel_id=1, source_target_pairs={{0,4},{2,6},{4,0},{6,2},{8,12},{10,14},{12,8},{14,10},{16,20},{18,... | collective-permute-start | bytes 786440 | tf_op jit(solution)/shard_map/ppermute | solution.py:55
  71.8 19.6 %collective-permute-start.18 = (bf16[512,2048]{1,0:T(8,128)(2,1)S(1)}, bf16[512,2048]{1,0:T(8,128)(2,1)}, u32[]{:S(2)}, u32[]{:S(2)}) collective-permute-start(bf16[512,2048]{1,0:T(8,128)(2,1)S(1)} %pad_maximum_fusion.1.refs_8_.refs_14_), channel_id=1, source_target_pairs={{0,1},{1,0},{2,3},{3,2},{4,5},{5,4},{6,7},{7,6},{8,9},{9,8},{10,11... | collective-permute-start | bytes 6291464 | tf_op jit(solution)/shard_map/ppermute | solution.py:58
  74.3 17.1 %collective-permute-start.15 = (bf16[128,1536]{1,0:T(8,128)(2,1)}, bf16[128,1536]{1,0:T(8,128)(2,1)S(1)}, u32[]{:S(2)}, u32[]{:S(2)}) collective-permute-start(bf16[128,1536]{1,0:T(8,128)(2,1)} %get-tuple-element.766), channel_id=1, source_target_pairs={{0,8},{2,10},{4,12},{6,14},{8,0},{10,2},{12,4},{14,6},{16,24},{18,... | collective-permute-start | bytes 1179656 | tf_op jit(solution)/shard_map/ppermute | solution.py:55
  75.4 16.0 %collective-permute-start.16 = (bf16[2,1,64,2048]{3,2,0,1:T(8,128)(2,1)}, bf16[2,1,64,2048]{3,2,0,1:T(8,128)(2,1)S(1)}, u32[]{:S(2)}, u32[]{:S(2)}) collective-permute-start(bf16[2,1,64,2048]{3,2,0,1:T(8,128)(2,1)} %get-tuple-element.769), channel_id=1, source_target_pairs={{0,2},{2,0},{4,6},{6,4},{8,10},{10,8},{12,14},{14,12},{16,18},{18,... | collective-permute-start | bytes 1572872 | tf_op jit(solution)/shard_map/ppermute | solution.py:55
  92.3 28.0 %collective-permute-start.22 = (bf16[128,2048]{1,0:T(8,128)(2,1)}, bf16[128,2048]{1,0:T(8,128)(2,1)}, u32[]{:S(2)}, u32[]{:S(2)}) collective-permute-start(bf16[128,2048]{1,0:T(8,128)(2,1)} %pad_maximum_fusion.10), channel_id=1, source_target_pairs={{0,16},{2,18},{4,20},{6,22},{8,24},{10,26},{12,28},{14,30},{16,0},... | collective-permute-start | bytes 1572872 | tf_op jit(solution)/shard_map/ppermute | solution.py:55
  95.6 29.0 %collective-permute-start.21 = (bf16[192,2048]{1,0:T(8,128)(2,1)}, bf16[192,2048]{1,0:T(8,128)(2,1)}, u32[]{:S(2)}, u32[]{:S(2)}) collective-permute-start(bf16[192,2048]{1,0:T(8,128)(2,1)} %pad_maximum_fusion.5), channel_id=1, source_target_pairs={{0,4},{2,6},{4,0},{6,2},{8,12},{10,14},{12,8},{14,10},{16,20},{18,... | collective-permute-start | bytes 2359304 | tf_op jit(solution)/shard_map/ppermute | solution.py:55
  98.6 23.2 %collective-permute-start.23 = (bf16[1,2,64,2048]{3,2,1,0:T(8,128)(2,1)}, bf16[1,2,64,2048]{3,2,1,0:T(8,128)(2,1)}, u32[]{:S(2)}, u32[]{:S(2)}) collective-permute-start(bf16[1,2,64,2048]{3,2,1,0:T(8,128)(2,1)} %get-tuple-element.1453), channel_id=1, source_target_pairs={{0,1},{1,0},{2,3},{3,2},{4,5},{5,4},{6,7},{7,6},{8,9},{9,8},{10,11... | collective-permute-start | bytes 1572872 | tf_op jit(solution)/shard_map/ppermute | solution.py:58
  98.7 27.3 %collective-permute-start.20 = (bf16[128,2048]{1,0:T(8,128)(2,1)}, bf16[128,2048]{1,0:T(8,128)(2,1)S(1)}, u32[]{:S(2)}, u32[]{:S(2)}) collective-permute-start(bf16[128,2048]{1,0:T(8,128)(2,1)} %bitcast.521), channel_id=1, source_target_pairs={{0,8},{2,10},{4,12},{6,14},{8,0},{10,2},{12,4},{14,6},{16,24},{18,... | collective-permute-start | bytes 1572872 | tf_op jit(solution)/shard_map/ppermute | solution.py:55
  99.7 26.2 %collective-permute-start.19 = (bf16[128,3584]{1,0:T(8,128)(2,1)}, bf16[128,3584]{1,0:T(8,128)(2,1)S(1)}, u32[]{:S(2)}, u32[]{:S(2)}) collective-permute-start(bf16[128,3584]{1,0:T(8,128)(2,1)} %pad_maximum_fusion.4), channel_id=1, source_target_pairs={{0,2},{2,0},{4,6},{6,4},{8,10},{10,8},{12,14},{14,12},{16,18},{18,... | collective-permute-start | bytes 2752520 | tf_op jit(solution)/shard_map/ppermute | solution.py:55
  126.2 15.8 %collective-permute-start.25 = (bf16[256,512]{1,0:T(8,128)(2,1)S(1)}, bf16[256,512]{1,0:T(8,128)(2,1)S(1)}, u32[]{:S(2)}, u32[]{:S(2)}) collective-permute-start(bf16[256,512]{1,0:T(8,128)(2,1)S(1)} %bitcast.463), channel_id=1, source_target_pairs={{0,16},{2,18},{4,20},{6,22},{8,24},{10,26},{12,28},{14,30},{16,0},... | collective-permute-start | bytes 786440 | tf_op jit(solution)/shard_map/ppermute | solution.py:55
  142.0 19.8 %collective-permute-start.28 = (bf16[64,2048]{1,0:T(8,128)(2,1)S(1)}, bf16[64,2048]{1,0:T(8,128)(2,1)S(1)}, u32[]{:S(2)}, u32[]{:S(2)}) collective-permute-start(bf16[64,2048]{1,0:T(8,128)(2,1)S(1)} %get-tuple-element.891), channel_id=1, source_target_pairs={{0,4},{2,6},{4,0},{6,2},{8,12},{10,14},{12,8},{14,10},{16,20},{18,... | collective-permute-start | bytes 786440 | tf_op jit(solution)/shard_map/ppermute | solution.py:55
  142.5 19.2 %collective-permute-start.30 = (bf16[256,512]{1,0:T(8,128)(2,1)S(1)}, bf16[256,512]{1,0:T(8,128)(2,1)S(1)}, u32[]{:S(2)}, u32[]{:S(2)}) collective-permute-start(bf16[256,512]{1,0:T(8,128)(2,1)S(1)} %bitcast.465), channel_id=1, source_target_pairs={{0,16},{2,18},{4,20},{6,22},{8,24},{10,26},{12,28},{14,30},{16,0},... | collective-permute-start | bytes 786440 | tf_op jit(solution)/shard_map/ppermute | solution.py:55
  145.2 15.7 %collective-permute-start.29 = (bf16[512,512]{1,0:T(8,128)(2,1)S(1)}, bf16[512,512]{1,0:T(8,128)(2,1)S(1)}, u32[]{:S(2)}, u32[]{:S(2)}) collective-permute-start(bf16[512,512]{1,0:T(8,128)(2,1)S(1)} %pad_maximum_fusion.12), channel_id=1, source_target_pairs={{0,4},{2,6},{4,0},{6,2},{8,12},{10,14},{12,8},{14,10},{16,20},{18,... | collective-permute-start | bytes 1572872 | tf_op jit(solution)/shard_map/ppermute | solution.py:55
  146.5 17.1 %collective-permute-start.27 = (bf16[128,2048]{1,0:T(8,128)(2,1)S(1)}, bf16[128,2048]{1,0:T(8,128)(2,1)S(1)}, u32[]{:S(2)}, u32[]{:S(2)}) collective-permute-start(bf16[128,2048]{1,0:T(8,128)(2,1)S(1)} %slice.354), channel_id=1, source_target_pairs={{0,8},{2,10},{4,12},{6,14},{8,0},{10,2},{12,4},{14,6},{16,24},{18,... | collective-permute-start | bytes 1572872 | tf_op jit(solution)/shard_map/ppermute | solution.py:55
  147.5 16.1 %collective-permute-start.31 = (bf16[128,2048]{1,0:T(8,128)(2,1)S(1)}, bf16[128,2048]{1,0:T(8,128)(2,1)S(1)}, u32[]{:S(2)}, u32[]{:S(2)}) collective-permute-start(bf16[128,2048]{1,0:T(8,128)(2,1)S(1)} %get-tuple-element.1419), channel_id=1, source_target_pairs={{0,2},{2,0},{4,6},{6,4},{8,10},{10,8},{12,14},{14,12},{16,18},{18,... | collective-permute-start | bytes 1572872 | tf_op jit(solution)/shard_map/ppermute | solution.py:55
  165.5 16.9 %collective-permute-start.36 = (bf16[128,2048]{1,0:T(8,128)(2,1)S(1)}, bf16[128,2048]{1,0:T(8,128)(2,1)S(1)}, u32[]{:S(2)}, u32[]{:S(2)}) collective-permute-start(bf16[128,2048]{1,0:T(8,128)(2,1)S(1)} %add_convert_fusion.4), channel_id=1, source_target_pairs={{0,8},{2,10},{4,12},{6,14},{8,0},{10,2},{12,4},{14,6},{16,24},{18,... | collective-permute-start | bytes 1572872 | tf_op jit(solution)/shard_map/ppermute | solution.py:55
  182.4 21.0 %collective-permute-start.37 = (bf16[2,1,192,2048]{3,2,0,1:T(8,128)(2,1)S(1)}, bf16[2,1,192,2048]{3,2,0,1:T(8,128)(2,1)S(1)}, u32[]{:S(2)}, u32[]{:S(2)}) collective-permute-start(bf16[2,1,192,2048]{3,2,0,1:T(8,128)(2,1)S(1)} %get-tuple-element.922), channel_id=1, source_target_pairs={{0,1},{1,0},{2,3},{3,2},{4,5},{5,4},{6,7},{7,6},{8,9},{9,8},{10,11... | collective-permute-start | bytes 4718600 | tf_op jit(solution)/shard_map/ppermute | solution.py:58
  183.9 19.5 %collective-permute-start.41 = (bf16[128,2048]{1,0:T(8,128)(2,1)S(1)}, bf16[128,2048]{1,0:T(8,128)(2,1)S(1)}, u32[]{:S(2)}, u32[]{:S(2)}) collective-permute-start(bf16[128,2048]{1,0:T(8,128)(2,1)S(1)} %multiply_convert_fusion), channel_id=1, source_target_pairs={{0,8},{2,10},{4,12},{6,14},{8,0},{10,2},{12,4},{14,6},{16,24},{18,... | collective-permute-start | bytes 1572872 | tf_op jit(solution)/shard_map/ppermute | solution.py:55
  184.7 18.7 %collective-permute-start.40 = (bf16[128,2048]{1,0:T(8,128)(2,1)S(1)}, bf16[128,2048]{1,0:T(8,128)(2,1)S(1)}, u32[]{:S(2)}, u32[]{:S(2)}) collective-permute-start(bf16[128,2048]{1,0:T(8,128)(2,1)S(1)} %multiply_convert_fusion), channel_id=1, source_target_pairs={{0,2},{2,0},{4,6},{6,4},{8,10},{10,8},{12,14},{14,12},{16,18},{18,... | collective-permute-start | bytes 1572872 | tf_op jit(solution)/shard_map/ppermute | solution.py:55
  222.7 17.5 %collective-permute-start.47 = (bf16[512,2048]{1,0:T(8,128)(2,1)}, bf16[512,2048]{1,0:T(8,128)(2,1)}, u32[]{:S(2)}, u32[]{:S(2)}) collective-permute-start(bf16[512,2048]{1,0:T(8,128)(2,1)} %constant_dynamic-update-slice_fusion.4.refs_8_), channel_id=1, source_target_pairs={{0,1},{1,0},{2,3},{3,2},{4,5},{5,4},{6,7},{7,6},{8,9},{9,8},{10,11... | collective-permute-start | bytes 6291464 | tf_op jit(solution)/shard_map/ppermute | solution.py:58
  255.7 17.2 %collective-permute-start.49 = (bf16[512,512]{1,0:T(8,128)(2,1)S(1)}, bf16[512,512]{1,0:T(8,128)(2,1)S(1)}, u32[]{:S(2)}, u32[]{:S(2)}) collective-permute-start(bf16[512,512]{1,0:T(8,128)(2,1)S(1)} %bitcast.516), channel_id=1, source_target_pairs={{0,4},{2,6},{4,0},{6,2},{8,12},{10,14},{12,8},{14,10},{16,20},{18,... | collective-permute-start | bytes 1572872 | tf_op jit(solution)/shard_map/ppermute | solution.py:55
  273.2 16.3 %collective-permute-start.51 = (bf16[512,512]{1,0:T(8,128)(2,1)S(1)}, bf16[512,512]{1,0:T(8,128)(2,1)S(1)}, u32[]{:S(2)}, u32[]{:S(2)}) collective-permute-start(bf16[512,512]{1,0:T(8,128)(2,1)S(1)} %bitcast.515), channel_id=1, source_target_pairs={{0,4},{2,6},{4,0},{6,2},{8,12},{10,14},{12,8},{14,10},{16,20},{18,... | collective-permute-start | bytes 1572872 | tf_op jit(solution)/shard_map/ppermute | solution.py:55
  273.8 16.0 %collective-permute-start.50 = (bf16[256,512]{1,0:T(8,128)(2,1)S(1)}, bf16[256,512]{1,0:T(8,128)(2,1)S(1)}, u32[]{:S(2)}, u32[]{:S(2)}) collective-permute-start(bf16[256,512]{1,0:T(8,128)(2,1)S(1)} %bitcast.563), channel_id=1, source_target_pairs={{0,16},{2,18},{4,20},{6,22},{8,24},{10,26},{12,28},{14,30},{16,0},... | collective-permute-start | bytes 786440 | tf_op jit(solution)/shard_map/ppermute | solution.py:55
  289.8 15.9 %collective-permute-start.54 = (bf16[512,2048]{1,0:T(8,128)(2,1)S(1)}, bf16[512,2048]{1,0:T(8,128)(2,1)S(1)}, u32[]{:S(2)}, u32[]{:S(2)}) collective-permute-start(bf16[512,2048]{1,0:T(8,128)(2,1)S(1)} %get-tuple-element.1146), channel_id=1, source_target_pairs={{0,1},{1,0},{2,3},{3,2},{4,5},{5,4},{6,7},{7,6},{8,9},{9,8},{10,11... | collective-permute-start | bytes 6291464 | tf_op jit(solution)/shard_map/ppermute | solution.py:58
  289.9 16.7 %collective-permute-start.52 = (bf16[256,512]{1,0:T(8,128)(2,1)S(1)}, bf16[256,512]{1,0:T(8,128)(2,1)S(1)}, u32[]{:S(2)}, u32[]{:S(2)}) collective-permute-start(bf16[256,512]{1,0:T(8,128)(2,1)S(1)} %bitcast.564), channel_id=1, source_target_pairs={{0,16},{2,18},{4,20},{6,22},{8,24},{10,26},{12,28},{14,30},{16,0},... | collective-permute-start | bytes 786440 | tf_op jit(solution)/shard_map/ppermute | solution.py:55
  326.7 16.5 %collective-permute-start.62 = (bf16[128,2048]{1,0:T(8,128)(2,1)S(1)}, bf16[128,2048]{1,0:T(8,128)(2,1)S(1)}, u32[]{:S(2)}, u32[]{:S(2)}) collective-permute-start(bf16[128,2048]{1,0:T(8,128)(2,1)S(1)} %add_convert_fusion.3), channel_id=1, source_target_pairs={{0,8},{2,10},{4,12},{6,14},{8,0},{10,2},{12,4},{14,6},{16,24},{18,... | collective-permute-start | bytes 1572872 | tf_op jit(solution)/shard_map/ppermute | solution.py:55
  347.0 16.6 %collective-permute-start.64 = (bf16[128,2048]{1,0:T(8,128)(2,1)S(1)}, bf16[128,2048]{1,0:T(8,128)(2,1)S(1)}, u32[]{:S(2)}, u32[]{:S(2)}) collective-permute-start(bf16[128,2048]{1,0:T(8,128)(2,1)S(1)} %get-tuple-element.1252), channel_id=1, source_target_pairs={{0,8},{2,10},{4,12},{6,14},{8,0},{10,2},{12,4},{14,6},{16,24},{18,... | collective-permute-start | bytes 1572872 | tf_op jit(solution)/shard_map/ppermute | solution.py:55
  347.0 16.6 %collective-permute-start.63 = (bf16[128,2048]{1,0:T(8,128)(2,1)S(1)}, bf16[128,2048]{1,0:T(8,128)(2,1)S(1)}, u32[]{:S(2)}, u32[]{:S(2)}) collective-permute-start(bf16[128,2048]{1,0:T(8,128)(2,1)S(1)} %get-tuple-element.1252), channel_id=1, source_target_pairs={{0,2},{2,0},{4,6},{6,4},{8,10},{10,8},{12,14},{14,12},{16,18},{18,... | collective-permute-start | bytes 1572872 | tf_op jit(solution)/shard_map/ppermute | solution.py:55
  365.3 16.9 %collective-permute-start.70 = (bf16[512,2048]{1,0:T(8,128)(2,1)}, bf16[512,2048]{1,0:T(8,128)(2,1)S(1)}, u32[]{:S(2)}, u32[]{:S(2)}) collective-permute-start(bf16[512,2048]{1,0:T(8,128)(2,1)} %get-tuple-element.1241), channel_id=1, source_target_pairs={{0,1},{1,0},{2,3},{3,2},{4,5},{5,4},{6,7},{7,6},{8,9},{9,8},{10,11... | collective-permute-start | bytes 6291464 | tf_op jit(solution)/shard_map/ppermute | solution.py:58
  365.6 19.4 %collective-permute-start.69 = (bf16[256,512]{1,0:T(8,128)(2,1)}, bf16[256,512]{1,0:T(8,128)(2,1)S(1)}, u32[]{:S(2)}, u32[]{:S(2)}) collective-permute-start(bf16[256,512]{1,0:T(8,128)(2,1)} %bitcast.561), channel_id=1, source_target_pairs={{0,16},{2,18},{4,20},{6,22},{8,24},{10,26},{12,28},{14,30},{16,0},... | collective-permute-start | bytes 786440 | tf_op jit(solution)/shard_map/ppermute | solution.py:55
  366.8 18.2 %collective-permute-start.68 = (bf16[128,2048]{1,0:T(8,128)(2,1)}, bf16[128,2048]{1,0:T(8,128)(2,1)S(1)}, u32[]{:S(2)}, u32[]{:S(2)}) collective-permute-start(bf16[128,2048]{1,0:T(8,128)(2,1)} %copy-done.107), channel_id=1, source_target_pairs={{0,2},{2,0},{4,6},{6,4},{8,10},{10,8},{12,14},{14,12},{16,18},{18,... | collective-permute-start | bytes 1572872 | tf_op jit(solution)/shard_map/ppermute | solution.py:55
  400.6 24.2 %collective-permute-start.76 = (bf16[128,2048]{1,0:T(8,128)(2,1)S(1)}, bf16[128,2048]{1,0:T(8,128)(2,1)S(1)}, u32[]{:S(2)}, u32[]{:S(2)}) collective-permute-start(bf16[128,2048]{1,0:T(8,128)(2,1)S(1)} %bitcast.544), channel_id=1, source_target_pairs={{0,4},{2,6},{4,0},{6,2},{8,12},{10,14},{12,8},{14,10},{16,20},{18,... | collective-permute-start | bytes 1572872 | tf_op jit(solution)/shard_map/ppermute | solution.py:55
  402.3 24.6 %collective-permute-start.75 = (bf16[64,2048]{1,0:T(8,128)(2,1)S(1)}, bf16[64,2048]{1,0:T(8,128)(2,1)S(1)}, u32[]{:S(2)}, u32[]{:S(2)}) collective-permute-start(bf16[64,2048]{1,0:T(8,128)(2,1)S(1)} %fusion.19), channel_id=1, source_target_pairs={{0,16},{2,18},{4,20},{6,22},{8,24},{10,26},{12,28},{14,30},{16,0},... | collective-permute-start | bytes 786440 | tf_op jit(solution)/shard_map/ppermute | solution.py:55
  404.0 22.9 %collective-permute-start.77 = (bf16[128,1536]{1,0:T(8,128)(2,1)S(1)}, bf16[128,1536]{1,0:T(8,128)(2,1)S(1)}, u32[]{:S(2)}, u32[]{:S(2)}) collective-permute-start(bf16[128,1536]{1,0:T(8,128)(2,1)S(1)} %pad_maximum_fusion.20), channel_id=1, source_target_pairs={{0,10},{2,8},{4,14},{6,12},{8,2},{10,0},{12,6},{14,4},{16,26},{18,... | collective-permute-start | bytes 1179656 | tf_op jit(solution)/shard_map/ppermute | solution.py:55
  405.6 21.3 %collective-permute-start.78 = (bf16[128,1536]{1,0:T(8,128)(2,1)S(1)}, bf16[128,1536]{1,0:T(8,128)(2,1)S(1)}, u32[]{:S(2)}, u32[]{:S(2)}) collective-permute-start(bf16[128,1536]{1,0:T(8,128)(2,1)S(1)} %pad_maximum_fusion.21), channel_id=1, source_target_pairs={{0,2},{2,0},{4,6},{6,4},{8,10},{10,8},{12,14},{14,12},{16,18},{18,... | collective-permute-start | bytes 1179656 | tf_op jit(solution)/shard_map/ppermute | solution.py:55
  406.1 20.9 %collective-permute-start.79 = (bf16[128,1536]{1,0:T(8,128)(2,1)S(1)}, bf16[128,1536]{1,0:T(8,128)(2,1)S(1)}, u32[]{:S(2)}, u32[]{:S(2)}) collective-permute-start(bf16[128,1536]{1,0:T(8,128)(2,1)S(1)} %pad_maximum_fusion.22), channel_id=1, source_target_pairs={{0,8},{2,10},{4,12},{6,14},{8,0},{10,2},{12,4},{14,6},{16,24},{18,... | collective-permute-start | bytes 1179656 | tf_op jit(solution)/shard_map/ppermute | solution.py:55
  427.6 15.9 %collective-permute-start.84 = (bf16[512,2048]{1,0:T(8,128)(2,1)}, bf16[512,2048]{1,0:T(8,128)(2,1)}, u32[]{:S(2)}, u32[]{:S(2)}) collective-permute-start(bf16[512,2048]{1,0:T(8,128)(2,1)} %get-tuple-element.1321), channel_id=1, source_target_pairs={{0,1},{1,0},{2,3},{3,2},{4,5},{5,4},{6,7},{7,6},{8,9},{9,8},{10,11... | collective-permute-start | bytes 6291464 | tf_op jit(solution)/shard_map/ppermute | solution.py:58
  428.9 17.2 %collective-permute-start.80 = (bf16[64,2048]{1,0:T(8,128)(2,1)S(1)}, bf16[64,2048]{1,0:T(8,128)(2,1)S(1)}, u32[]{:S(2)}, u32[]{:S(2)}) collective-permute-start(bf16[64,2048]{1,0:T(8,128)(2,1)S(1)} %fusion.20), channel_id=1, source_target_pairs={{0,16},{2,18},{4,20},{6,22},{8,24},{10,26},{12,28},{14,30},{16,0},... | collective-permute-start | bytes 786440 | tf_op jit(solution)/shard_map/ppermute | solution.py:55
  431.7 19.2 %collective-permute-start.83 = (bf16[128,2048]{1,0:T(8,128)(2,1)S(1)}, bf16[128,2048]{1,0:T(8,128)(2,1)S(1)}, u32[]{:S(2)}, u32[]{:S(2)}) collective-permute-start(bf16[128,2048]{1,0:T(8,128)(2,1)S(1)} %add_convert_fusion.2), channel_id=1, source_target_pairs={{0,8},{2,10},{4,12},{6,14},{8,0},{10,2},{12,4},{14,6},{16,24},{18,... | collective-permute-start | bytes 1572872 | tf_op jit(solution)/shard_map/ppermute | solution.py:55
  433.1 17.9 %collective-permute-start.82 = (bf16[1,128,2048]{2,1,0:T(8,128)(2,1)S(1)}, bf16[1,128,2048]{2,1,0:T(8,128)(2,1)S(1)}, u32[]{:S(2)}, u32[]{:S(2)}) collective-permute-start(bf16[1,128,2048]{2,1,0:T(8,128)(2,1)S(1)} %copy-done.113), channel_id=1, source_target_pairs={{0,2},{2,0},{4,6},{6,4},{8,10},{10,8},{12,14},{14,12},{16,18},{18,... | collective-permute-start | bytes 1572872 | tf_op jit(solution)/shard_map/ppermute | solution.py:55
  471.6 18.9 %collective-permute-start.96 = (bf16[128,2048]{1,0:T(8,128)(2,1)S(1)}, bf16[128,2048]{1,0:T(8,128)(2,1)S(1)}, u32[]{:S(2)}, u32[]{:S(2)}) collective-permute-start(bf16[128,2048]{1,0:T(8,128)(2,1)S(1)} %add_convert_fusion.1), channel_id=1, source_target_pairs={{0,8},{2,10},{4,12},{6,14},{8,0},{10,2},{12,4},{14,6},{16,24},{18,... | collective-permute-start | bytes 1572872 | tf_op jit(solution)/shard_map/ppermute | solution.py:55
  473.9 16.7 %collective-permute-start.93 = (bf16[4,128,1536]{2,1,0:T(8,128)(2,1)S(1)}, bf16[4,128,1536]{2,1,0:T(8,128)(2,1)S(1)}, u32[]{:S(2)}, u32[]{:S(2)}) collective-permute-start(bf16[4,128,1536]{2,1,0:T(8,128)(2,1)S(1)} %pad_maximum_fusion.3), channel_id=1, source_target_pairs={{0,1},{1,0},{2,3},{3,2},{4,5},{5,4},{6,7},{7,6},{8,9},{9,8},{10,11... | collective-permute-start | bytes 4718600 | tf_op jit(solution)/shard_map/ppermute | solution.py:58
  474.1 16.4 %collective-permute-start.95 = (bf16[128,2048]{1,0:T(8,128)(2,1)S(1)}, bf16[128,2048]{1,0:T(8,128)(2,1)S(1)}, u32[]{:S(2)}, u32[]{:S(2)}) collective-permute-start(bf16[128,2048]{1,0:T(8,128)(2,1)S(1)} %get-tuple-element.1361), channel_id=1, source_target_pairs={{0,2},{2,0},{4,6},{6,4},{8,10},{10,8},{12,14},{14,12},{16,18},{18,... | collective-permute-start | bytes 1572872 | tf_op jit(solution)/shard_map/ppermute | solution.py:55
  495.8 16.9 %collective-permute-start.98 = (bf16[128,2048]{1,0:T(8,128)(2,1)S(1)}, bf16[128,2048]{1,0:T(8,128)(2,1)S(1)}, u32[]{:S(2)}, u32[]{:S(2)}) collective-permute-start(bf16[128,2048]{1,0:T(8,128)(2,1)S(1)} %copy-done.111), channel_id=1, source_target_pairs={{0,2},{2,0},{4,6},{6,4},{8,10},{10,8},{12,14},{14,12},{16,18},{18,... | collective-permute-start | bytes 1572872 | tf_op jit(solution)/shard_map/ppermute | solution.py:55
  (191 other events, 1755.9 us)

commit v4 on v3

--- a/solution.py
+++ b/solution.py
@@ -109,40 +109,49 @@
 LANES = 128
 
 
-def cut_columns(sources, pieces):
+def cut_columns(sources, pieces, tail):
     rows = sources[0].shape[0]
     cuts = [cut for piece in pieces for cut in piece]
+    widths = [sum(w for _, _, w in piece) for piece in pieces]
+    heights = [rows if rest is None else rows + rest.shape[0] for rest in tail]
     if any(c[2] % LANES for c in cuts) or rows % 16:
-        return [
+        out = [
             jnp.concatenate(
                 [lax.dynamic_slice(sources[k], (0, at), (rows, w)) for k, at, w in piece], axis=1
             )
             for piece in pieces
         ]
+        return [
+            x if rest is None else jnp.concatenate([x, jnp.pad(rest, ((0, 0), (0, w - rest.shape[1])))])
+            for x, rest, w in zip(out, tail, widths)
+        ]
+    (rest,) = {id(x): x for x in tail if x is not None}.values()
 
     def kernel(at_ref, *refs):
-        ins, outs = refs[: len(sources)], refs[len(sources) :]
+        ins, rest_ref, outs = refs[: len(sources)], refs[len(sources)], refs[len(sources) + 1 :]
         j = 0
-        for out, piece in zip(outs, pieces):
+        for out, piece, height in zip(outs, pieces, heights):
             to = 0
             for k, _, w in piece:
                 start = pl.multiple_of(at_ref[j] * LANES, LANES)
-                out[:, to : to + w] = ins[k][:, pl.ds(start, w)]
+                out[:rows, to : to + w] = ins[k][:, pl.ds(start, w)]
                 to += w
                 j += 1
+            if height > rows:
+                out[rows:, :] = jnp.zeros((height - rows, to), out.dtype)
+                out[rows:, : rest.shape[1]] = rest_ref[...]
 
     vmem = pl.BlockSpec(memory_space=pltpu.VMEM)
     return pl.pallas_call(
         kernel,
-        in_specs=[pl.BlockSpec(memory_space=pltpu.SMEM)] + [vmem] * len(sources),
+        in_specs=[pl.BlockSpec(memory_space=pltpu.SMEM)] + [vmem] * (len(sources) + 1),
         out_specs=[vmem] * len(pieces),
         out_shape=[
-            jax.ShapeDtypeStruct((rows, sum(w for _, _, w in piece)), sources[0].dtype)
-            for piece in pieces
+            jax.ShapeDtypeStruct(shape, sources[0].dtype) for shape in zip(heights, widths)
         ],
         compiler_params=pltpu.CompilerParams(vmem_limit_bytes=24 << 20),
         name="cut_columns",
-    )(jnp.stack([jnp.asarray(at // LANES, jnp.int32) for _, at, _ in cuts]), *sources)
+    )(jnp.stack([jnp.asarray(at // LANES, jnp.int32) for _, at, _ in cuts]), *sources, rest)
 
 
 def place_columns(pieces, widths, places):
@@ -227,8 +236,20 @@
     def __init__(self, g, live):
         self.g, self.live = g, live
 
-    def fetch(self, name, parts):
+    def fetch(self, name, parts, whole=None):
         self.live[name] = {(p, 0, 0): x for p, x in enumerate(parts)}
+        if whole is not None:
+            self.live[name + "_whole"] = whole
+
+    def fetch_b_own(self, name):
+        whole = self.live.pop(name + "_whole")
+        own = {p: x for (p, d, e), x in self.live[name].items() if d == e == 0}
+        for e in range(1, self.g.B):
+            got, at = self.g.pb(whole, e), 0
+            for p in sorted(own):
+                rows = own[p].shape[0]
+                self.live[name] = {**self.live[name], (p, 0, e): got[at : at + rows]}
+                at += rows
 
     def fetch_a(self, *jobs):
         for d in range(1, self.g.A):
@@ -667,7 +688,7 @@
     half_d = lax.dynamic_slice(w_d, (g.c * (rows_d // 2), 0), (rows_d // 2, width))
     third = rows_d // 6
     seg_low = segments[0].astype(BF16)[None]
-    seg_low = jnp.pad(seg_low, ((0, 15), (0, width - seq_len)))
+    seg_low = jnp.pad(seg_low, ((0, 15), (0, 0)))
     qkv_cuts, gu_cuts = [], []
     for dt, du in ORDER:
         t, u = g.t ^ dt, g.u ^ du
@@ -683,11 +704,11 @@
         )
     cuts = [qkv_cuts[0], qkv_cuts[1], qkv_cuts[2] + gu_cuts[2], qkv_cuts[3]]
     cuts += [gu_cuts[0], gu_cuts[3] + gu_cuts[1]]
-    cut = cut_columns([w_g, w_u, w_q, w_k, w_v], cuts)
+    cut = cut_columns([w_g, w_u, w_q, w_k, w_v], cuts, [seg_low] * 4 + [None] * 2)
     L = Live(qkv=cut[:4])
     S = Shards(g, L)
     S.fetch("o", [half_o])
-    S.fetch("d", [half_d[k * third : (k + 1) * third] for k in range(3)])
+    S.fetch("d", [half_d[k * third : (k + 1) * third] for k in range(3)], half_d)
 
     def done(*floating):
         new = lax.optimization_barrier({k: v for k, v in L.items() if k not in floating})
@@ -701,13 +722,14 @@
     L.qkv = chips_swap(g, L.qkv)
     S.fetch_a(("o", 0))
     S.fetch_b(("o", 0, False))
-    L.xn, L.cot = jnp.concatenate([xn_own, seg_low]), cotangent[0]
+    L.xn, L.cot = xn_own, cotangent[0]
     L.gu, L.gu_t, L.gu_f = cut[4], cut[5][:, : 2 * units], cut[5][:, 2 * units :]
     done()
 
     L.xn = gather_one(g, L.xn)
-    L.gu_u = L.qkv[2][:, 4 * HD :]
-    L.qkv[2] = L.qkv[2][:, : 4 * HD]
+    L.gu_u = L.qkv[2][:rows_in, 4 * HD :]
+    L.seg = [x[rows_in, :seq_len] for x in L.qkv]
+    L.qkv = [x[:rows_in, : 4 * HD] for x in L.qkv]
     S.fetch("qkv", pairs(L.qkv))
     S.fetch_a(("qkv", 0))
     S.fetch_b(("qkv", 0, False), ("qkv", 1, False), ("o", 0, True))
@@ -720,8 +742,7 @@
     L.o = (pick(o_blocks, g.u), pick(o_blocks, 1 - g.u))
     done()
 
-    near = jnp.concatenate([x[:span] for x in L.xn])
-    L.seg = [x[span, :seq_len] for x in L.xn]
+    near = jnp.concatenate(L.xn)
     L.xn = (near, g.pc(near))
     L.gu_t = g.pt(L.gu_t, 1, 0)
     joined = rows_in == span
@@ -764,7 +785,7 @@
     L.gu = [L.gu, L.gu_f, L.gu_u, L.gu_t]
     del L["gu_t"], L["gu_u"], L["gu_f"]
     S.fetch_a(("d", 1), ("d", 2))
-    S.fetch_b(("d", 0, False), ("d", 1, False), ("d", 2, False))
+    S.fetch_b_own("d")
     o_mine, o_next = L.o
     o_pair = jnp.where(g.u == 0, jnp.stack([o_mine, o_next]), jnp.stack([o_next, o_mine]))
     o_pair = o_pair.transpose(1, 2, 0, 3, 4)
@@ -777,7 +798,8 @@
 
     L.part = core_sum(*L.part)
     for k in range(PARTS):
-        S.fetch(f"gu{k + 1}", pairs([x[:, 2 * pw * k : 2 * pw * (k + 1)] for x in L.gu]))
+        pieces = [x[:, 2 * pw * k : 2 * pw * (k + 1)] for x in L.gu]
+        S.fetch(f"gu{k + 1}", pairs(pieces), jnp.stack(pieces))
     del L["gu"]
     S.fetch_a(("gu1", 0))
     S.fetch_b(("d", 0, True), ("d", 1, True))
@@ -785,7 +807,8 @@
 
     L.part = scatter_one(g, chip_blocks(L.part))
     S.fetch_a(("gu1", 1))
-    S.fetch_b(("d", 2, True), ("gu1", 0, False), ("gu1", 1, False))
+    S.fetch_b(("d", 2, True))
+    S.fetch_b_own("gu1")
     L.cot = gather_two_along_t(g, L.cot)
     done()
     L.part = scatter_two(g, L.part)
@@ -801,7 +824,7 @@
     xn2_own, post_back = jax.vjp(rms_scale, mid, g_post)
     L.xn2 = gather_one(g, xn2_own.astype(BF16))
     S.fetch_a(("gu2", 1))
-    S.fetch_b(("gu2", 0, False), ("gu2", 1, False))
+    S.fetch_b_own("gu2")
     L.d = (L.d[0], g.pc(L.d[1]))
     done()
     L.xn2 = gather_two(g, L.xn2)
@@ -814,7 +837,7 @@
     near = jnp.concatenate(L.xn2)
     L.xn2 = (near, g.pc(near))
     S.fetch_a(("gu3", 1))
-    S.fetch_b(("gu3", 0, False), ("gu3", 1, False))
+    S.fetch_b_own("gu3")
     done()
     w_d_all = L.w_d_all
 

time: 527 us -> 525 us (level)
    unnamed x271 -> x300, local copies, waits for them, and re-layouts: 24.6 us -> 26.3 us
  transfers between devices with their start and end apart: 107 -> 107, of which waited for: 42 -> 42; matrix products, arithmetic and copies ran while one was open for 13% -> 12% of each run, Pallas kernels for 15% -> 15%
where the time goes in v4:
time: 525 us; the launch traced here: 517 us
  waiting for transfers between devices  222 us (42%)
  starting transfers between devices  105 us (20%)
  Pallas kernels  80.6 us (15%)
  local copies, waits for them, and re-layouts  64.2 us (12%)
  other arithmetic  41 us (8%)
    ppermute x90, waiting for transfers between devices, px(): return lax.ppermute(x, 'fsdp', [(i, i ^ mask) for i in range(self.n)])  222 us
    ppermute x90, starting transfers between devices, px(): return lax.ppermute(x, 'fsdp', [(i, i ^ mask) for i in range(self.n)])  104 us
    pallas_call x7, Pallas kernels, kernel_call(): pl.pallas_call(kernel, in_specs=[smem if x.dtype == jnp.int32 else vmem f...  73.9 us
    unnamed x300, local copies, waits for them, and re-layouts  26.3 us
  transfers between devices with their start and end apart: 107, of which 42 were waited for; matrix products, arithmetic and copies ran while one was open for 12% of the time, Pallas kernels for 15%

profile of v4, /device:TPU:0, one launch (start us, length us, event | category | flops | bytes accessed | tf_op | source)
XLA Modules:
  0.0 517.4 jit_solution(12694495527256344679)
XLA Ops:
  12.2 4.1 collective-permute-start.1
  17.9 2.5 collective-permute-start.2
  22.6 7.4 %collective-permute-done.2 = bf16[144,512]{1,0:T(8,128)(2,1)S(1)} collective-permute-done((bf16[144,512]{1,0:T(8,128)(2,1)S(1)}, bf16[144,512]{1,0:T(8,128)(2,1)S(1)}, u32[]{:S(2)}, u32[]{:S(2)}) %collective-permute-start.2) | collective-permute-done | bytes 147488 | tf_op jit(solution)/shard_map/ppermute | solution.py:55
  31.5 5.0 collective-permute-done.3
  37.3 3.1 collective-permute-start.9
  45.3 6.4 %collective-permute-done.6 = bf16[512,512]{1,0:T(8,128)(2,1)S(1)} collective-permute-done((bf16[512,512]{1,0:T(8,128)(2,1)S(1)}, bf16[512,512]{1,0:T(8,128)(2,1)S(1)}, u32[]{:S(2)}, u32[]{:S(2)}) %collective-permute-start.6) | collective-permute-done | bytes 524320 | tf_op jit(solution)/shard_map/ppermute | solution.py:55
  52.5 3.2 collective-permute-done.7
  56.4 2.8 collective-permute-start.12
  62.6 6.5 %collective-permute-done.12 = bf16[256,512]{1,0:T(8,128)(2,1)} collective-permute-done((bf16[256,512]{1,0:T(8,128)(2,1)S(1)}, bf16[256,512]{1,0:T(8,128)(2,1)}, u32[]{:S(2)}, u32[]{:S(2)}) %collective-permute-start.12) | collective-permute-done | bytes 262176 | tf_op jit(solution)/shard_map/ppermute | solution.py:55
  69.0 4.1 collective-permute-done.10
  84.0 6.7 %collective-permute-done.14 = bf16[64,2048]{1,0:T(8,128)(2,1)S(1)} collective-permute-done((bf16[64,2048]{1,0:T(8,128)(2,1)}, bf16[64,2048]{1,0:T(8,128)(2,1)S(1)}, u32[]{:S(2)}, u32[]{:S(2)}) %collective-permute-start.14) | collective-permute-done | bytes 262176 | tf_op jit(solution)/shard_map/ppermute | solution.py:55
  105.7 10.2 %attend.1 = (bf16[2048,512]{1,0:T(8,128)(2,1)S(1)}, f32[1024,384]{1,0:T(8,128)S(1)}, bf16[4,256,256]{2,1,0:T(8,128)(2,1)S(1)}, bf16[4,256,128]{2,1,0:T(8,128)(2,...) custom-call(s32[16]{0:T(128)S(1)} %stack.700.rows_ref, ...), custom_call_target="tpu_custom_call" | custom-call | flops 1048576 | bytes 65536 | tf_op jit(solution)/shard_map/attend/pallas_call | solution.py:359
  128.9 11.6 %collective-permute-done.24 = bf16[128,2048]{1,0:T(8,128)(2,1)S(1)} collective-permute-done((bf16[128,2048]{1,0:T(8,128)(2,1)S(1)}, bf16[128,2048]{1,0:T(8,128)(2,1)S(1)}, u32[]{:S(2)}, u32[]{:S(2)}) %collective-permute-start.24) | collective-permute-done | bytes 524320 | tf_op jit(solution)/shard_map/ppermute | solution.py:55
  147.5 15.0 %collective-permute-done.29 = bf16[4,128,512]{2,1,0:T(8,128)(2,1)S(1)} collective-permute-done((bf16[4,128,512]{2,1,0:T(8,128)(2,1)S(1)}, bf16[4,128,512]{2,1,0:T(8,128)(2,1)S(1)}, u32[]{:S(2)}, u32[]{:S(2)}) %collective-permute-start.29) | collective-permute-done | bytes 524320 | tf_op jit(solution)/shard_map/ppermute | solution.py:55
  171.2 5.2 %collective-permute-done.33 = bf16[512,512]{1,0:T(8,128)(2,1)S(1)} collective-permute-done((bf16[512,512]{1,0:T(8,128)(2,1)S(1)}, bf16[512,512]{1,0:T(8,128)(2,1)S(1)}, u32[]{:S(2)}, u32[]{:S(2)}) %collective-permute-start.33) | collective-permute-done | bytes 524320 | tf_op jit(solution)/shard_map/ppermute | solution.py:55
  177.3 5.4 %collective-permute-done.36 = bf16[128,2048]{1,0:T(8,128)(2,1)S(1)} collective-permute-done((bf16[128,2048]{1,0:T(8,128)(2,1)S(1)}, bf16[128,2048]{1,0:T(8,128)(2,1)S(1)}, u32[]{:S(2)}, u32[]{:S(2)}) %collective-permute-start.36) | collective-permute-done | bytes 524320 | tf_op jit(solution)/shard_map/ppermute | solution.py:55
  185.7 2.7 collective-permute-start.39
  188.4 8.7 %collective-permute-done.38 = bf16[4,128,512]{2,1,0:T(8,128)(2,1)S(1)} collective-permute-done((bf16[4,128,512]{2,1,0:T(8,128)(2,1)S(1)}, bf16[4,128,512]{2,1,0:T(8,128)(2,1)S(1)}, u32[]{:S(2)}, u32[]{:S(2)}) %collective-permute-start.38) | collective-permute-done | bytes 524320 | tf_op jit(solution)/shard_map/ppermute | solution.py:55
  198.0 4.2 collective-permute-done.39
  208.5 9.1 %collective-permute-done.42 = bf16[512,512]{1,0:T(8,128)(2,1)S(1)} collective-permute-done((bf16[512,512]{1,0:T(8,128)(2,1)S(1)}, bf16[512,512]{1,0:T(8,128)(2,1)S(1)}, u32[]{:S(2)}, u32[]{:S(2)}) %collective-permute-start.42) | collective-permute-done | bytes 524320 | tf_op jit(solution)/shard_map/ppermute | solution.py:55
  225.5 12.0 %collective-permute-done.45 = bf16[4,128,512]{2,1,0:T(8,128)(2,1)} collective-permute-done((bf16[4,128,512]{2,1,0:T(8,128)(2,1)}, bf16[4,128,512]{2,1,0:T(8,128)(2,1)}, u32[]{:S(2)}, u32[]{:S(2)}) %collective-permute-start.45) | collective-permute-done | bytes 524320 | tf_op jit(solution)/shard_map/ppermute | solution.py:55
  243.1 11.6 %feed.3 = (bf16[1024,256]{1,0:T(8,128)(2,1)S(1)}, bf16[256,2048]{1,0:T(8,128)(2,1)S(1)}, bf16[2,2,128,512]{3,2,1,0:T(8,128)(2,1)S(1)}, bf16[2,2,128,512]{3,2,1,0...) custom-call(s32[16]{0:T(128)S(1)} %stack.700.rows_ref, ...), custom_call_target="tpu_custom_call" | custom-call | flops 1048576 | bytes 65536 | tf_op jit(solution)/shard_map/feed/pallas_call | solution.py:359
  255.8 15.5 %feed.4 = (bf16[1024,256]{1,0:T(8,128)(2,1)S(1)}, bf16[256,2048]{1,0:T(8,128)(2,1)S(1)}, bf16[2,2,128,512]{3,2,1,0:T(8,128)(2,1)S(1)}, bf16[2,2,128,512]{3,2,1,0...) custom-call(s32[16]{0:T(128)S(1)} %stack.700.rows_ref, ...), custom_call_target="tpu_custom_call" | custom-call | flops 1048576 | bytes 65536 | tf_op jit(solution)/shard_map/feed/pallas_call | solution.py:359
  273.5 14.4 %feed.5 = (bf16[1024,256]{1,0:T(8,128)(2,1)S(1)}, bf16[256,2048]{1,0:T(8,128)(2,1)S(1)}, bf16[2,2,128,512]{3,2,1,0:T(8,128)(2,1)S(1)}, bf16[2,2,128,512]{3,2,1,0...) custom-call(s32[16]{0:T(128)S(1)} %stack.700.rows_ref, ...), custom_call_target="tpu_custom_call" | custom-call | flops 1048576 | bytes 65536 | tf_op jit(solution)/shard_map/feed/pallas_call | solution.py:359
  288.2 2.3 collective-permute-start.52
  292.0 12.6 %collective-permute-done.53 = bf16[512,512]{1,0:T(8,128)(2,1)S(1)} collective-permute-done((bf16[512,512]{1,0:T(8,128)(2,1)S(1)}, bf16[512,512]{1,0:T(8,128)(2,1)S(1)}, u32[]{:S(2)}, u32[]{:S(2)}) %collective-permute-start.53) | collective-permute-done | bytes 524320 | tf_op jit(solution)/shard_map/ppermute | solution.py:55
  310.7 8.6 %collective-permute-done.57 = bf16[512,512]{1,0:T(8,128)(2,1)S(1)} collective-permute-done((bf16[512,512]{1,0:T(8,128)(2,1)S(1)}, bf16[512,512]{1,0:T(8,128)(2,1)S(1)}, u32[]{:S(2)}, u32[]{:S(2)}) %collective-permute-start.57) | collective-permute-done | bytes 524320 | tf_op jit(solution)/shard_map/ppermute | solution.py:55
  330.1 4.8 project_out.3
  337.2 5.4 %collective-permute-done.62 = bf16[128,2048]{1,0:T(8,128)(2,1)S(1)} collective-permute-done((bf16[128,2048]{1,0:T(8,128)(2,1)S(1)}, bf16[128,2048]{1,0:T(8,128)(2,1)S(1)}, u32[]{:S(2)}, u32[]{:S(2)}) %collective-permute-start.62) | collective-permute-done | bytes 524320 | tf_op jit(solution)/shard_map/ppermute | solution.py:55
  346.9 2.8 collective-permute-start.65
  351.3 3.0 collective-permute-done.66
  356.1 3.7 collective-permute-done.65
  366.5 11.7 %collective-permute-done.67 = bf16[128,2048]{1,0:T(8,128)(2,1)} collective-permute-done((bf16[128,2048]{1,0:T(8,128)(2,1)}, bf16[128,2048]{1,0:T(8,128)(2,1)}, u32[]{:S(2)}, u32[]{:S(2)}) %collective-permute-start.67) | collective-permute-done | bytes 524320 | tf_op jit(solution)/shard_map/ppermute | solution.py:55
  380.4 2.8 convert_add_fusion.1
  391.1 6.7 %collective-permute-done.72 = bf16[128,2048]{1,0:T(8,128)(2,1)S(1)} collective-permute-done((bf16[128,2048]{1,0:T(8,128)(2,1)S(1)}, bf16[128,2048]{1,0:T(8,128)(2,1)S(1)}, u32[]{:S(2)}, u32[]{:S(2)}) %collective-permute-start.72) | collective-permute-done | bytes 524320 | tf_op jit(solution)/shard_map/ppermute | solution.py:55
  402.3 2.3 collective-permute-start.77
  405.9 16.1 %attend_back.1 = (f32[512,2048]{1,0:T(8,128)S(1)}, bf16[512,2048]{1,0:T(8,128)(2,1)}, bf16[256,2048]{1,0:T(8,128)(2,1)S(1)}, f32[2,128]{1,0:T(2,128)S(1)}, f32[1...) custom-call(s32[8]{0:T(128)S(1)} %stack.742.rows_out_ref.rows_ref, ...), custom_call_target="tpu_custom_call" | custom-call | flops 1048576 | bytes 65536 | tf_op jit(solution)/shard_map/attend_back/pallas_call | solution.py:359
  433.5 7.1 %collective-permute-done.85 = bf16[512,512]{1,0:T(8,128)(2,1)} collective-permute-done((bf16[512,512]{1,0:T(8,128)(2,1)}, bf16[512,512]{1,0:T(8,128)(2,1)}, u32[]{:S(2)}, u32[]{:S(2)}) %collective-permute-start.85) | collective-permute-done | bytes 524320 | tf_op jit(solution)/shard_map/ppermute | solution.py:55
  441.9 2.5 convert_add_fusion
  444.4 5.3 %collective-permute-done.83 = bf16[128,2048]{1,0:T(8,128)(2,1)S(1)} collective-permute-done((bf16[128,2048]{1,0:T(8,128)(2,1)S(1)}, bf16[128,2048]{1,0:T(8,128)(2,1)S(1)}, u32[]{:S(2)}, u32[]{:S(2)}) %collective-permute-start.83) | collective-permute-done | bytes 524320 | tf_op jit(solution)/shard_map/ppermute | solution.py:55
  455.6 9.2 %collective-permute-done.87 = f32[4352]{0:T(1024)S(1)} collective-permute-done((f32[4352]{0:T(1024)S(1)}, f32[4352]{0:T(1024)S(1)}, u32[]{:S(2)}, u32[]{:S(2)}) %collective-permute-start.87) | collective-permute-done | bytes 17440 | tf_op jit(solution)/shard_map/ppermute | solution.py:55
  465.4 2.6 collective-permute-done.89
  468.0 2.5 collective-permute-start.92
  474.6 9.8 %collective-permute-done.97 = bf16[256,512]{1,0:T(8,128)(2,1)S(1)} collective-permute-done((bf16[256,512]{1,0:T(8,128)(2,1)S(1)}, bf16[256,512]{1,0:T(8,128)(2,1)S(1)}, u32[]{:S(2)}, u32[]{:S(2)}) %collective-permute-start.97) | collective-permute-done | bytes 262176 | tf_op jit(solution)/shard_map/ppermute | solution.py:55
  484.8 4.7 collective-permute-done.96
  496.6 3.8 place_columns.2
  500.4 4.1 collective-permute-done.100.refs_1_
  505.4 3.8 collective-permute-done.106
  (689 shorter events, 197.2 us)
Async XLA Ops:
  12.2 19.2 %collective-permute-start.1 = (bf16[64,2048]{1,0:T(8,128)(2,1)S(1)}, bf16[64,2048]{1,0:T(8,128)(2,1)S(1)}, u32[]{:S(2)}, u32[]{:S(2)}) collective-permute-start(bf16[64,2048]{1,0:T(8,128)(2,1)S(1)} %copy-done.103), channel_id=1, source_target_pairs={{0,16},{2,18},{4,20},{6,22},{8,24},{10,26},{12,28},{14,30},{16,0},... | collective-permute-start | bytes 786440 | tf_op jit(solution)/shard_map/ppermute | solution.py:55
  20.8 15.6 %collective-permute-start.3 = (bf16[144,2048]{1,0:T(8,128)(2,1)S(1)}, bf16[144,2048]{1,0:T(8,128)(2,1)S(1)}, u32[]{:S(2)}, u32[]{:S(2)}) collective-permute-start(bf16[144,2048]{1,0:T(8,128)(2,1)S(1)} %get-tuple-element.742), channel_id=1, source_target_pairs={{0,2},{2,0},{4,6},{6,4},{8,10},{10,8},{12,14},{14,12},{16,18},{18,... | collective-permute-start | bytes 1769480 | tf_op jit(solution)/shard_map/ppermute | solution.py:55
  37.3 19.1 %collective-permute-start.9 = (bf16[128,2048]{1,0:T(8,128)(2,1)S(1)}, bf16[128,2048]{1,0:T(8,128)(2,1)S(1)}, u32[]{:S(2)}, u32[]{:S(2)}) collective-permute-start(bf16[128,2048]{1,0:T(8,128)(2,1)S(1)} %fusion.6), channel_id=1, source_target_pairs={{0,8},{2,10},{4,12},{6,14},{8,0},{10,2},{12,4},{14,6},{16,24},{18,... | collective-permute-start | bytes 1572872 | tf_op jit(solution)/shard_map/ppermute | solution.py:55
  40.4 16.1 %collective-permute-start.8 = (bf16[128,2048]{1,0:T(8,128)(2,1)S(1)}, bf16[128,2048]{1,0:T(8,128)(2,1)S(1)}, u32[]{:S(2)}, u32[]{:S(2)}) collective-permute-start(bf16[128,2048]{1,0:T(8,128)(2,1)S(1)} %fusion.6), channel_id=1, source_target_pairs={{0,2},{2,0},{4,6},{6,4},{8,10},{10,8},{12,14},{14,12},{16,18},{18,... | collective-permute-start | bytes 1572872 | tf_op jit(solution)/shard_map/ppermute | solution.py:55
  74.1 18.8 %collective-permute-start.18 = (bf16[512,2048]{1,0:T(8,128)(2,1)S(1)}, bf16[512,2048]{1,0:T(8,128)(2,1)}, u32[]{:S(2)}, u32[]{:S(2)}) collective-permute-start(bf16[512,2048]{1,0:T(8,128)(2,1)S(1)} %constant_dynamic-update-slice_fusion.refs_8_.refs_14_), channel_id=1, source_target_pairs={{0,1},{1,0},{2,3},{3,2},{4,5},{5,4},{6,7},{7,6},{8,9},{9,8},{10,11... | collective-permute-start | bytes 6291464 | tf_op jit(solution)/shard_map/ppermute | solution.py:58
  76.1 16.8 %collective-permute-start.15 = (bf16[128,1536]{1,0:T(8,128)(2,1)}, bf16[128,1536]{1,0:T(8,128)(2,1)S(1)}, u32[]{:S(2)}, u32[]{:S(2)}) collective-permute-start(bf16[128,1536]{1,0:T(8,128)(2,1)} %get-tuple-element.796), channel_id=1, source_target_pairs={{0,8},{2,10},{4,12},{6,14},{8,0},{10,2},{12,4},{14,6},{16,24},{18,... | collective-permute-start | bytes 1179656 | tf_op jit(solution)/shard_map/ppermute | solution.py:55
  93.8 25.5 %collective-permute-start.22 = (bf16[128,2048]{1,0:T(8,128)(2,1)}, bf16[128,2048]{1,0:T(8,128)(2,1)}, u32[]{:S(2)}, u32[]{:S(2)}) collective-permute-start(bf16[128,2048]{1,0:T(8,128)(2,1)} %pad_maximum_fusion.8), channel_id=1, source_target_pairs={{0,16},{2,18},{4,20},{6,22},{8,24},{10,26},{12,28},{14,30},{16,0},... | collective-permute-start | bytes 1572872 | tf_op jit(solution)/shard_map/ppermute | solution.py:55
  95.0 28.6 %collective-permute-start.21 = (bf16[192,2048]{1,0:T(8,128)(2,1)}, bf16[192,2048]{1,0:T(8,128)(2,1)}, u32[]{:S(2)}, u32[]{:S(2)}) collective-permute-start(bf16[192,2048]{1,0:T(8,128)(2,1)} %dynamic-slice_bitcast_fusion.4), channel_id=1, source_target_pairs={{0,4},{2,6},{4,0},{6,2},{8,12},{10,14},{12,8},{14,10},{16,20},{18,... | collective-permute-start | bytes 2359304 | tf_op jit(solution)/shard_map/ppermute | solution.py:55
  96.6 24.1 %collective-permute-start.23 = (bf16[1,2,64,2048]{3,2,1,0:T(8,128)(2,1)}, bf16[1,2,64,2048]{3,2,1,0:T(8,128)(2,1)}, u32[]{:S(2)}, u32[]{:S(2)}) collective-permute-start(bf16[1,2,64,2048]{3,2,1,0:T(8,128)(2,1)} %get-tuple-element.1497), channel_id=1, source_target_pairs={{0,1},{1,0},{2,3},{3,2},{4,5},{5,4},{6,7},{7,6},{8,9},{9,8},{10,11... | collective-permute-start | bytes 1572872 | tf_op jit(solution)/shard_map/ppermute | solution.py:58
  96.7 28.2 %collective-permute-start.20 = (bf16[128,2048]{1,0:T(8,128)(2,1)}, bf16[128,2048]{1,0:T(8,128)(2,1)S(1)}, u32[]{:S(2)}, u32[]{:S(2)}) collective-permute-start(bf16[128,2048]{1,0:T(8,128)(2,1)} %bitcast.505), channel_id=1, source_target_pairs={{0,8},{2,10},{4,12},{6,14},{8,0},{10,2},{12,4},{14,6},{16,24},{18,... | collective-permute-start | bytes 1572872 | tf_op jit(solution)/shard_map/ppermute | solution.py:55
  98.2 26.6 %collective-permute-start.19 = (bf16[128,3584]{1,0:T(8,128)(2,1)}, bf16[128,3584]{1,0:T(8,128)(2,1)S(1)}, u32[]{:S(2)}, u32[]{:S(2)}) collective-permute-start(bf16[128,3584]{1,0:T(8,128)(2,1)} %pad_maximum_fusion.3), channel_id=1, source_target_pairs={{0,2},{2,0},{4,6},{6,4},{8,10},{10,8},{12,14},{14,12},{16,18},{18,... | collective-permute-start | bytes 2752520 | tf_op jit(solution)/shard_map/ppermute | solution.py:55
  125.1 16.3 %collective-permute-start.25 = (bf16[256,512]{1,0:T(8,128)(2,1)S(1)}, bf16[256,512]{1,0:T(8,128)(2,1)S(1)}, u32[]{:S(2)}, u32[]{:S(2)}) collective-permute-start(bf16[256,512]{1,0:T(8,128)(2,1)S(1)} %bitcast.467), channel_id=1, source_target_pairs={{0,16},{2,18},{4,20},{6,22},{8,24},{10,26},{12,28},{14,30},{16,0},... | collective-permute-start | bytes 786440 | tf_op jit(solution)/shard_map/ppermute | solution.py:55
  141.5 21.9 %collective-permute-start.30 = (bf16[256,512]{1,0:T(8,128)(2,1)S(1)}, bf16[256,512]{1,0:T(8,128)(2,1)S(1)}, u32[]{:S(2)}, u32[]{:S(2)}) collective-permute-start(bf16[256,512]{1,0:T(8,128)(2,1)S(1)} %bitcast.468), channel_id=1, source_target_pairs={{0,16},{2,18},{4,20},{6,22},{8,24},{10,26},{12,28},{14,30},{16,0},... | collective-permute-start | bytes 786440 | tf_op jit(solution)/shard_map/ppermute | solution.py:55
  143.6 19.7 %collective-permute-start.28 = (bf16[64,2048]{1,0:T(8,128)(2,1)S(1)}, bf16[64,2048]{1,0:T(8,128)(2,1)S(1)}, u32[]{:S(2)}, u32[]{:S(2)}) collective-permute-start(bf16[64,2048]{1,0:T(8,128)(2,1)S(1)} %get-tuple-element.929), channel_id=1, source_target_pairs={{0,4},{2,6},{4,0},{6,2},{8,12},{10,14},{12,8},{14,10},{16,20},{18,... | collective-permute-start | bytes 786440 | tf_op jit(solution)/shard_map/ppermute | solution.py:55
  144.6 17.9 %collective-permute-start.29 = (bf16[4,128,512]{2,1,0:T(8,128)(2,1)S(1)}, bf16[4,128,512]{2,1,0:T(8,128)(2,1)S(1)}, u32[]{:S(2)}, u32[]{:S(2)}) collective-permute-start(bf16[4,128,512]{2,1,0:T(8,128)(2,1)S(1)} %pad_maximum_fusion.10), channel_id=1, source_target_pairs={{0,4},{2,6},{4,0},{6,2},{8,12},{10,14},{12,8},{14,10},{16,20},{18,... | collective-permute-start | bytes 1572872 | tf_op jit(solution)/shard_map/ppermute | solution.py:55
  145.6 17.7 %collective-permute-start.27 = (bf16[128,2048]{1,0:T(8,128)(2,1)S(1)}, bf16[128,2048]{1,0:T(8,128)(2,1)S(1)}, u32[]{:S(2)}, u32[]{:S(2)}) collective-permute-start(bf16[128,2048]{1,0:T(8,128)(2,1)S(1)} %slice.350), channel_id=1, source_target_pairs={{0,8},{2,10},{4,12},{6,14},{8,0},{10,2},{12,4},{14,6},{16,24},{18,... | collective-permute-start | bytes 1572872 | tf_op jit(solution)/shard_map/ppermute | solution.py:55
  145.9 17.5 %collective-permute-start.31 = (bf16[128,2048]{1,0:T(8,128)(2,1)S(1)}, bf16[128,2048]{1,0:T(8,128)(2,1)S(1)}, u32[]{:S(2)}, u32[]{:S(2)}) collective-permute-start(bf16[128,2048]{1,0:T(8,128)(2,1)S(1)} %get-tuple-element.1463), channel_id=1, source_target_pairs={{0,2},{2,0},{4,6},{6,4},{8,10},{10,8},{12,14},{14,12},{16,18},{18,... | collective-permute-start | bytes 1572872 | tf_op jit(solution)/shard_map/ppermute | solution.py:55
  165.3 17.4 %collective-permute-start.36 = (bf16[128,2048]{1,0:T(8,128)(2,1)S(1)}, bf16[128,2048]{1,0:T(8,128)(2,1)S(1)}, u32[]{:S(2)}, u32[]{:S(2)}) collective-permute-start(bf16[128,2048]{1,0:T(8,128)(2,1)S(1)} %add_convert_fusion.4), channel_id=1, source_target_pairs={{0,8},{2,10},{4,12},{6,14},{8,0},{10,2},{12,4},{14,6},{16,24},{18,... | collective-permute-start | bytes 1572872 | tf_op jit(solution)/shard_map/ppermute | solution.py:55
  167.0 15.7 %collective-permute-start.35 = (bf16[128,2048]{1,0:T(8,128)(2,1)S(1)}, bf16[128,2048]{1,0:T(8,128)(2,1)S(1)}, u32[]{:S(2)}, u32[]{:S(2)}) collective-permute-start(bf16[128,2048]{1,0:T(8,128)(2,1)S(1)} %get-tuple-element.945), channel_id=1, source_target_pairs={{0,2},{2,0},{4,6},{6,4},{8,10},{10,8},{12,14},{14,12},{16,18},{18,... | collective-permute-start | bytes 1572872 | tf_op jit(solution)/shard_map/ppermute | solution.py:55
  182.7 21.7 %collective-permute-start.37 = (bf16[2,1,192,2048]{3,2,0,1:T(8,128)(2,1)S(1)}, bf16[2,1,192,2048]{3,2,0,1:T(8,128)(2,1)S(1)}, u32[]{:S(2)}, u32[]{:S(2)}) collective-permute-start(bf16[2,1,192,2048]{3,2,0,1:T(8,128)(2,1)S(1)} %get-tuple-element.962), channel_id=1, source_target_pairs={{0,1},{1,0},{2,3},{3,2},{4,5},{5,4},{6,7},{7,6},{8,9},{9,8},{10,11... | collective-permute-start | bytes 4718600 | tf_op jit(solution)/shard_map/ppermute | solution.py:58
  184.7 19.7 %collective-permute-start.41 = (bf16[128,2048]{1,0:T(8,128)(2,1)S(1)}, bf16[128,2048]{1,0:T(8,128)(2,1)S(1)}, u32[]{:S(2)}, u32[]{:S(2)}) collective-permute-start(bf16[128,2048]{1,0:T(8,128)(2,1)S(1)} %multiply_convert_fusion), channel_id=1, source_target_pairs={{0,8},{2,10},{4,12},{6,14},{8,0},{10,2},{12,4},{14,6},{16,24},{18,... | collective-permute-start | bytes 1572872 | tf_op jit(solution)/shard_map/ppermute | solution.py:55
  184.8 19.6 %collective-permute-start.40 = (bf16[128,2048]{1,0:T(8,128)(2,1)S(1)}, bf16[128,2048]{1,0:T(8,128)(2,1)S(1)}, u32[]{:S(2)}, u32[]{:S(2)}) collective-permute-start(bf16[128,2048]{1,0:T(8,128)(2,1)S(1)} %multiply_convert_fusion), channel_id=1, source_target_pairs={{0,2},{2,0},{4,6},{6,4},{8,10},{10,8},{12,14},{14,12},{16,18},{18,... | collective-permute-start | bytes 1572872 | tf_op jit(solution)/shard_map/ppermute | solution.py:55
  185.7 16.4 %collective-permute-start.39 = (bf16[256,512]{1,0:T(8,128)(2,1)S(1)}, bf16[256,512]{1,0:T(8,128)(2,1)S(1)}, u32[]{:S(2)}, u32[]{:S(2)}) collective-permute-start(bf16[256,512]{1,0:T(8,128)(2,1)S(1)} %bitcast.477), channel_id=1, source_target_pairs={{0,16},{2,18},{4,20},{6,22},{8,24},{10,26},{12,28},{14,30},{16,0},... | collective-permute-start | bytes 786440 | tf_op jit(solution)/shard_map/ppermute | solution.py:55
  222.8 16.5 %collective-permute-start.47 = (bf16[512,2048]{1,0:T(8,128)(2,1)}, bf16[512,2048]{1,0:T(8,128)(2,1)}, u32[]{:S(2)}, u32[]{:S(2)}) collective-permute-start(bf16[512,2048]{1,0:T(8,128)(2,1)} %constant_dynamic-update-slice_fusion.8.refs_8_), channel_id=1, source_target_pairs={{0,1},{1,0},{2,3},{3,2},{4,5},{5,4},{6,7},{7,6},{8,9},{9,8},{10,11... | collective-permute-start | bytes 6291464 | tf_op jit(solution)/shard_map/ppermute | solution.py:58
  254.8 16.5 %collective-permute-start.49 = (bf16[512,512]{1,0:T(8,128)(2,1)S(1)}, bf16[512,512]{1,0:T(8,128)(2,1)S(1)}, u32[]{:S(2)}, u32[]{:S(2)}) collective-permute-start(bf16[512,512]{1,0:T(8,128)(2,1)S(1)} %bitcast.500), channel_id=1, source_target_pairs={{0,4},{2,6},{4,0},{6,2},{8,12},{10,14},{12,8},{14,10},{16,20},{18,... | collective-permute-start | bytes 1572872 | tf_op jit(solution)/shard_map/ppermute | solution.py:55
  271.6 16.3 %collective-permute-start.51 = (bf16[512,512]{1,0:T(8,128)(2,1)S(1)}, bf16[512,512]{1,0:T(8,128)(2,1)S(1)}, u32[]{:S(2)}, u32[]{:S(2)}) collective-permute-start(bf16[512,512]{1,0:T(8,128)(2,1)S(1)} %bitcast.499), channel_id=1, source_target_pairs={{0,4},{2,6},{4,0},{6,2},{8,12},{10,14},{12,8},{14,10},{16,20},{18,... | collective-permute-start | bytes 1572872 | tf_op jit(solution)/shard_map/ppermute | solution.py:55
  288.1 16.7 %collective-permute-start.54 = (bf16[512,2048]{1,0:T(8,128)(2,1)S(1)}, bf16[512,2048]{1,0:T(8,128)(2,1)S(1)}, u32[]{:S(2)}, u32[]{:S(2)}) collective-permute-start(bf16[512,2048]{1,0:T(8,128)(2,1)S(1)} %get-tuple-element.1190), channel_id=1, source_target_pairs={{0,1},{1,0},{2,3},{3,2},{4,5},{5,4},{6,7},{7,6},{8,9},{9,8},{10,11... | collective-permute-start | bytes 6291464 | tf_op jit(solution)/shard_map/ppermute | solution.py:58
  288.2 17.5 %collective-permute-start.52 = (bf16[256,512]{1,0:T(8,128)(2,1)S(1)}, bf16[256,512]{1,0:T(8,128)(2,1)S(1)}, u32[]{:S(2)}, u32[]{:S(2)}) collective-permute-start(bf16[256,512]{1,0:T(8,128)(2,1)S(1)} %bitcast.548), channel_id=1, source_target_pairs={{0,16},{2,18},{4,20},{6,22},{8,24},{10,26},{12,28},{14,30},{16,0},... | collective-permute-start | bytes 786440 | tf_op jit(solution)/shard_map/ppermute | solution.py:55
  325.7 16.8 %collective-permute-start.62 = (bf16[128,2048]{1,0:T(8,128)(2,1)S(1)}, bf16[128,2048]{1,0:T(8,128)(2,1)S(1)}, u32[]{:S(2)}, u32[]{:S(2)}) collective-permute-start(bf16[128,2048]{1,0:T(8,128)(2,1)S(1)} %add_convert_fusion.3), channel_id=1, source_target_pairs={{0,8},{2,10},{4,12},{6,14},{8,0},{10,2},{12,4},{14,6},{16,24},{18,... | collective-permute-start | bytes 1572872 | tf_op jit(solution)/shard_map/ppermute | solution.py:55
  326.4 16.1 %collective-permute-start.61 = (bf16[128,2048]{1,0:T(8,128)(2,1)S(1)}, bf16[128,2048]{1,0:T(8,128)(2,1)S(1)}, u32[]{:S(2)}, u32[]{:S(2)}) collective-permute-start(bf16[128,2048]{1,0:T(8,128)(2,1)S(1)} %get-tuple-element.1235), channel_id=1, source_target_pairs={{0,2},{2,0},{4,6},{6,4},{8,10},{10,8},{12,14},{14,12},{16,18},{18,... | collective-permute-start | bytes 1572872 | tf_op jit(solution)/shard_map/ppermute | solution.py:55
  345.5 16.5 %collective-permute-start.64 = (bf16[128,2048]{1,0:T(8,128)(2,1)S(1)}, bf16[128,2048]{1,0:T(8,128)(2,1)S(1)}, u32[]{:S(2)}, u32[]{:S(2)}) collective-permute-start(bf16[128,2048]{1,0:T(8,128)(2,1)S(1)} %get-tuple-element.1296), channel_id=1, source_target_pairs={{0,8},{2,10},{4,12},{6,14},{8,0},{10,2},{12,4},{14,6},{16,24},{18,... | collective-permute-start | bytes 1572872 | tf_op jit(solution)/shard_map/ppermute | solution.py:55
  345.5 16.5 %collective-permute-start.63 = (bf16[128,2048]{1,0:T(8,128)(2,1)S(1)}, bf16[128,2048]{1,0:T(8,128)(2,1)S(1)}, u32[]{:S(2)}, u32[]{:S(2)}) collective-permute-start(bf16[128,2048]{1,0:T(8,128)(2,1)S(1)} %get-tuple-element.1296), channel_id=1, source_target_pairs={{0,2},{2,0},{4,6},{6,4},{8,10},{10,8},{12,14},{14,12},{16,18},{18,... | collective-permute-start | bytes 1572872 | tf_op jit(solution)/shard_map/ppermute | solution.py:55
  363.5 16.9 %collective-permute-start.70 = (bf16[512,2048]{1,0:T(8,128)(2,1)}, bf16[512,2048]{1,0:T(8,128)(2,1)S(1)}, u32[]{:S(2)}, u32[]{:S(2)}) collective-permute-start(bf16[512,2048]{1,0:T(8,128)(2,1)} %get-tuple-element.1285), channel_id=1, source_target_pairs={{0,1},{1,0},{2,3},{3,2},{4,5},{5,4},{6,7},{7,6},{8,9},{9,8},{10,11... | collective-permute-start | bytes 6291464 | tf_op jit(solution)/shard_map/ppermute | solution.py:58
  364.8 18.5 %collective-permute-start.69 = (bf16[256,512]{1,0:T(8,128)(2,1)}, bf16[256,512]{1,0:T(8,128)(2,1)S(1)}, u32[]{:S(2)}, u32[]{:S(2)}) collective-permute-start(bf16[256,512]{1,0:T(8,128)(2,1)} %bitcast.545), channel_id=1, source_target_pairs={{0,16},{2,18},{4,20},{6,22},{8,24},{10,26},{12,28},{14,30},{16,0},... | collective-permute-start | bytes 786440 | tf_op jit(solution)/shard_map/ppermute | solution.py:55
  366.0 17.3 %collective-permute-start.68 = (bf16[128,2048]{1,0:T(8,128)(2,1)}, bf16[128,2048]{1,0:T(8,128)(2,1)S(1)}, u32[]{:S(2)}, u32[]{:S(2)}) collective-permute-start(bf16[128,2048]{1,0:T(8,128)(2,1)} %copy-done.111), channel_id=1, source_target_pairs={{0,2},{2,0},{4,6},{6,4},{8,10},{10,8},{12,14},{14,12},{16,18},{18,... | collective-permute-start | bytes 1572872 | tf_op jit(solution)/shard_map/ppermute | solution.py:55
  399.7 23.4 %collective-permute-start.76 = (bf16[128,2048]{1,0:T(8,128)(2,1)S(1)}, bf16[128,2048]{1,0:T(8,128)(2,1)S(1)}, u32[]{:S(2)}, u32[]{:S(2)}) collective-permute-start(bf16[128,2048]{1,0:T(8,128)(2,1)S(1)} %bitcast.528), channel_id=1, source_target_pairs={{0,4},{2,6},{4,0},{6,2},{8,12},{10,14},{12,8},{14,10},{16,20},{18,... | collective-permute-start | bytes 1572872 | tf_op jit(solution)/shard_map/ppermute | solution.py:55
  400.6 24.6 %collective-permute-start.75 = (bf16[64,2048]{1,0:T(8,128)(2,1)S(1)}, bf16[64,2048]{1,0:T(8,128)(2,1)S(1)}, u32[]{:S(2)}, u32[]{:S(2)}) collective-permute-start(bf16[64,2048]{1,0:T(8,128)(2,1)S(1)} %fusion.17), channel_id=1, source_target_pairs={{0,16},{2,18},{4,20},{6,22},{8,24},{10,26},{12,28},{14,30},{16,0},... | collective-permute-start | bytes 786440 | tf_op jit(solution)/shard_map/ppermute | solution.py:55
  402.3 22.9 %collective-permute-start.77 = (bf16[128,1536]{1,0:T(8,128)(2,1)S(1)}, bf16[128,1536]{1,0:T(8,128)(2,1)S(1)}, u32[]{:S(2)}, u32[]{:S(2)}) collective-permute-start(bf16[128,1536]{1,0:T(8,128)(2,1)S(1)} %pad_maximum_fusion.18), channel_id=1, source_target_pairs={{0,10},{2,8},{4,14},{6,12},{8,2},{10,0},{12,6},{14,4},{16,26},{18,... | collective-permute-start | bytes 1179656 | tf_op jit(solution)/shard_map/ppermute | solution.py:55
  404.6 20.6 %collective-permute-start.78 = (bf16[128,1536]{1,0:T(8,128)(2,1)S(1)}, bf16[128,1536]{1,0:T(8,128)(2,1)S(1)}, u32[]{:S(2)}, u32[]{:S(2)}) collective-permute-start(bf16[128,1536]{1,0:T(8,128)(2,1)S(1)} %pad_maximum_fusion.19), channel_id=1, source_target_pairs={{0,2},{2,0},{4,6},{6,4},{8,10},{10,8},{12,14},{14,12},{16,18},{18,... | collective-permute-start | bytes 1179656 | tf_op jit(solution)/shard_map/ppermute | solution.py:55
  405.0 20.3 %collective-permute-start.79 = (bf16[128,1536]{1,0:T(8,128)(2,1)S(1)}, bf16[128,1536]{1,0:T(8,128)(2,1)S(1)}, u32[]{:S(2)}, u32[]{:S(2)}) collective-permute-start(bf16[128,1536]{1,0:T(8,128)(2,1)S(1)} %pad_maximum_fusion.20), channel_id=1, source_target_pairs={{0,8},{2,10},{4,12},{6,14},{8,0},{10,2},{12,4},{14,6},{16,24},{18,... | collective-permute-start | bytes 1179656 | tf_op jit(solution)/shard_map/ppermute | solution.py:55
  425.9 15.9 %collective-permute-start.84 = (bf16[512,2048]{1,0:T(8,128)(2,1)}, bf16[512,2048]{1,0:T(8,128)(2,1)}, u32[]{:S(2)}, u32[]{:S(2)}) collective-permute-start(bf16[512,2048]{1,0:T(8,128)(2,1)} %get-tuple-element.1365), channel_id=1, source_target_pairs={{0,1},{1,0},{2,3},{3,2},{4,5},{5,4},{6,7},{7,6},{8,9},{9,8},{10,11... | collective-permute-start | bytes 6291464 | tf_op jit(solution)/shard_map/ppermute | solution.py:58
  427.7 16.7 %collective-permute-start.80 = (bf16[64,2048]{1,0:T(8,128)(2,1)S(1)}, bf16[64,2048]{1,0:T(8,128)(2,1)S(1)}, u32[]{:S(2)}, u32[]{:S(2)}) collective-permute-start(bf16[64,2048]{1,0:T(8,128)(2,1)S(1)} %fusion.18), channel_id=1, source_target_pairs={{0,16},{2,18},{4,20},{6,22},{8,24},{10,26},{12,28},{14,30},{16,0},... | collective-permute-start | bytes 786440 | tf_op jit(solution)/shard_map/ppermute | solution.py:55
  430.5 19.2 %collective-permute-start.83 = (bf16[128,2048]{1,0:T(8,128)(2,1)S(1)}, bf16[128,2048]{1,0:T(8,128)(2,1)S(1)}, u32[]{:S(2)}, u32[]{:S(2)}) collective-permute-start(bf16[128,2048]{1,0:T(8,128)(2,1)S(1)} %add_convert_fusion.2), channel_id=1, source_target_pairs={{0,8},{2,10},{4,12},{6,14},{8,0},{10,2},{12,4},{14,6},{16,24},{18,... | collective-permute-start | bytes 1572872 | tf_op jit(solution)/shard_map/ppermute | solution.py:55
  431.9 17.8 %collective-permute-start.82 = (bf16[1,128,2048]{2,1,0:T(8,128)(2,1)S(1)}, bf16[1,128,2048]{2,1,0:T(8,128)(2,1)S(1)}, u32[]{:S(2)}, u32[]{:S(2)}) collective-permute-start(bf16[1,128,2048]{2,1,0:T(8,128)(2,1)S(1)} %copy-done.117), channel_id=1, source_target_pairs={{0,2},{2,0},{4,6},{6,4},{8,10},{10,8},{12,14},{14,12},{16,18},{18,... | collective-permute-start | bytes 1572872 | tf_op jit(solution)/shard_map/ppermute | solution.py:55
  470.6 18.9 %collective-permute-start.96 = (bf16[128,2048]{1,0:T(8,128)(2,1)S(1)}, bf16[128,2048]{1,0:T(8,128)(2,1)S(1)}, u32[]{:S(2)}, u32[]{:S(2)}) collective-permute-start(bf16[128,2048]{1,0:T(8,128)(2,1)S(1)} %add_convert_fusion.1), channel_id=1, source_target_pairs={{0,8},{2,10},{4,12},{6,14},{8,0},{10,2},{12,4},{14,6},{16,24},{18,... | collective-permute-start | bytes 1572872 | tf_op jit(solution)/shard_map/ppermute | solution.py:55
  472.8 16.7 %collective-permute-start.93 = (bf16[4,128,1536]{2,1,0:T(8,128)(2,1)S(1)}, bf16[4,128,1536]{2,1,0:T(8,128)(2,1)S(1)}, u32[]{:S(2)}, u32[]{:S(2)}) collective-permute-start(bf16[4,128,1536]{2,1,0:T(8,128)(2,1)S(1)} %pad_maximum_fusion.2), channel_id=1, source_target_pairs={{0,1},{1,0},{2,3},{3,2},{4,5},{5,4},{6,7},{7,6},{8,9},{9,8},{10,11... | collective-permute-start | bytes 4718600 | tf_op jit(solution)/shard_map/ppermute | solution.py:58
  473.0 16.5 %collective-permute-start.95 = (bf16[128,2048]{1,0:T(8,128)(2,1)S(1)}, bf16[128,2048]{1,0:T(8,128)(2,1)S(1)}, u32[]{:S(2)}, u32[]{:S(2)}) collective-permute-start(bf16[128,2048]{1,0:T(8,128)(2,1)S(1)} %get-tuple-element.1405), channel_id=1, source_target_pairs={{0,2},{2,0},{4,6},{6,4},{8,10},{10,8},{12,14},{14,12},{16,18},{18,... | collective-permute-start | bytes 1572872 | tf_op jit(solution)/shard_map/ppermute | solution.py:55
  494.8 16.7 %collective-permute-start.98 = (bf16[128,2048]{1,0:T(8,128)(2,1)S(1)}, bf16[128,2048]{1,0:T(8,128)(2,1)S(1)}, u32[]{:S(2)}, u32[]{:S(2)}) collective-permute-start(bf16[128,2048]{1,0:T(8,128)(2,1)S(1)} %copy-done.115), channel_id=1, source_target_pairs={{0,2},{2,0},{4,6},{6,4},{8,10},{10,8},{12,14},{14,12},{16,18},{18,... | collective-permute-start | bytes 1572872 | tf_op jit(solution)/shard_map/ppermute | solution.py:55
  (203 other events, 1852.5 us)

commit v5 on v4

--- a/solution.py
+++ b/solution.py
@@ -149,7 +149,7 @@
         out_shape=[
             jax.ShapeDtypeStruct(shape, sources[0].dtype) for shape in zip(heights, widths)
         ],
-        compiler_params=pltpu.CompilerParams(vmem_limit_bytes=24 << 20),
+        compiler_params=pltpu.CompilerParams(vmem_limit_bytes=10 << 20),
         name="cut_columns",
     )(jnp.stack([jnp.asarray(at // LANES, jnp.int32) for _, at, _ in cuts]), *sources, rest)
 
@@ -175,7 +175,7 @@
         in_specs=[pl.BlockSpec(memory_space=pltpu.SMEM)] + [vmem] * len(pieces),
         out_specs=[vmem] * len(widths),
         out_shape=[jax.ShapeDtypeStruct((rows, w), F32) for w in widths],
-        compiler_params=pltpu.CompilerParams(vmem_limit_bytes=24 << 20),
+        compiler_params=pltpu.CompilerParams(vmem_limit_bytes=10 << 20),
         name="place_columns",
     )(jnp.stack([jnp.asarray(to // LANES, jnp.int32) for *_, to in places]), *pieces)
 

time: 525 us -> 526 us (level)
  no operation moved by 1% of the time
where the time goes in v5:
time: 526 us; the launch traced here: 518 us
  waiting for transfers between devices  222 us (42%)
  starting transfers between devices  105 us (20%)
  Pallas kernels  80.6 us (15%)
  local copies, waits for them, and re-layouts  64.9 us (12%)
  other arithmetic  41.1 us (8%)
    ppermute x90, waiting for transfers between devices, px(): return lax.ppermute(x, 'fsdp', [(i, i ^ mask) for i in range(self.n)])  222 us
    ppermute x90, starting transfers between devices, px(): return lax.ppermute(x, 'fsdp', [(i, i ^ mask) for i in range(self.n)])  104 us
    pallas_call x7, Pallas kernels, kernel_call(): pl.pallas_call(kernel, in_specs=[smem if x.dtype == jnp.int32 else vmem f...  73.9 us
    unnamed x300, local copies, waits for them, and re-layouts  27 us
  transfers between devices with their start and end apart: 107, of which 42 were waited for; matrix products, arithmetic and copies ran while one was open for 12% of the time, Pallas kernels for 15%

profile of v5, /device:TPU:0, one launch (start us, length us, event | category | flops | bytes accessed | tf_op | source)
XLA Modules:
  0.0 518.0 jit_solution(11037975102078702637)
XLA Ops:
  13.0 4.0 collective-permute-start.1
  18.5 2.5 collective-permute-start.2
  23.2 7.4 %collective-permute-done.2 = bf16[144,512]{1,0:T(8,128)(2,1)S(1)} collective-permute-done((bf16[144,512]{1,0:T(8,128)(2,1)S(1)}, bf16[144,512]{1,0:T(8,128)(2,1)S(1)}, u32[]{:S(2)}, u32[]{:S(2)}) %collective-permute-start.2) | collective-permute-done | bytes 147488 | tf_op jit(solution)/shard_map/ppermute | solution.py:55
  32.1 5.0 collective-permute-done.3
  37.9 3.1 collective-permute-start.9
  45.9 6.4 %collective-permute-done.6 = bf16[512,512]{1,0:T(8,128)(2,1)S(1)} collective-permute-done((bf16[512,512]{1,0:T(8,128)(2,1)S(1)}, bf16[512,512]{1,0:T(8,128)(2,1)S(1)}, u32[]{:S(2)}, u32[]{:S(2)}) %collective-permute-start.6) | collective-permute-done | bytes 524320 | tf_op jit(solution)/shard_map/ppermute | solution.py:55
  53.1 3.2 collective-permute-done.7
  57.1 2.8 collective-permute-start.12
  63.2 6.4 %collective-permute-done.12 = bf16[256,512]{1,0:T(8,128)(2,1)} collective-permute-done((bf16[256,512]{1,0:T(8,128)(2,1)S(1)}, bf16[256,512]{1,0:T(8,128)(2,1)}, u32[]{:S(2)}, u32[]{:S(2)}) %collective-permute-start.12) | collective-permute-done | bytes 262176 | tf_op jit(solution)/shard_map/ppermute | solution.py:55
  69.7 4.1 collective-permute-done.10
  84.7 6.7 %collective-permute-done.14 = bf16[64,2048]{1,0:T(8,128)(2,1)S(1)} collective-permute-done((bf16[64,2048]{1,0:T(8,128)(2,1)}, bf16[64,2048]{1,0:T(8,128)(2,1)S(1)}, u32[]{:S(2)}, u32[]{:S(2)}) %collective-permute-start.14) | collective-permute-done | bytes 262176 | tf_op jit(solution)/shard_map/ppermute | solution.py:55
  106.4 10.2 %attend.1 = (bf16[2048,512]{1,0:T(8,128)(2,1)S(1)}, f32[1024,384]{1,0:T(8,128)S(1)}, bf16[4,256,256]{2,1,0:T(8,128)(2,1)S(1)}, bf16[4,256,128]{2,1,0:T(8,128)(2,...) custom-call(s32[16]{0:T(128)S(1)} %stack.700.rows_ref, ...), custom_call_target="tpu_custom_call" | custom-call | flops 1048576 | bytes 65536 | tf_op jit(solution)/shard_map/attend/pallas_call | solution.py:359
  129.6 11.6 %collective-permute-done.24 = bf16[128,2048]{1,0:T(8,128)(2,1)S(1)} collective-permute-done((bf16[128,2048]{1,0:T(8,128)(2,1)S(1)}, bf16[128,2048]{1,0:T(8,128)(2,1)S(1)}, u32[]{:S(2)}, u32[]{:S(2)}) %collective-permute-start.24) | collective-permute-done | bytes 524320 | tf_op jit(solution)/shard_map/ppermute | solution.py:55
  148.1 15.0 %collective-permute-done.29 = bf16[4,128,512]{2,1,0:T(8,128)(2,1)S(1)} collective-permute-done((bf16[4,128,512]{2,1,0:T(8,128)(2,1)S(1)}, bf16[4,128,512]{2,1,0:T(8,128)(2,1)S(1)}, u32[]{:S(2)}, u32[]{:S(2)}) %collective-permute-start.29) | collective-permute-done | bytes 524320 | tf_op jit(solution)/shard_map/ppermute | solution.py:55
  171.9 5.3 %collective-permute-done.33 = bf16[512,512]{1,0:T(8,128)(2,1)S(1)} collective-permute-done((bf16[512,512]{1,0:T(8,128)(2,1)S(1)}, bf16[512,512]{1,0:T(8,128)(2,1)S(1)}, u32[]{:S(2)}, u32[]{:S(2)}) %collective-permute-start.33) | collective-permute-done | bytes 524320 | tf_op jit(solution)/shard_map/ppermute | solution.py:55
  178.0 5.4 %collective-permute-done.36 = bf16[128,2048]{1,0:T(8,128)(2,1)S(1)} collective-permute-done((bf16[128,2048]{1,0:T(8,128)(2,1)S(1)}, bf16[128,2048]{1,0:T(8,128)(2,1)S(1)}, u32[]{:S(2)}, u32[]{:S(2)}) %collective-permute-start.36) | collective-permute-done | bytes 524320 | tf_op jit(solution)/shard_map/ppermute | solution.py:55
  186.4 2.7 collective-permute-start.39
  189.1 8.7 %collective-permute-done.38 = bf16[4,128,512]{2,1,0:T(8,128)(2,1)S(1)} collective-permute-done((bf16[4,128,512]{2,1,0:T(8,128)(2,1)S(1)}, bf16[4,128,512]{2,1,0:T(8,128)(2,1)S(1)}, u32[]{:S(2)}, u32[]{:S(2)}) %collective-permute-start.38) | collective-permute-done | bytes 524320 | tf_op jit(solution)/shard_map/ppermute | solution.py:55
  198.6 4.2 collective-permute-done.39
  209.2 9.1 %collective-permute-done.42 = bf16[512,512]{1,0:T(8,128)(2,1)S(1)} collective-permute-done((bf16[512,512]{1,0:T(8,128)(2,1)S(1)}, bf16[512,512]{1,0:T(8,128)(2,1)S(1)}, u32[]{:S(2)}, u32[]{:S(2)}) %collective-permute-start.42) | collective-permute-done | bytes 524320 | tf_op jit(solution)/shard_map/ppermute | solution.py:55
  226.1 11.9 %collective-permute-done.45 = bf16[4,128,512]{2,1,0:T(8,128)(2,1)} collective-permute-done((bf16[4,128,512]{2,1,0:T(8,128)(2,1)}, bf16[4,128,512]{2,1,0:T(8,128)(2,1)}, u32[]{:S(2)}, u32[]{:S(2)}) %collective-permute-start.45) | collective-permute-done | bytes 524320 | tf_op jit(solution)/shard_map/ppermute | solution.py:55
  243.8 11.6 %feed.3 = (bf16[1024,256]{1,0:T(8,128)(2,1)S(1)}, bf16[256,2048]{1,0:T(8,128)(2,1)S(1)}, bf16[2,2,128,512]{3,2,1,0:T(8,128)(2,1)S(1)}, bf16[2,2,128,512]{3,2,1,0...) custom-call(s32[16]{0:T(128)S(1)} %stack.700.rows_ref, ...), custom_call_target="tpu_custom_call" | custom-call | flops 1048576 | bytes 65536 | tf_op jit(solution)/shard_map/feed/pallas_call | solution.py:359
  256.4 15.5 %feed.4 = (bf16[1024,256]{1,0:T(8,128)(2,1)S(1)}, bf16[256,2048]{1,0:T(8,128)(2,1)S(1)}, bf16[2,2,128,512]{3,2,1,0:T(8,128)(2,1)S(1)}, bf16[2,2,128,512]{3,2,1,0...) custom-call(s32[16]{0:T(128)S(1)} %stack.700.rows_ref, ...), custom_call_target="tpu_custom_call" | custom-call | flops 1048576 | bytes 65536 | tf_op jit(solution)/shard_map/feed/pallas_call | solution.py:359
  274.1 14.4 %feed.5 = (bf16[1024,256]{1,0:T(8,128)(2,1)S(1)}, bf16[256,2048]{1,0:T(8,128)(2,1)S(1)}, bf16[2,2,128,512]{3,2,1,0:T(8,128)(2,1)S(1)}, bf16[2,2,128,512]{3,2,1,0...) custom-call(s32[16]{0:T(128)S(1)} %stack.700.rows_ref, ...), custom_call_target="tpu_custom_call" | custom-call | flops 1048576 | bytes 65536 | tf_op jit(solution)/shard_map/feed/pallas_call | solution.py:359
  288.8 2.4 collective-permute-start.52
  292.6 12.6 %collective-permute-done.53 = bf16[512,512]{1,0:T(8,128)(2,1)S(1)} collective-permute-done((bf16[512,512]{1,0:T(8,128)(2,1)S(1)}, bf16[512,512]{1,0:T(8,128)(2,1)S(1)}, u32[]{:S(2)}, u32[]{:S(2)}) %collective-permute-start.53) | collective-permute-done | bytes 524320 | tf_op jit(solution)/shard_map/ppermute | solution.py:55
  311.4 8.6 %collective-permute-done.57 = bf16[512,512]{1,0:T(8,128)(2,1)S(1)} collective-permute-done((bf16[512,512]{1,0:T(8,128)(2,1)S(1)}, bf16[512,512]{1,0:T(8,128)(2,1)S(1)}, u32[]{:S(2)}, u32[]{:S(2)}) %collective-permute-start.57) | collective-permute-done | bytes 524320 | tf_op jit(solution)/shard_map/ppermute | solution.py:55
  330.8 4.8 project_out.3
  337.8 5.4 %collective-permute-done.62 = bf16[128,2048]{1,0:T(8,128)(2,1)S(1)} collective-permute-done((bf16[128,2048]{1,0:T(8,128)(2,1)S(1)}, bf16[128,2048]{1,0:T(8,128)(2,1)S(1)}, u32[]{:S(2)}, u32[]{:S(2)}) %collective-permute-start.62) | collective-permute-done | bytes 524320 | tf_op jit(solution)/shard_map/ppermute | solution.py:55
  347.6 2.7 collective-permute-start.65
  351.9 3.0 collective-permute-done.66
  356.7 3.6 collective-permute-done.65
  367.2 11.6 %collective-permute-done.67 = bf16[128,2048]{1,0:T(8,128)(2,1)} collective-permute-done((bf16[128,2048]{1,0:T(8,128)(2,1)}, bf16[128,2048]{1,0:T(8,128)(2,1)}, u32[]{:S(2)}, u32[]{:S(2)}) %collective-permute-start.67) | collective-permute-done | bytes 524320 | tf_op jit(solution)/shard_map/ppermute | solution.py:55
  381.1 2.8 convert_add_fusion.1
  391.8 6.7 %collective-permute-done.72 = bf16[128,2048]{1,0:T(8,128)(2,1)S(1)} collective-permute-done((bf16[128,2048]{1,0:T(8,128)(2,1)S(1)}, bf16[128,2048]{1,0:T(8,128)(2,1)S(1)}, u32[]{:S(2)}, u32[]{:S(2)}) %collective-permute-start.72) | collective-permute-done | bytes 524320 | tf_op jit(solution)/shard_map/ppermute | solution.py:55
  403.0 2.3 collective-permute-start.77
  406.6 16.1 %attend_back.1 = (f32[512,2048]{1,0:T(8,128)S(1)}, bf16[512,2048]{1,0:T(8,128)(2,1)}, bf16[256,2048]{1,0:T(8,128)(2,1)S(1)}, f32[2,128]{1,0:T(2,128)S(1)}, f32[1...) custom-call(s32[8]{0:T(128)S(1)} %stack.742.rows_out_ref.rows_ref, ...), custom_call_target="tpu_custom_call" | custom-call | flops 1048576 | bytes 65536 | tf_op jit(solution)/shard_map/attend_back/pallas_call | solution.py:359
  434.1 7.1 %collective-permute-done.85 = bf16[512,512]{1,0:T(8,128)(2,1)} collective-permute-done((bf16[512,512]{1,0:T(8,128)(2,1)}, bf16[512,512]{1,0:T(8,128)(2,1)}, u32[]{:S(2)}, u32[]{:S(2)}) %collective-permute-start.85) | collective-permute-done | bytes 524320 | tf_op jit(solution)/shard_map/ppermute | solution.py:55
  442.5 2.5 convert_add_fusion
  445.0 5.4 %collective-permute-done.83 = bf16[128,2048]{1,0:T(8,128)(2,1)S(1)} collective-permute-done((bf16[128,2048]{1,0:T(8,128)(2,1)S(1)}, bf16[128,2048]{1,0:T(8,128)(2,1)S(1)}, u32[]{:S(2)}, u32[]{:S(2)}) %collective-permute-start.83) | collective-permute-done | bytes 524320 | tf_op jit(solution)/shard_map/ppermute | solution.py:55
  456.2 9.2 %collective-permute-done.87 = f32[4352]{0:T(1024)S(1)} collective-permute-done((f32[4352]{0:T(1024)S(1)}, f32[4352]{0:T(1024)S(1)}, u32[]{:S(2)}, u32[]{:S(2)}) %collective-permute-start.87) | collective-permute-done | bytes 17440 | tf_op jit(solution)/shard_map/ppermute | solution.py:55
  466.0 2.6 collective-permute-done.89
  468.6 2.5 collective-permute-start.92
  475.2 9.8 %collective-permute-done.97 = bf16[256,512]{1,0:T(8,128)(2,1)S(1)} collective-permute-done((bf16[256,512]{1,0:T(8,128)(2,1)S(1)}, bf16[256,512]{1,0:T(8,128)(2,1)S(1)}, u32[]{:S(2)}, u32[]{:S(2)}) %collective-permute-start.97) | collective-permute-done | bytes 262176 | tf_op jit(solution)/shard_map/ppermute | solution.py:55
  485.4 4.7 collective-permute-done.96
  497.2 3.8 place_columns.2
  501.0 4.1 collective-permute-done.100.refs_1_
  506.0 3.8 collective-permute-done.106
  (689 shorter events, 197.9 us)
Async XLA Ops:
  13.0 19.1 %collective-permute-start.1 = (bf16[64,2048]{1,0:T(8,128)(2,1)S(1)}, bf16[64,2048]{1,0:T(8,128)(2,1)S(1)}, u32[]{:S(2)}, u32[]{:S(2)}) collective-permute-start(bf16[64,2048]{1,0:T(8,128)(2,1)S(1)} %copy-done.103), channel_id=1, source_target_pairs={{0,16},{2,18},{4,20},{6,22},{8,24},{10,26},{12,28},{14,30},{16,0},... | collective-permute-start | bytes 786440 | tf_op jit(solution)/shard_map/ppermute | solution.py:55
  21.5 15.6 %collective-permute-start.3 = (bf16[144,2048]{1,0:T(8,128)(2,1)S(1)}, bf16[144,2048]{1,0:T(8,128)(2,1)S(1)}, u32[]{:S(2)}, u32[]{:S(2)}) collective-permute-start(bf16[144,2048]{1,0:T(8,128)(2,1)S(1)} %get-tuple-element.742), channel_id=1, source_target_pairs={{0,2},{2,0},{4,6},{6,4},{8,10},{10,8},{12,14},{14,12},{16,18},{18,... | collective-permute-start | bytes 1769480 | tf_op jit(solution)/shard_map/ppermute | solution.py:55
  37.9 19.1 %collective-permute-start.9 = (bf16[128,2048]{1,0:T(8,128)(2,1)S(1)}, bf16[128,2048]{1,0:T(8,128)(2,1)S(1)}, u32[]{:S(2)}, u32[]{:S(2)}) collective-permute-start(bf16[128,2048]{1,0:T(8,128)(2,1)S(1)} %fusion.6), channel_id=1, source_target_pairs={{0,8},{2,10},{4,12},{6,14},{8,0},{10,2},{12,4},{14,6},{16,24},{18,... | collective-permute-start | bytes 1572872 | tf_op jit(solution)/shard_map/ppermute | solution.py:55
  41.0 16.1 %collective-permute-start.8 = (bf16[128,2048]{1,0:T(8,128)(2,1)S(1)}, bf16[128,2048]{1,0:T(8,128)(2,1)S(1)}, u32[]{:S(2)}, u32[]{:S(2)}) collective-permute-start(bf16[128,2048]{1,0:T(8,128)(2,1)S(1)} %fusion.6), channel_id=1, source_target_pairs={{0,2},{2,0},{4,6},{6,4},{8,10},{10,8},{12,14},{14,12},{16,18},{18,... | collective-permute-start | bytes 1572872 | tf_op jit(solution)/shard_map/ppermute | solution.py:55
  74.7 18.8 %collective-permute-start.18 = (bf16[512,2048]{1,0:T(8,128)(2,1)S(1)}, bf16[512,2048]{1,0:T(8,128)(2,1)}, u32[]{:S(2)}, u32[]{:S(2)}) collective-permute-start(bf16[512,2048]{1,0:T(8,128)(2,1)S(1)} %constant_dynamic-update-slice_fusion.refs_8_.refs_14_), channel_id=1, source_target_pairs={{0,1},{1,0},{2,3},{3,2},{4,5},{5,4},{6,7},{7,6},{8,9},{9,8},{10,11... | collective-permute-start | bytes 6291464 | tf_op jit(solution)/shard_map/ppermute | solution.py:58
  76.7 16.8 %collective-permute-start.15 = (bf16[128,1536]{1,0:T(8,128)(2,1)}, bf16[128,1536]{1,0:T(8,128)(2,1)S(1)}, u32[]{:S(2)}, u32[]{:S(2)}) collective-permute-start(bf16[128,1536]{1,0:T(8,128)(2,1)} %get-tuple-element.796), channel_id=1, source_target_pairs={{0,8},{2,10},{4,12},{6,14},{8,0},{10,2},{12,4},{14,6},{16,24},{18,... | collective-permute-start | bytes 1179656 | tf_op jit(solution)/shard_map/ppermute | solution.py:55
  94.4 25.5 %collective-permute-start.22 = (bf16[128,2048]{1,0:T(8,128)(2,1)}, bf16[128,2048]{1,0:T(8,128)(2,1)}, u32[]{:S(2)}, u32[]{:S(2)}) collective-permute-start(bf16[128,2048]{1,0:T(8,128)(2,1)} %pad_maximum_fusion.8), channel_id=1, source_target_pairs={{0,16},{2,18},{4,20},{6,22},{8,24},{10,26},{12,28},{14,30},{16,0},... | collective-permute-start | bytes 1572872 | tf_op jit(solution)/shard_map/ppermute | solution.py:55
  95.6 28.6 %collective-permute-start.21 = (bf16[192,2048]{1,0:T(8,128)(2,1)}, bf16[192,2048]{1,0:T(8,128)(2,1)}, u32[]{:S(2)}, u32[]{:S(2)}) collective-permute-start(bf16[192,2048]{1,0:T(8,128)(2,1)} %dynamic-slice_bitcast_fusion.4), channel_id=1, source_target_pairs={{0,4},{2,6},{4,0},{6,2},{8,12},{10,14},{12,8},{14,10},{16,20},{18,... | collective-permute-start | bytes 2359304 | tf_op jit(solution)/shard_map/ppermute | solution.py:55
  97.3 24.1 %collective-permute-start.23 = (bf16[1,2,64,2048]{3,2,1,0:T(8,128)(2,1)}, bf16[1,2,64,2048]{3,2,1,0:T(8,128)(2,1)}, u32[]{:S(2)}, u32[]{:S(2)}) collective-permute-start(bf16[1,2,64,2048]{3,2,1,0:T(8,128)(2,1)} %get-tuple-element.1497), channel_id=1, source_target_pairs={{0,1},{1,0},{2,3},{3,2},{4,5},{5,4},{6,7},{7,6},{8,9},{9,8},{10,11... | collective-permute-start | bytes 1572872 | tf_op jit(solution)/shard_map/ppermute | solution.py:58
  97.4 28.2 %collective-permute-start.20 = (bf16[128,2048]{1,0:T(8,128)(2,1)}, bf16[128,2048]{1,0:T(8,128)(2,1)S(1)}, u32[]{:S(2)}, u32[]{:S(2)}) collective-permute-start(bf16[128,2048]{1,0:T(8,128)(2,1)} %bitcast.505), channel_id=1, source_target_pairs={{0,8},{2,10},{4,12},{6,14},{8,0},{10,2},{12,4},{14,6},{16,24},{18,... | collective-permute-start | bytes 1572872 | tf_op jit(solution)/shard_map/ppermute | solution.py:55
  98.9 26.6 %collective-permute-start.19 = (bf16[128,3584]{1,0:T(8,128)(2,1)}, bf16[128,3584]{1,0:T(8,128)(2,1)S(1)}, u32[]{:S(2)}, u32[]{:S(2)}) collective-permute-start(bf16[128,3584]{1,0:T(8,128)(2,1)} %pad_maximum_fusion.3), channel_id=1, source_target_pairs={{0,2},{2,0},{4,6},{6,4},{8,10},{10,8},{12,14},{14,12},{16,18},{18,... | collective-permute-start | bytes 2752520 | tf_op jit(solution)/shard_map/ppermute | solution.py:55
  125.7 16.3 %collective-permute-start.25 = (bf16[256,512]{1,0:T(8,128)(2,1)S(1)}, bf16[256,512]{1,0:T(8,128)(2,1)S(1)}, u32[]{:S(2)}, u32[]{:S(2)}) collective-permute-start(bf16[256,512]{1,0:T(8,128)(2,1)S(1)} %bitcast.467), channel_id=1, source_target_pairs={{0,16},{2,18},{4,20},{6,22},{8,24},{10,26},{12,28},{14,30},{16,0},... | collective-permute-start | bytes 786440 | tf_op jit(solution)/shard_map/ppermute | solution.py:55
  142.1 21.9 %collective-permute-start.30 = (bf16[256,512]{1,0:T(8,128)(2,1)S(1)}, bf16[256,512]{1,0:T(8,128)(2,1)S(1)}, u32[]{:S(2)}, u32[]{:S(2)}) collective-permute-start(bf16[256,512]{1,0:T(8,128)(2,1)S(1)} %bitcast.468), channel_id=1, source_target_pairs={{0,16},{2,18},{4,20},{6,22},{8,24},{10,26},{12,28},{14,30},{16,0},... | collective-permute-start | bytes 786440 | tf_op jit(solution)/shard_map/ppermute | solution.py:55
  144.2 19.7 %collective-permute-start.28 = (bf16[64,2048]{1,0:T(8,128)(2,1)S(1)}, bf16[64,2048]{1,0:T(8,128)(2,1)S(1)}, u32[]{:S(2)}, u32[]{:S(2)}) collective-permute-start(bf16[64,2048]{1,0:T(8,128)(2,1)S(1)} %get-tuple-element.929), channel_id=1, source_target_pairs={{0,4},{2,6},{4,0},{6,2},{8,12},{10,14},{12,8},{14,10},{16,20},{18,... | collective-permute-start | bytes 786440 | tf_op jit(solution)/shard_map/ppermute | solution.py:55
  145.2 17.9 %collective-permute-start.29 = (bf16[4,128,512]{2,1,0:T(8,128)(2,1)S(1)}, bf16[4,128,512]{2,1,0:T(8,128)(2,1)S(1)}, u32[]{:S(2)}, u32[]{:S(2)}) collective-permute-start(bf16[4,128,512]{2,1,0:T(8,128)(2,1)S(1)} %pad_maximum_fusion.10), channel_id=1, source_target_pairs={{0,4},{2,6},{4,0},{6,2},{8,12},{10,14},{12,8},{14,10},{16,20},{18,... | collective-permute-start | bytes 1572872 | tf_op jit(solution)/shard_map/ppermute | solution.py:55
  146.3 17.7 %collective-permute-start.27 = (bf16[128,2048]{1,0:T(8,128)(2,1)S(1)}, bf16[128,2048]{1,0:T(8,128)(2,1)S(1)}, u32[]{:S(2)}, u32[]{:S(2)}) collective-permute-start(bf16[128,2048]{1,0:T(8,128)(2,1)S(1)} %slice.350), channel_id=1, source_target_pairs={{0,8},{2,10},{4,12},{6,14},{8,0},{10,2},{12,4},{14,6},{16,24},{18,... | collective-permute-start | bytes 1572872 | tf_op jit(solution)/shard_map/ppermute | solution.py:55
  146.5 17.5 %collective-permute-start.31 = (bf16[128,2048]{1,0:T(8,128)(2,1)S(1)}, bf16[128,2048]{1,0:T(8,128)(2,1)S(1)}, u32[]{:S(2)}, u32[]{:S(2)}) collective-permute-start(bf16[128,2048]{1,0:T(8,128)(2,1)S(1)} %get-tuple-element.1463), channel_id=1, source_target_pairs={{0,2},{2,0},{4,6},{6,4},{8,10},{10,8},{12,14},{14,12},{16,18},{18,... | collective-permute-start | bytes 1572872 | tf_op jit(solution)/shard_map/ppermute | solution.py:55
  165.9 17.4 %collective-permute-start.36 = (bf16[128,2048]{1,0:T(8,128)(2,1)S(1)}, bf16[128,2048]{1,0:T(8,128)(2,1)S(1)}, u32[]{:S(2)}, u32[]{:S(2)}) collective-permute-start(bf16[128,2048]{1,0:T(8,128)(2,1)S(1)} %add_convert_fusion.4), channel_id=1, source_target_pairs={{0,8},{2,10},{4,12},{6,14},{8,0},{10,2},{12,4},{14,6},{16,24},{18,... | collective-permute-start | bytes 1572872 | tf_op jit(solution)/shard_map/ppermute | solution.py:55
  167.7 15.6 %collective-permute-start.35 = (bf16[128,2048]{1,0:T(8,128)(2,1)S(1)}, bf16[128,2048]{1,0:T(8,128)(2,1)S(1)}, u32[]{:S(2)}, u32[]{:S(2)}) collective-permute-start(bf16[128,2048]{1,0:T(8,128)(2,1)S(1)} %get-tuple-element.945), channel_id=1, source_target_pairs={{0,2},{2,0},{4,6},{6,4},{8,10},{10,8},{12,14},{14,12},{16,18},{18,... | collective-permute-start | bytes 1572872 | tf_op jit(solution)/shard_map/ppermute | solution.py:55
  183.3 21.7 %collective-permute-start.37 = (bf16[2,1,192,2048]{3,2,0,1:T(8,128)(2,1)S(1)}, bf16[2,1,192,2048]{3,2,0,1:T(8,128)(2,1)S(1)}, u32[]{:S(2)}, u32[]{:S(2)}) collective-permute-start(bf16[2,1,192,2048]{3,2,0,1:T(8,128)(2,1)S(1)} %get-tuple-element.962), channel_id=1, source_target_pairs={{0,1},{1,0},{2,3},{3,2},{4,5},{5,4},{6,7},{7,6},{8,9},{9,8},{10,11... | collective-permute-start | bytes 4718600 | tf_op jit(solution)/shard_map/ppermute | solution.py:58
  185.3 19.7 %collective-permute-start.41 = (bf16[128,2048]{1,0:T(8,128)(2,1)S(1)}, bf16[128,2048]{1,0:T(8,128)(2,1)S(1)}, u32[]{:S(2)}, u32[]{:S(2)}) collective-permute-start(bf16[128,2048]{1,0:T(8,128)(2,1)S(1)} %multiply_convert_fusion), channel_id=1, source_target_pairs={{0,8},{2,10},{4,12},{6,14},{8,0},{10,2},{12,4},{14,6},{16,24},{18,... | collective-permute-start | bytes 1572872 | tf_op jit(solution)/shard_map/ppermute | solution.py:55
  185.4 19.6 %collective-permute-start.40 = (bf16[128,2048]{1,0:T(8,128)(2,1)S(1)}, bf16[128,2048]{1,0:T(8,128)(2,1)S(1)}, u32[]{:S(2)}, u32[]{:S(2)}) collective-permute-start(bf16[128,2048]{1,0:T(8,128)(2,1)S(1)} %multiply_convert_fusion), channel_id=1, source_target_pairs={{0,2},{2,0},{4,6},{6,4},{8,10},{10,8},{12,14},{14,12},{16,18},{18,... | collective-permute-start | bytes 1572872 | tf_op jit(solution)/shard_map/ppermute | solution.py:55
  186.4 16.4 %collective-permute-start.39 = (bf16[256,512]{1,0:T(8,128)(2,1)S(1)}, bf16[256,512]{1,0:T(8,128)(2,1)S(1)}, u32[]{:S(2)}, u32[]{:S(2)}) collective-permute-start(bf16[256,512]{1,0:T(8,128)(2,1)S(1)} %bitcast.477), channel_id=1, source_target_pairs={{0,16},{2,18},{4,20},{6,22},{8,24},{10,26},{12,28},{14,30},{16,0},... | collective-permute-start | bytes 786440 | tf_op jit(solution)/shard_map/ppermute | solution.py:55
  223.4 16.5 %collective-permute-start.47 = (bf16[512,2048]{1,0:T(8,128)(2,1)}, bf16[512,2048]{1,0:T(8,128)(2,1)}, u32[]{:S(2)}, u32[]{:S(2)}) collective-permute-start(bf16[512,2048]{1,0:T(8,128)(2,1)} %constant_dynamic-update-slice_fusion.8.refs_8_), channel_id=1, source_target_pairs={{0,1},{1,0},{2,3},{3,2},{4,5},{5,4},{6,7},{7,6},{8,9},{9,8},{10,11... | collective-permute-start | bytes 6291464 | tf_op jit(solution)/shard_map/ppermute | solution.py:58
  255.5 16.4 %collective-permute-start.49 = (bf16[512,512]{1,0:T(8,128)(2,1)S(1)}, bf16[512,512]{1,0:T(8,128)(2,1)S(1)}, u32[]{:S(2)}, u32[]{:S(2)}) collective-permute-start(bf16[512,512]{1,0:T(8,128)(2,1)S(1)} %bitcast.500), channel_id=1, source_target_pairs={{0,4},{2,6},{4,0},{6,2},{8,12},{10,14},{12,8},{14,10},{16,20},{18,... | collective-permute-start | bytes 1572872 | tf_op jit(solution)/shard_map/ppermute | solution.py:55
  272.2 16.3 %collective-permute-start.51 = (bf16[512,512]{1,0:T(8,128)(2,1)S(1)}, bf16[512,512]{1,0:T(8,128)(2,1)S(1)}, u32[]{:S(2)}, u32[]{:S(2)}) collective-permute-start(bf16[512,512]{1,0:T(8,128)(2,1)S(1)} %bitcast.499), channel_id=1, source_target_pairs={{0,4},{2,6},{4,0},{6,2},{8,12},{10,14},{12,8},{14,10},{16,20},{18,... | collective-permute-start | bytes 1572872 | tf_op jit(solution)/shard_map/ppermute | solution.py:55
  288.8 16.7 %collective-permute-start.54 = (bf16[512,2048]{1,0:T(8,128)(2,1)S(1)}, bf16[512,2048]{1,0:T(8,128)(2,1)S(1)}, u32[]{:S(2)}, u32[]{:S(2)}) collective-permute-start(bf16[512,2048]{1,0:T(8,128)(2,1)S(1)} %get-tuple-element.1190), channel_id=1, source_target_pairs={{0,1},{1,0},{2,3},{3,2},{4,5},{5,4},{6,7},{7,6},{8,9},{9,8},{10,11... | collective-permute-start | bytes 6291464 | tf_op jit(solution)/shard_map/ppermute | solution.py:58
  288.8 17.5 %collective-permute-start.52 = (bf16[256,512]{1,0:T(8,128)(2,1)S(1)}, bf16[256,512]{1,0:T(8,128)(2,1)S(1)}, u32[]{:S(2)}, u32[]{:S(2)}) collective-permute-start(bf16[256,512]{1,0:T(8,128)(2,1)S(1)} %bitcast.548), channel_id=1, source_target_pairs={{0,16},{2,18},{4,20},{6,22},{8,24},{10,26},{12,28},{14,30},{16,0},... | collective-permute-start | bytes 786440 | tf_op jit(solution)/shard_map/ppermute | solution.py:55
  326.4 16.8 %collective-permute-start.62 = (bf16[128,2048]{1,0:T(8,128)(2,1)S(1)}, bf16[128,2048]{1,0:T(8,128)(2,1)S(1)}, u32[]{:S(2)}, u32[]{:S(2)}) collective-permute-start(bf16[128,2048]{1,0:T(8,128)(2,1)S(1)} %add_convert_fusion.3), channel_id=1, source_target_pairs={{0,8},{2,10},{4,12},{6,14},{8,0},{10,2},{12,4},{14,6},{16,24},{18,... | collective-permute-start | bytes 1572872 | tf_op jit(solution)/shard_map/ppermute | solution.py:55
  327.1 16.2 %collective-permute-start.61 = (bf16[128,2048]{1,0:T(8,128)(2,1)S(1)}, bf16[128,2048]{1,0:T(8,128)(2,1)S(1)}, u32[]{:S(2)}, u32[]{:S(2)}) collective-permute-start(bf16[128,2048]{1,0:T(8,128)(2,1)S(1)} %get-tuple-element.1235), channel_id=1, source_target_pairs={{0,2},{2,0},{4,6},{6,4},{8,10},{10,8},{12,14},{14,12},{16,18},{18,... | collective-permute-start | bytes 1572872 | tf_op jit(solution)/shard_map/ppermute | solution.py:55
  346.1 16.5 %collective-permute-start.64 = (bf16[128,2048]{1,0:T(8,128)(2,1)S(1)}, bf16[128,2048]{1,0:T(8,128)(2,1)S(1)}, u32[]{:S(2)}, u32[]{:S(2)}) collective-permute-start(bf16[128,2048]{1,0:T(8,128)(2,1)S(1)} %get-tuple-element.1296), channel_id=1, source_target_pairs={{0,8},{2,10},{4,12},{6,14},{8,0},{10,2},{12,4},{14,6},{16,24},{18,... | collective-permute-start | bytes 1572872 | tf_op jit(solution)/shard_map/ppermute | solution.py:55
  346.1 16.5 %collective-permute-start.63 = (bf16[128,2048]{1,0:T(8,128)(2,1)S(1)}, bf16[128,2048]{1,0:T(8,128)(2,1)S(1)}, u32[]{:S(2)}, u32[]{:S(2)}) collective-permute-start(bf16[128,2048]{1,0:T(8,128)(2,1)S(1)} %get-tuple-element.1296), channel_id=1, source_target_pairs={{0,2},{2,0},{4,6},{6,4},{8,10},{10,8},{12,14},{14,12},{16,18},{18,... | collective-permute-start | bytes 1572872 | tf_op jit(solution)/shard_map/ppermute | solution.py:55
  364.2 16.9 %collective-permute-start.70 = (bf16[512,2048]{1,0:T(8,128)(2,1)}, bf16[512,2048]{1,0:T(8,128)(2,1)S(1)}, u32[]{:S(2)}, u32[]{:S(2)}) collective-permute-start(bf16[512,2048]{1,0:T(8,128)(2,1)} %get-tuple-element.1285), channel_id=1, source_target_pairs={{0,1},{1,0},{2,3},{3,2},{4,5},{5,4},{6,7},{7,6},{8,9},{9,8},{10,11... | collective-permute-start | bytes 6291464 | tf_op jit(solution)/shard_map/ppermute | solution.py:58
  365.4 18.5 %collective-permute-start.69 = (bf16[256,512]{1,0:T(8,128)(2,1)}, bf16[256,512]{1,0:T(8,128)(2,1)S(1)}, u32[]{:S(2)}, u32[]{:S(2)}) collective-permute-start(bf16[256,512]{1,0:T(8,128)(2,1)} %bitcast.545), channel_id=1, source_target_pairs={{0,16},{2,18},{4,20},{6,22},{8,24},{10,26},{12,28},{14,30},{16,0},... | collective-permute-start | bytes 786440 | tf_op jit(solution)/shard_map/ppermute | solution.py:55
  366.6 17.3 %collective-permute-start.68 = (bf16[128,2048]{1,0:T(8,128)(2,1)}, bf16[128,2048]{1,0:T(8,128)(2,1)S(1)}, u32[]{:S(2)}, u32[]{:S(2)}) collective-permute-start(bf16[128,2048]{1,0:T(8,128)(2,1)} %copy-done.111), channel_id=1, source_target_pairs={{0,2},{2,0},{4,6},{6,4},{8,10},{10,8},{12,14},{14,12},{16,18},{18,... | collective-permute-start | bytes 1572872 | tf_op jit(solution)/shard_map/ppermute | solution.py:55
  400.4 23.3 %collective-permute-start.76 = (bf16[128,2048]{1,0:T(8,128)(2,1)S(1)}, bf16[128,2048]{1,0:T(8,128)(2,1)S(1)}, u32[]{:S(2)}, u32[]{:S(2)}) collective-permute-start(bf16[128,2048]{1,0:T(8,128)(2,1)S(1)} %bitcast.528), channel_id=1, source_target_pairs={{0,4},{2,6},{4,0},{6,2},{8,12},{10,14},{12,8},{14,10},{16,20},{18,... | collective-permute-start | bytes 1572872 | tf_op jit(solution)/shard_map/ppermute | solution.py:55
  401.3 24.6 %collective-permute-start.75 = (bf16[64,2048]{1,0:T(8,128)(2,1)S(1)}, bf16[64,2048]{1,0:T(8,128)(2,1)S(1)}, u32[]{:S(2)}, u32[]{:S(2)}) collective-permute-start(bf16[64,2048]{1,0:T(8,128)(2,1)S(1)} %fusion.17), channel_id=1, source_target_pairs={{0,16},{2,18},{4,20},{6,22},{8,24},{10,26},{12,28},{14,30},{16,0},... | collective-permute-start | bytes 786440 | tf_op jit(solution)/shard_map/ppermute | solution.py:55
  403.0 22.9 %collective-permute-start.77 = (bf16[128,1536]{1,0:T(8,128)(2,1)S(1)}, bf16[128,1536]{1,0:T(8,128)(2,1)S(1)}, u32[]{:S(2)}, u32[]{:S(2)}) collective-permute-start(bf16[128,1536]{1,0:T(8,128)(2,1)S(1)} %pad_maximum_fusion.18), channel_id=1, source_target_pairs={{0,10},{2,8},{4,14},{6,12},{8,2},{10,0},{12,6},{14,4},{16,26},{18,... | collective-permute-start | bytes 1179656 | tf_op jit(solution)/shard_map/ppermute | solution.py:55
  405.2 20.6 %collective-permute-start.78 = (bf16[128,1536]{1,0:T(8,128)(2,1)S(1)}, bf16[128,1536]{1,0:T(8,128)(2,1)S(1)}, u32[]{:S(2)}, u32[]{:S(2)}) collective-permute-start(bf16[128,1536]{1,0:T(8,128)(2,1)S(1)} %pad_maximum_fusion.19), channel_id=1, source_target_pairs={{0,2},{2,0},{4,6},{6,4},{8,10},{10,8},{12,14},{14,12},{16,18},{18,... | collective-permute-start | bytes 1179656 | tf_op jit(solution)/shard_map/ppermute | solution.py:55
  405.6 20.3 %collective-permute-start.79 = (bf16[128,1536]{1,0:T(8,128)(2,1)S(1)}, bf16[128,1536]{1,0:T(8,128)(2,1)S(1)}, u32[]{:S(2)}, u32[]{:S(2)}) collective-permute-start(bf16[128,1536]{1,0:T(8,128)(2,1)S(1)} %pad_maximum_fusion.20), channel_id=1, source_target_pairs={{0,8},{2,10},{4,12},{6,14},{8,0},{10,2},{12,4},{14,6},{16,24},{18,... | collective-permute-start | bytes 1179656 | tf_op jit(solution)/shard_map/ppermute | solution.py:55
  426.6 15.9 %collective-permute-start.84 = (bf16[512,2048]{1,0:T(8,128)(2,1)}, bf16[512,2048]{1,0:T(8,128)(2,1)}, u32[]{:S(2)}, u32[]{:S(2)}) collective-permute-start(bf16[512,2048]{1,0:T(8,128)(2,1)} %get-tuple-element.1365), channel_id=1, source_target_pairs={{0,1},{1,0},{2,3},{3,2},{4,5},{5,4},{6,7},{7,6},{8,9},{9,8},{10,11... | collective-permute-start | bytes 6291464 | tf_op jit(solution)/shard_map/ppermute | solution.py:58
  428.4 16.6 %collective-permute-start.80 = (bf16[64,2048]{1,0:T(8,128)(2,1)S(1)}, bf16[64,2048]{1,0:T(8,128)(2,1)S(1)}, u32[]{:S(2)}, u32[]{:S(2)}) collective-permute-start(bf16[64,2048]{1,0:T(8,128)(2,1)S(1)} %fusion.18), channel_id=1, source_target_pairs={{0,16},{2,18},{4,20},{6,22},{8,24},{10,26},{12,28},{14,30},{16,0},... | collective-permute-start | bytes 786440 | tf_op jit(solution)/shard_map/ppermute | solution.py:55
  431.2 19.2 %collective-permute-start.83 = (bf16[128,2048]{1,0:T(8,128)(2,1)S(1)}, bf16[128,2048]{1,0:T(8,128)(2,1)S(1)}, u32[]{:S(2)}, u32[]{:S(2)}) collective-permute-start(bf16[128,2048]{1,0:T(8,128)(2,1)S(1)} %add_convert_fusion.2), channel_id=1, source_target_pairs={{0,8},{2,10},{4,12},{6,14},{8,0},{10,2},{12,4},{14,6},{16,24},{18,... | collective-permute-start | bytes 1572872 | tf_op jit(solution)/shard_map/ppermute | solution.py:55
  432.6 17.8 %collective-permute-start.82 = (bf16[1,128,2048]{2,1,0:T(8,128)(2,1)S(1)}, bf16[1,128,2048]{2,1,0:T(8,128)(2,1)S(1)}, u32[]{:S(2)}, u32[]{:S(2)}) collective-permute-start(bf16[1,128,2048]{2,1,0:T(8,128)(2,1)S(1)} %copy-done.117), channel_id=1, source_target_pairs={{0,2},{2,0},{4,6},{6,4},{8,10},{10,8},{12,14},{14,12},{16,18},{18,... | collective-permute-start | bytes 1572872 | tf_op jit(solution)/shard_map/ppermute | solution.py:55
  471.2 18.9 %collective-permute-start.96 = (bf16[128,2048]{1,0:T(8,128)(2,1)S(1)}, bf16[128,2048]{1,0:T(8,128)(2,1)S(1)}, u32[]{:S(2)}, u32[]{:S(2)}) collective-permute-start(bf16[128,2048]{1,0:T(8,128)(2,1)S(1)} %add_convert_fusion.1), channel_id=1, source_target_pairs={{0,8},{2,10},{4,12},{6,14},{8,0},{10,2},{12,4},{14,6},{16,24},{18,... | collective-permute-start | bytes 1572872 | tf_op jit(solution)/shard_map/ppermute | solution.py:55
  473.4 16.7 %collective-permute-start.93 = (bf16[4,128,1536]{2,1,0:T(8,128)(2,1)S(1)}, bf16[4,128,1536]{2,1,0:T(8,128)(2,1)S(1)}, u32[]{:S(2)}, u32[]{:S(2)}) collective-permute-start(bf16[4,128,1536]{2,1,0:T(8,128)(2,1)S(1)} %pad_maximum_fusion.2), channel_id=1, source_target_pairs={{0,1},{1,0},{2,3},{3,2},{4,5},{5,4},{6,7},{7,6},{8,9},{9,8},{10,11... | collective-permute-start | bytes 4718600 | tf_op jit(solution)/shard_map/ppermute | solution.py:58
  473.6 16.5 %collective-permute-start.95 = (bf16[128,2048]{1,0:T(8,128)(2,1)S(1)}, bf16[128,2048]{1,0:T(8,128)(2,1)S(1)}, u32[]{:S(2)}, u32[]{:S(2)}) collective-permute-start(bf16[128,2048]{1,0:T(8,128)(2,1)S(1)} %get-tuple-element.1405), channel_id=1, source_target_pairs={{0,2},{2,0},{4,6},{6,4},{8,10},{10,8},{12,14},{14,12},{16,18},{18,... | collective-permute-start | bytes 1572872 | tf_op jit(solution)/shard_map/ppermute | solution.py:55
  495.4 16.7 %collective-permute-start.98 = (bf16[128,2048]{1,0:T(8,128)(2,1)S(1)}, bf16[128,2048]{1,0:T(8,128)(2,1)S(1)}, u32[]{:S(2)}, u32[]{:S(2)}) collective-permute-start(bf16[128,2048]{1,0:T(8,128)(2,1)S(1)} %copy-done.115), channel_id=1, source_target_pairs={{0,2},{2,0},{4,6},{6,4},{8,10},{10,8},{12,14},{14,12},{16,18},{18,... | collective-permute-start | bytes 1572872 | tf_op jit(solution)/shard_map/ppermute | solution.py:55
  (203 other events, 1829.3 us)
